TPU v7x, 128 devices: a whole 4x4x4 slice. The times are simulated.
128 devices in a mesh: rows: 32 (over y, z, core), ch: 4 (over x).
Axes of the slice: x: 4, y: 4, z: 4, core: 2. Of those that a mesh axis runs over, the one named last changes fastest.
Arguments:
- tile_image: bfloat16 [768, 256, 256], P('ch', 'rows'), may hold values from -23 to 23
- spectral_filter: float32 [2, 768, 256, 256], P(None, 'ch', 'rows'), may hold values from -4 to 4
- conv_taps: float32 [768, 9], P('ch'), may hold values from -4 to 4
- norm_gain: float32 [768], replicated, may hold values from 0.25 to 1.75
- up_weight: bfloat16 [768, 3072], P(None, 'ch'), may hold values from -0.21875 to 0.21875
- down_weight: bfloat16 [3072, 768], P('ch'), may hold values from -0.109375 to 0.109375
- upstream: bfloat16 [768, 256, 256], P('ch', 'rows'), may hold values from -5 to 5
Outputs:
- block_out: bfloat16 [768, 256, 256], P('ch', 'rows')
- grad_image: float32 [768, 256, 256], P('ch', 'rows')
- grad_filter: float32 [2, 768, 256, 256], P(None, 'ch', 'rows')
All inputs are finite; a program needn't handle non-finite values.
Results may differ from a plain program's by a relative error of at most 0.012.
Values may be sent and summed in bfloat16 or wider, within the bound.
No kernel may reach another device: no remote copies, remote signals or barrier semaphores. Data moves between devices by JAX's collectives and lax.ppermute only.
A program may use at most 128 MiB of HBM per device.

v0:
```python
import math

import jax
import jax.numpy as jnp
from jax import lax
from jax.sharding import PartitionSpec as P

norm_epsilon = 1e-05
root_half = 0.7071067811865476
density = 0.3989422804014327


def in_one_piece(arrays, axis, split_dim, concat_dim, along):
    both = jnp.concatenate(arrays, axis=along)
    out, at, outs = (
        lax.all_to_all(both, axis, split_axis=split_dim, concat_axis=concat_dim, tiled=True),
        0,
        [],
    )
    for a in arrays:
        outs.append(lax.slice_in_dim(out, at, at + a.shape[along], axis=along))
        at += a.shape[along]
    return tuple(outs)


def with_halo(block, sides, width):
    for axis, dim in sides:
        count = lax.axis_size(axis)
        forward = [(i, i + 1) for i in range(count - 1)]
        backward = [(target, source) for source, target in forward]
        low = lax.ppermute(
            lax.slice_in_dim(block, block.shape[dim] - width, None, axis=dim), axis, forward
        )
        high = lax.ppermute(lax.slice_in_dim(block, 0, width, axis=dim), axis, backward)
        block = jnp.concatenate([low, block, high], axis=dim)
    return block


def turned_gather(arrays, axis, dims):
    turned = [jnp.moveaxis(a, dim, 0) for a, dim in zip(arrays, dims)]
    widths = [t[0].size for t in turned]
    both = jnp.concatenate([t.reshape(-1, w) for t, w in zip(turned, widths)], axis=1)
    out = lax.all_gather(both, axis, axis=0, tiled=True)
    pieces = jnp.split(out, [sum(widths[:k]) for k in range(1, len(widths))], axis=1)
    return tuple(
        (
            jnp.moveaxis(b.reshape(-1, *t.shape[1:]), 0, dim)
            for b, t, dim in zip(pieces, turned, dims)
        )
    )


def contract(form, left, right):
    return jnp.einsum(
        form, left, right, precision=lax.Precision.HIGHEST, preferred_element_type=jnp.float32
    )


def angle_tables(length):
    indices = jnp.arange(length, dtype=jnp.int32)
    products = indices[:, None] * indices[None, :] % length
    angles = products.astype(jnp.float32) * (2.0 * math.pi / length)
    return (jnp.cos(angles), jnp.sin(angles))


def filter_pass(signal, kernel_re, kernel_im):
    col_len = signal.shape[2]
    cos_w, sin_w = angle_tables(col_len)
    head_re = contract("chw,kw->ckh", signal, cos_w)
    head_im = -contract("chw,kw->ckh", signal, sin_w)
    col_re, col_im = tuple(
        (
            part.astype(jnp.float32)
            for part in in_one_piece(
                (head_re.astype(jnp.bfloat16), head_im.astype(jnp.bfloat16)), "rows", 1, 2, 0
            )
        )
    )
    row_len = col_re.shape[2]
    cos_h, sin_h = angle_tables(row_len)
    spec_re = contract("cwh,kh->cwk", col_re, cos_h) + contract("cwh,kh->cwk", col_im, sin_h)
    spec_im = contract("cwh,kh->cwk", col_im, cos_h) - contract("cwh,kh->cwk", col_re, sin_h)
    prod_re = kernel_re * spec_re - kernel_im * spec_im
    prod_im = kernel_re * spec_im + kernel_im * spec_re
    back_re = contract("cwk,kh->cwh", prod_re, cos_h) - contract("cwk,kh->cwh", prod_im, sin_h)
    back_im = contract("cwk,kh->cwh", prod_im, cos_h) + contract("cwk,kh->cwh", prod_re, sin_h)
    row_re, row_im = tuple(
        (
            part.astype(jnp.float32)
            for part in in_one_piece(
                (back_re.astype(jnp.bfloat16), back_im.astype(jnp.bfloat16)), "rows", 2, 1, 0
            )
        )
    )
    outcome = contract("ckh,kw->chw", row_re, cos_w) - contract("ckh,kw->chw", row_im, sin_w)
    return (outcome * (1.0 / (row_len * col_len)), spec_re, spec_im)


def depthwise(signal, tap_weights):
    token_row_count, col_count = (signal.shape[1], signal.shape[2])
    padded = with_halo(signal.astype(jnp.bfloat16), (("rows", 1),), 1).astype(signal.dtype)
    padded = jnp.pad(padded, ((0, 0), (0, 0), (1, 1)))
    running = jnp.zeros_like(signal)
    for row_off in range(3):
        for col_off in range(3):
            running = (
                running
                + tap_weights[:, 3 * row_off + col_off][:, None, None]
                * padded[:, row_off : row_off + token_row_count, col_off : col_off + col_count]
            )
    return running


def layer_norm(whole):
    values = whole.astype(jnp.float32)
    centred = values - jnp.mean(values, axis=0)[None]
    inv_std = lax.rsqrt(jnp.mean(centred * centred, axis=0) + norm_epsilon)
    return (centred * inv_std[None], inv_std)


def gelu_slope(pre_act):
    return 0.5 * (1.0 + lax.erf(pre_act * root_half)) + pre_act * density * jnp.exp(
        -0.5 * pre_act * pre_act
    )


def norm_back(normed_gradient, normed, inv_std, gain):
    weighted = normed_gradient * gain[None, :, None, None]
    mean_one = jnp.mean(weighted, axis=1, keepdims=True)
    second = jnp.mean(weighted * normed[None], axis=1, keepdims=True)
    return inv_std[None, None] * (weighted - mean_one - normed[None] * second)


def settle(partials):
    return jnp.sum(
        lax.optimization_barrier(partials.astype(jnp.bfloat16)).astype(jnp.float32), axis=0
    )


def to_tokens(values):
    return lax.all_to_all(values, "ch", split_axis=2, concat_axis=0, tiled=True)


def to_channels(values):
    return lax.all_to_all(
        values.astype(jnp.bfloat16), "ch", split_axis=0, concat_axis=2, tiled=True
    ).astype(values.dtype)


def on_device(tile_image, spectral_filter, conv_taps, norm_gain, up_weight, down_weight, upstream):
    signal = tile_image.astype(jnp.float32)
    filtered, spec_re, spec_im = filter_pass(signal, spectral_filter[0], spectral_filter[1])
    hidden_state = signal + depthwise(filtered, conv_taps)
    rounded = hidden_state.astype(jnp.bfloat16)
    gain_column = norm_gain[:, None, None]
    full_up, full_down = turned_gather((up_weight, down_weight), "ch", (1, 0))
    blocks = lax.axis_size("ch")
    channels, hidden_units = (full_up.shape[0], full_up.shape[1])
    hidden_share_units = hidden_units // blocks
    normed, inv_std = layer_norm(to_tokens(rounded))
    scaled = (normed * gain_column).astype(jnp.bfloat16)
    pre_act = jnp.einsum("chw,cf->fhw", scaled, full_up, preferred_element_type=jnp.float32)
    activated = jax.nn.gelu(pre_act, approximate=False).astype(jnp.bfloat16)
    token_row_count, col_count = (activated.shape[1], activated.shape[2])
    partials = jnp.einsum(
        "bfhw,bfc->bchw",
        activated.reshape(blocks, hidden_share_units, token_row_count, col_count),
        full_down.reshape(blocks, hidden_share_units, channels),
        preferred_element_type=jnp.float32,
    )
    out_sum = to_channels(settle(partials))
    block_out = (hidden_state + out_sum).astype(jnp.bfloat16)
    whole_dy = to_tokens(upstream)
    grad_act = jnp.einsum("chw,fc->fhw", whole_dy, full_down, preferred_element_type=jnp.float32)
    preactivation_gradient = (grad_act * gelu_slope(pre_act)).astype(jnp.bfloat16)
    normed_gradient = jnp.einsum(
        "pjra,spj->psra",
        preactivation_gradient.reshape(blocks, hidden_share_units, token_row_count, col_count),
        full_up.reshape(channels, blocks, hidden_share_units),
        preferred_element_type=jnp.float32,
    )
    grad_mlp = to_channels(settle(norm_back(normed_gradient, normed, inv_std, norm_gain)))
    grad_hidden = upstream.astype(jnp.float32) + grad_mlp
    grad_filtered = depthwise(grad_hidden, conv_taps[:, ::-1])
    adjoint, grad_re, grad_im = filter_pass(grad_filtered, spectral_filter[0], -spectral_filter[1])
    grad_image = grad_hidden + adjoint
    factor = 1.0 / (tile_image.shape[2] * spec_re.shape[2])
    grad_filter = jnp.stack(
        [
            (grad_re * spec_re + grad_im * spec_im) * factor,
            (grad_im * spec_re - grad_re * spec_im) * factor,
        ]
    )
    return (block_out, grad_image, grad_filter)


def solution(mesh):
    return jax.shard_map(
        on_device,
        mesh=mesh,
        in_specs=(
            P("ch", "rows", None),
            P(None, "ch", "rows", None),
            P("ch", None),
            P(),
            P(None, "ch"),
            P("ch", None),
            P("ch", "rows", None),
        ),
        out_specs=(P("ch", "rows", None), P("ch", "rows", None), P(None, "ch", "rows", None)),
        check_vma=False,
    )
```

profile of v0, /device:TPU:1, one launch (start us, length us, event | category | flops | bytes accessed | tf_op | source)
XLA Modules:
  0.0 390.0 jit_solution(16197978958838597289)
XLA Ops:
  16.7 32.3 %all_to_all.105 = bf16[384,256,8]{0,2,1:T(8,128)(2,1)S(1)} all-to-all(bf16[384,256,8]{0,2,1:T(8,128)(2,1)S(1)} %copy.203), channel_id=1, replica_groups=mesh['rows'=32,'ch'=4] {'rows'}, dimensions={1} | all-to-all | bytes 3145728 | tf_op jit(solution)/shard_map/all_to_all | solution.py:16
  74.7 4.6 %all-to-all-start.1 = ((bf16[384,8,256]{0,1,2:T(8,128)(2,1)}), bf16[384,8,256]{0,1,2:T(8,128)(2,1)}, u32[]{:S(2)}, u32[]{:S(2)}) async-start(bf16[384,8,256]{0,1,2:T(8,128)(2,1)} %copy.210), calls=%async_computation.1 | async-start | bytes 3145728 | tf_op jit(solution)/shard_map/all_to_all | solution.py:16
  81.2 20.5 %all-to-all-done.1 = bf16[384,8,256]{0,1,2:T(8,128)(2,1)} async-done(((bf16[384,8,256]{0,1,2:T(8,128)(2,1)}), bf16[384,8,256]{0,1,2:T(8,128)(2,1)}, u32[]{:S(2)}, u32[]{:S(2)}) %all-to-all-start.1) | async-done | bytes 1572896 | tf_op jit(solution)/shard_map/all_to_all | solution.py:16
  101.7 4.7 %all-to-all-start.4 = ((bf16[192,8,256]{0,1,2:T(8,128)(2,1)}), bf16[192,8,256]{0,1,2:T(8,128)(2,1)}, u32[]{:S(2)}, u32[]{:S(2)}) async-start(bf16[192,8,256]{0,1,2:T(8,128)(2,1)} %copy.225), calls=%async_computation.4 | async-start | bytes 2097152 | tf_op jit(solution)/shard_map/all_to_all | solution.py:141
  123.7 4.4 %collective-permute-done.1 = bf16[192,1,256]{2,1,0:T(2,128)(2,1)S(1)} collective-permute-done((bf16[192,1,256]{2,1,0:T(2,128)(2,1)S(1)}, bf16[192,1,256]{2,1,0:T(2,128)(2,1)S(1)}, u32[]{:S(2)}, u32[]{:S(2)}) %collective-permute-start.1) | collective-permute-done | bytes 98336 | tf_op jit(solution)/shard_map/ppermute | solution.py:34
  129.0 5.7 %fusion.232 = (bf16[192,8,256]{2,1,0:T(8,128)(2,1)S(1)}, f32[192,8,256]{2,1,0:T(8,128)}) fusion(f32[192]{0:T(256)S(1)} %bitcast.242, f32[192,10,256]{2,1,0:T(8,128)S(1)} %maximum_convert_fusion, f32[192]{0:T(256)S(1)} %bitcast.244, f32[192]{0:T(256)S(1)} %bitcast.230, f32[192]{0:T(256)S(1)} %bitcast.232, f32[192]{0:T(256)S(1)} %bitcast.234, ...), kind=kLoop, calls=%fused_computation.284 | loop fusion | flops 7864320 | bytes 11019264 | tf_op jit(solution)/shard_map/convert_element_type | solution.py:154
  136.6 4.7 %all-to-all-start.2 = ((bf16[192,8,256]{0,1,2:T(8,128)(2,1)}), bf16[192,8,256]{0,1,2:T(8,128)(2,1)}, u32[]{:S(2)}, u32[]{:S(2)}) async-start(bf16[192,8,256]{0,1,2:T(8,128)(2,1)} %copy.217), calls=%async_computation.2 | async-start | bytes 2097152 | tf_op jit(solution)/shard_map/all_to_all | solution.py:141
  145.2 8.8 %all-to-all-done.2 = bf16[192,8,256]{0,1,2:T(8,128)(2,1)} async-done(((bf16[192,8,256]{0,1,2:T(8,128)(2,1)}), bf16[192,8,256]{0,1,2:T(8,128)(2,1)}, u32[]{:S(2)}, u32[]{:S(2)}) %all-to-all-start.2) | async-done | bytes 786464 | tf_op jit(solution)/shard_map/all_to_all | solution.py:141
  164.3 4.9 %fusion.230 = f32[3072,512]{0,1:S(1)} fusion(bf16[768,512]{0,1:T(8,128)(2,1)} %bitcast.227, bf16[3072,1536]{1,0:T(8,128)(2,1)} %all-gather.2.cloned.1.call-done), kind=kOutput, calls=%fused_computation.282 | convolution fusion | flops 2415919104 | bytes 11796480
  172.4 17.2 %fusion.7 = (bf16[3072,8,64]{0,2,1:T(8,128)(2,1)S(1)}, bf16[3072,8,64]{0,2,1:T(8,128)(2,1)}) fusion(f32[3072,8,64]{0,2,1:T(8,128)S(1)} %bitcast.215, f32[3072,8,64]{0,2,1:T(8,128)S(1)} %bitcast.214), kind=kLoop, calls=%fused_computation.21 | loop fusion | flops 117964800 | bytes 18874368 | tf_op jit(solution)/shard_map/convert_element_type | solution.py:175
  191.6 6.6 %fusion.234 = (bf16[3072,768]{1,0:T(8,128)(2,1)S(1)}, bf16[3072,768]{1,0:T(8,128)(2,1)}) fusion(bf16[3072,1536]{1,0:T(8,128)(2,1)} %all-gather.2.cloned.1.call-done), kind=kLoop, calls=%fused_computation.285 | loop fusion | bytes 18874368 | tf_op jit(solution)/shard_map/split | solution.py:44
  198.2 4.5 %fusion.245 = f32[4,768,512]{1,2,0:S(1)} fusion(bf16[4,768,512]{1,2,0:T(8,128)(2,1)} %bitcast.225, bf16[768,4,768]{0,2,1:T(8,128)(2,1)S(1)} %bitcast.218), kind=kOutput, calls=%fused_computation.294 | convolution fusion | flops 2415919104 | bytes 14155776
  214.4 15.1 %all_to_all.106 = bf16[4,2,49152]{2,1,0:T(2,128)(2,1)} all-to-all(bf16[4,2,49152]{2,1,0:T(2,128)(2,1)} %reshape.112), channel_id=1, replica_groups=mesh['rows'=32,'ch'=4] {'ch'}, dimensions={0} | all-to-all | bytes 1572864 | tf_op jit(solution)/shard_map/all_to_all | solution.py:145
  244.5 7.6 %collective-permute-start.2 = (bf16[192,1,256]{2,1,0:T(2,128)(2,1)S(1)}, bf16[192,1,256]{2,1,0:T(2,128)(2,1)S(1)}, u32[]{:S(2)}, u32[]{:S(2)}) collective-permute-start(bf16[192,1,256]{2,1,0:T(2,128)(2,1)S(1)} %get-tuple-element.31), channel_id=1, source_target_pairs={{0,4},{4,8},{8,12},{12,16},{16,20},{20,24},{24,28},{28,32},{32,36}... | collective-permute-start | bytes 294920 | tf_op jit(solution)/shard_map/ppermute | solution.py:31
  254.7 4.4 %collective-permute-done.3 = bf16[192,1,256]{2,1,0:T(2,128)(2,1)S(1)} collective-permute-done((bf16[192,1,256]{2,1,0:T(2,128)(2,1)S(1)}, bf16[192,1,256]{2,1,0:T(2,128)(2,1)S(1)}, u32[]{:S(2)}, u32[]{:S(2)}) %collective-permute-start.3) | collective-permute-done | bytes 98336 | tf_op jit(solution)/shard_map/ppermute | solution.py:34
  260.0 5.3 %fusion.38 = f32[192,8,256]{2,1,0:T(8,128)S(1)} fusion(f32[192,10,256]{2,1,0:T(8,128)S(1)} %maximum_convert_fusion.1, f32[192]{0:T(256)S(1)} %bitcast.243, f32[192]{0:T(256)S(1)} %bitcast.245, f32[192]{0:T(256)S(1)} %bitcast.231, f32[192]{0:T(256)S(1)} %bitcast.233, f32[192]{0:T(256)S(1)} %bitcast.235, f32[192]{0:T(256)S(1)} %bitcast.237, ...), kind=kLoop, calls=%fused_computation.69 | loop fusion | flops 6684672 | bytes 9446400 | tf_op jit(solution)/shard_map/add | solution.py:107
  274.6 4.5 %all-to-all-start.6 = ((bf16[384,256,8]{0,2,1:T(8,128)(2,1)}), bf16[384,256,8]{0,2,1:T(8,128)(2,1)}, u32[]{:S(2)}, u32[]{:S(2)}) async-start(bf16[384,256,8]{0,2,1:T(8,128)(2,1)} %copy.236), calls=%async_computation.6 | async-start | bytes 3145728 | tf_op jit(solution)/shard_map/all_to_all | solution.py:16
  281.5 4.5 %fusion.244 = f32[4,768,512]{1,2,0:S(1)} fusion(bf16[4,768,512]{1,2,0:T(8,128)(2,1)S(1)} %bitcast.226, bf16[4,768,768]{2,1,0:T(8,128)(2,1)} %bitcast.217), kind=kOutput, calls=%fused_computation.293 | convolution fusion | flops 2415919104 | bytes 14155776
  294.4 4.0 %reshape.110 = bf16[4,2,49152]{2,1,0:T(2,128)(2,1)} reshape(bf16[768,8,64]{2,1,0:T(8,128)(2,1)} %copy.221) | data formatting | bytes 1572864
  301.9 4.4 %all-to-all-start.3 = ((bf16[4,2,49152]{2,1,0:T(2,128)(2,1)}), bf16[4,2,49152]{2,1,0:T(2,128)(2,1)}, u32[]{:S(2)}, u32[]{:S(2)}) async-start(bf16[4,2,49152]{2,1,0:T(2,128)(2,1)} %reshape.110), calls=%async_computation.3 | async-start | bytes 1572864 | tf_op jit(solution)/shard_map/all_to_all | solution.py:145
  323.9 4.3 %multiply_bitcast_fusion.1 = (f32[1,192,8,256]{3,2,1,0:T(8,128)}, f32[1,192,8,256]{3,2,1,0:T(8,128)}, f32[192,8,256]{2,1,0:T(8,128)S(1)}, f32[192,8,256]{2,1,0:T(8,128)S(1)}) fusion(f32[192,8,256]{2,1,0:T(8,128)S(1)} %convolution_subtract_fusion, f32[192,8,256]{2,1,0:T(8,128)S(1)} %copy-done.5, f32[192,8,256]{2,1,0:T(8,128)S(1)} %convolution_add_fusion.1, ...), kind=kOutput, calls=%fused_computation.101 | convolution fusion | flops 1215168512 | bytes 16515072 | tf_op jit(solution)/shard_map/cwh,kh->cwk/dot_general | solution.py:54
  340.4 5.4 %all-to-all-start.7 = ((bf16[384,8,256]{0,1,2:T(8,128)(2,1)}), bf16[384,8,256]{0,1,2:T(8,128)(2,1)}, u32[]{:S(2)}, u32[]{:S(2)}) async-start(bf16[384,8,256]{0,1,2:T(8,128)(2,1)} %copy.243), calls=%async_computation.7 | async-start | bytes 3145728 | tf_op jit(solution)/shard_map/all_to_all | solution.py:16
  350.3 3.6 reshape.97
  364.5 3.9 %all-to-all-done.7 = bf16[384,8,256]{0,1,2:T(8,128)(2,1)} async-done(((bf16[384,8,256]{0,1,2:T(8,128)(2,1)}), bf16[384,8,256]{0,1,2:T(8,128)(2,1)}, u32[]{:S(2)}, u32[]{:S(2)}) %all-to-all-start.7) | async-done | bytes 1572896 | tf_op jit(solution)/shard_map/all_to_all | solution.py:16
  (145 shorter events, 189.2 us)
Async XLA Ops:
  7.2 157.1 %all-gather.2.cloned.1.call-start = ((), (), s32[]{:S(2)}) async-start(), calls=%async_computation.8 | async-start | bytes 11796480 | tf_op jit(solution)/shard_map/all_gather | solution.py:43
  56.9 2.0 copy-start.10
  74.7 4.6 %copy-start.2 = (bf16[192,8,256]{2,1,0:T(8,128)(2,1)S(1)}, bf16[192,8,256]{2,1,0:T(8,128)(2,1)}, u32[]{:S(2)}) copy-start(bf16[192,8,256]{2,1,0:T(8,128)(2,1)} %param.13) | copy-start | bytes 2359300
  74.7 27.0 %all-to-all-start.1 = ((bf16[384,8,256]{0,1,2:T(8,128)(2,1)}), bf16[384,8,256]{0,1,2:T(8,128)(2,1)}, u32[]{:S(2)}, u32[]{:S(2)}) async-start(bf16[384,8,256]{0,1,2:T(8,128)(2,1)} %copy.210), calls=%async_computation.1 | async-start | bytes 3145728 | tf_op jit(solution)/shard_map/all_to_all | solution.py:16
  101.7 34.9 %all-to-all-start.4 = ((bf16[192,8,256]{0,1,2:T(8,128)(2,1)}), bf16[192,8,256]{0,1,2:T(8,128)(2,1)}, u32[]{:S(2)}, u32[]{:S(2)}) async-start(bf16[192,8,256]{0,1,2:T(8,128)(2,1)} %copy.225), calls=%async_computation.4 | async-start | bytes 2097152 | tf_op jit(solution)/shard_map/all_to_all | solution.py:141
  117.1 6.5 %copy-start.18 = (f32[192,9]{0,1:T(8,128)S(1)}, f32[192,9]{0,1:T(8,128)}, u32[]{:S(2)}) copy-start(f32[192,9]{0,1:T(8,128)} %param.9) | copy-start | bytes 20740
  119.2 4.5 %collective-permute-start = (bf16[192,1,256]{2,1,0:T(2,128)(2,1)S(1)}, bf16[192,1,256]{2,1,0:T(2,128)(2,1)S(1)}, u32[]{:S(2)}, u32[]{:S(2)}) collective-permute-start(bf16[192,1,256]{2,1,0:T(2,128)(2,1)S(1)} %get-tuple-element.33), channel_id=1, source_target_pairs={{0,4},{4,8},{8,12},{12,16},{16,20},{20,24},{24,28},{28,32},{32,36}... | collective-permute-start | bytes 294920 | tf_op jit(solution)/shard_map/ppermute | solution.py:31
  121.1 7.0 %collective-permute-start.1 = (bf16[192,1,256]{2,1,0:T(2,128)(2,1)S(1)}, bf16[192,1,256]{2,1,0:T(2,128)(2,1)S(1)}, u32[]{:S(2)}, u32[]{:S(2)}) collective-permute-start(bf16[192,1,256]{2,1,0:T(2,128)(2,1)S(1)} %get-tuple-element.34), channel_id=1, source_target_pairs={{4,0},{8,4},{12,8},{16,12},{20,16},{24,20},{28,24},{32,28},{36,32}... | collective-permute-start | bytes 294920 | tf_op jit(solution)/shard_map/ppermute | solution.py:34
  123.6 5.4 %copy-start.15 = (bf16[192,8,256]{2,1,0:T(8,128)(2,1)S(1)}, bf16[192,8,256]{2,1,0:T(8,128)(2,1)}, u32[]{:S(2)}) copy-start(bf16[192,8,256]{2,1,0:T(8,128)(2,1)} %param.7) | copy-start | bytes 2359300
  136.6 17.4 %all-to-all-start.2 = ((bf16[192,8,256]{0,1,2:T(8,128)(2,1)}), bf16[192,8,256]{0,1,2:T(8,128)(2,1)}, u32[]{:S(2)}, u32[]{:S(2)}) async-start(bf16[192,8,256]{0,1,2:T(8,128)(2,1)} %copy.217), calls=%async_computation.2 | async-start | bytes 2097152 | tf_op jit(solution)/shard_map/all_to_all | solution.py:141
  164.3 5.3 %copy-start = (bf16[3072,1536]{1,0:T(8,128)(2,1)S(1)}, bf16[3072,1536]{1,0:T(8,128)(2,1)}, u32[]{:S(2)}) copy-start(bf16[3072,1536]{1,0:T(8,128)(2,1)} %all-gather.2.cloned.1.call-done) | copy-start | bytes 28311556
  164.3 5.5 %copy-start.16 = (bf16[768,512]{0,1:T(8,128)(2,1)S(1)}, bf16[768,512]{0,1:T(8,128)(2,1)}, u32[]{:S(2)}) copy-start(bf16[768,512]{0,1:T(8,128)(2,1)} %reshape.105) | copy-start | bytes 2359300
  244.5 10.2 %collective-permute-start.2 = (bf16[192,1,256]{2,1,0:T(2,128)(2,1)S(1)}, bf16[192,1,256]{2,1,0:T(2,128)(2,1)S(1)}, u32[]{:S(2)}, u32[]{:S(2)}) collective-permute-start(bf16[192,1,256]{2,1,0:T(2,128)(2,1)S(1)} %get-tuple-element.31), channel_id=1, source_target_pairs={{0,4},{4,8},{8,12},{12,16},{16,20},{20,24},{24,28},{28,32},{32,36}... | collective-permute-start | bytes 294920 | tf_op jit(solution)/shard_map/ppermute | solution.py:31
  252.1 7.0 %collective-permute-start.3 = (bf16[192,1,256]{2,1,0:T(2,128)(2,1)S(1)}, bf16[192,1,256]{2,1,0:T(2,128)(2,1)S(1)}, u32[]{:S(2)}, u32[]{:S(2)}) collective-permute-start(bf16[192,1,256]{2,1,0:T(2,128)(2,1)S(1)} %get-tuple-element.32), channel_id=1, source_target_pairs={{4,0},{8,4},{12,8},{16,12},{20,16},{24,20},{28,24},{32,28},{36,32}... | collective-permute-start | bytes 294920 | tf_op jit(solution)/shard_map/ppermute | solution.py:34
  274.6 27.3 %all-to-all-start.6 = ((bf16[384,256,8]{0,2,1:T(8,128)(2,1)}), bf16[384,256,8]{0,2,1:T(8,128)(2,1)}, u32[]{:S(2)}, u32[]{:S(2)}) async-start(bf16[384,256,8]{0,2,1:T(8,128)(2,1)} %copy.236), calls=%async_computation.6 | async-start | bytes 3145728 | tf_op jit(solution)/shard_map/all_to_all | solution.py:16
  301.9 38.5 %all-to-all-start.3 = ((bf16[4,2,49152]{2,1,0:T(2,128)(2,1)}), bf16[4,2,49152]{2,1,0:T(2,128)(2,1)}, u32[]{:S(2)}, u32[]{:S(2)}) async-start(bf16[4,2,49152]{2,1,0:T(2,128)(2,1)} %reshape.110), calls=%async_computation.3 | async-start | bytes 1572864 | tf_op jit(solution)/shard_map/all_to_all | solution.py:145
  317.3 3.0 copy-start.4
  320.3 3.6 copy-start.11
  340.4 28.1 %all-to-all-start.7 = ((bf16[384,8,256]{0,1,2:T(8,128)(2,1)}), bf16[384,8,256]{0,1,2:T(8,128)(2,1)}, u32[]{:S(2)}, u32[]{:S(2)}) async-start(bf16[384,8,256]{0,1,2:T(8,128)(2,1)} %copy.243), calls=%async_computation.7 | async-start | bytes 3145728 | tf_op jit(solution)/shard_map/all_to_all | solution.py:16
  357.1 2.9 copy-start.6
  360.1 2.6 copy-start.7
  360.1 2.6 copy-start.8
  376.8 3.1 copy-start.3
  376.8 3.1 copy-start.12
  (6 other events, 9.4 us)
Sparse Core Ops, SparseCore 0:
  10.6 95.1 all-gather.1
where the time goes:
time: 397 us; the launch traced here: 390 us
  local copies, waits for them, and re-layouts  109 us (27%)
  matrix products  75.1 us (19%)
  other arithmetic  55.2 us (14%)
  blocking collectives  47.4 us (12%)
  waiting for transfers between devices  46.4 us (12%)
  starting transfers between devices  42.2 us (11%)
  between operations  15 us (4%)
    dot_general x24, matrix products, contract(): jnp.einsum(form, left, right, precision=lax.Precision.HIGHEST, preferred_...  58.6 us
    all_to_all x1, blocking collectives, in_one_piece(): lax.all_to_all(both, axis, split_axis=split_dim, concat_axis=concat_dim,...  32.3 us
    slice x19, local copies, waits for them, and re-layouts, in_one_piece(): outs.append(lax.slice_in_dim(out, at, at + a.shape[along], axis=along))  28.1 us
    all_to_all x3, waiting for transfers between devices, in_one_piece(): lax.all_to_all(both, axis, split_axis=split_dim, concat_axis=concat_dim,...  27.9 us
    unnamed x45, local copies, waits for them, and re-layouts  20 us
    convert_element_type x6, local copies, waits for them, and re-layouts, to_channels(): return lax.all_to_all(values.astype(jnp.bfloat16), 'ch', split_axis=0, co...  18.7 us
    convert_element_type x1, other arithmetic, on_device(): (grad_act * gelu_slope(pre_act)).astype(jnp.bfloat16)  17.2 us
    unnamed x4, matrix products  16.5 us
  transfers between devices with their start and end apart: 11, of which 8 were waited for; matrix products, arithmetic and copies ran while one was open for 36% of the time, Pallas kernels for 0%

commit v1 on v0

v1 whole, which is shorter than its diff:
```python
import functools

import jax
import jax.numpy as jnp
import ml_dtypes
import numpy as np
from jax import lax
from jax.experimental import pallas as pl
from jax.experimental.pallas import tpu as pltpu
from jax.sharding import PartitionSpec as P

norm_epsilon = 1e-05
root_half = 0.7071067811865476
density = 0.3989422804014327

ROWS_DEVICES = 32
CH_DEVICES = 4
LEN = 256
SLAB = 8
CH = 192
ALL_CH = 768
LANES = SLAB * CH
WIDE = SLAB * 128
POINTS = LEN * LEN
HALF_UNITS = 384
F32 = jnp.float32
BF16 = jnp.bfloat16
MIB = 1 << 20


def narrow_at(h):
    return WIDE + 64 * (2 * (h % 4) + h // 4)


def columns_of(device):
    base = SLAB * device
    return [base + 1, base + 2, base + 3, base + 4 if device < 16 else base]


def column_tables():
    w = np.arange(LEN)
    forward, inverse = np.zeros((LEN, LEN)), np.zeros((LEN, LEN))
    for device in range(ROWS_DEVICES):
        for j, kw in enumerate(columns_of(device)):
            turn = 2 * np.pi * (kw * w % LEN) / LEN
            re, im = SLAB * device + j, SLAB * device + 4 + j
            if device == 16 and j == 3:
                forward[re] = inverse[re] = 1.0
                forward[im] = inverse[im] = np.where(w % 2 == 0, 1.0, -1.0)
            else:
                forward[re], forward[im] = np.cos(turn), -np.sin(turn)
                inverse[re], inverse[im] = 2 * np.cos(turn), -2 * np.sin(turn)
    return forward, inverse


def row_tables():
    k1, src = np.arange(32)[:, None], np.arange(32)[None, :]
    turn = 2 * np.pi * (k1 * src % 32) / 32
    cos, sin = np.cos(turn), np.sin(turn)
    forward = np.zeros((2, 5, 32, 32, 2, 4))
    inverse = np.zeros((32, 2, 4, 2, 4, 32))
    for j in range(4):
        forward[0, j, :, :, 0, j], forward[0, j, :, :, 1, j] = cos, sin
        forward[1, j, :, :, 0, j], forward[1, j, :, :, 1, j] = -sin, cos
        inverse[:, 0, j, 0, j, :], inverse[:, 0, j, 1, j, :] = cos.T, -sin.T
        inverse[:, 1, j, 0, j, :], inverse[:, 1, j, 1, j, :] = sin.T, cos.T
    forward[0, 4, :, :, 0, 3], forward[0, 4, :, :, 1, 3] = cos, -sin
    forward[1, 4, :, :, 0, 3], forward[1, 4, :, :, 1, 3] = -sin, -cos
    return forward.reshape(320, 256), inverse.reshape(256, 256)


def twiddle_tables():
    token_row = np.zeros(LANES, np.int64)
    for h in range(SLAB):
        token_row[128 * h : 128 * h + 128] = h
        token_row[narrow_at(h) : narrow_at(h) + 64] = h
    turn = 2 * np.pi * (np.arange(32)[:, None] * token_row[None, :] % LEN) / LEN
    return np.cos(turn), np.sin(turn)


def turn_tables():
    k2, k1 = np.divmod(np.arange(LEN), 32)
    kh = k1 + 32 * k2
    straight, mirrored = np.zeros((LEN, LEN)), np.zeros((LEN, LEN))
    straight[np.arange(LEN), kh] = 1.0
    mirrored[np.arange(LEN), -kh % LEN] = 1.0
    return straight, mirrored


def narrow(table):
    return np.asarray(table, np.float64).astype(ml_dtypes.bfloat16)


FORWARD_COLUMNS, INVERSE_COLUMNS = (narrow(t) for t in column_tables())
FORWARD_ROWS, INVERSE_ROWS = (narrow(t) for t in row_tables())
TWIDDLE_COS, TWIDDLE_SIN = (t.astype(np.float32) for t in twiddle_tables())
STRAIGHT, MIRRORED = (narrow(t) for t in turn_tables())
UNIT = narrow(np.eye(LEN))


def nn(a, b):
    return lax.dot_general(a, b, (((1,), (0,)), ((), ())), preferred_element_type=F32)


def nt(a, b):
    return lax.dot_general(a, b, (((1,), (1,)), ((), ())), preferred_element_type=F32)


def tn(a, b):
    return lax.dot_general(a, b, (((0,), (0,)), ((), ())), preferred_element_type=F32)


def kernel_call(body, name, outs, scratch, operands, vmem, flops=0, smem=0):
    whole = pl.BlockSpec(memory_space=pltpu.VMEM)
    scalar = pl.BlockSpec(memory_space=pltpu.SMEM)
    moved = sum(a.size * a.dtype.itemsize for a in operands)
    moved += sum(o.size * np.dtype(o.dtype).itemsize for o in outs)
    return pl.pallas_call(
        body,
        name=name,
        out_shape=tuple(outs),
        in_specs=[scalar] * smem + [whole] * (len(operands) - smem),
        out_specs=tuple(whole for _ in outs),
        scratch_shapes=scratch,
        cost_estimate=pl.CostEstimate(flops=flops, bytes_accessed=moved, transcendentals=0),
        compiler_params=pltpu.CompilerParams(vmem_limit_bytes=vmem * MIB),
    )(*operands)


def shape(dims, dtype):
    return jax.ShapeDtypeStruct(dims, dtype)


def fill_wide(wide_ref, values):
    for side in range(2):
        wide_ref[side] = values[:, side * 128 : side * 128 + 128]


def every_eighth(wide_ref, h):
    return jnp.concatenate([wide_ref[side, pl.ds(h, CH, stride=SLAB), :] for side in range(2)], axis=1)


def put_eighth(wide_ref, first, values):
    for side in range(2):
        at = pl.ds(first, values.shape[0], stride=SLAB)
        wide_ref[side, at, :] = values[:, side * 128 : side * 128 + 128]


def take_wide(wide_ref):
    return jnp.concatenate([wide_ref[side] for side in range(2)], axis=1)


def unfold_rows(source_ref, wide_ref):
    fill_wide(wide_ref, source_ref[...].astype(F32))
    for h in range(SLAB):
        yield h, every_eighth(wide_ref, h).astype(BF16)


def columns_kernel(image_ref, table_ref, message_ref, kept_ref, wide_ref, lanes_ref):
    for h, rows in unfold_rows(image_ref, wide_ref):
        kept_ref[h * CH : (h + 1) * CH] = rows
        lanes_ref[h * 128 : h * 128 + 128] = rows[:128]
        lanes_ref[narrow_at(h) : narrow_at(h) + 64] = rows[128:]
    send_columns(table_ref, lanes_ref, message_ref)


def send_columns(table_ref, lanes_ref, message_ref):
    for at in range(0, LANES, 512):
        message_ref[:, at : at + 512] = nt(table_ref[...], lanes_ref[at : at + 512]).astype(BF16)


def unfold_kernel(source_ref, kept_ref, wide_ref):
    for h, rows in unfold_rows(source_ref, wide_ref):
        kept_ref[h * CH : (h + 1) * CH] = rows


def filter_split_kernel(filter_ref, turned_ref, wide_ref):
    for part in range(2):
        fill_wide(wide_ref, filter_ref[part])
        for i in range(SLAB):
            turned_ref[i, part] = every_eighth(wide_ref, i).astype(BF16)


def put_spectrum(target_ref, part, column, block):
    rows = slice(column * 32, column * 32 + 32)
    for k2 in range(SLAB):
        piece = block[k2 * 32 : k2 * 32 + 32]
        target_ref[part, rows, k2 * 128 : k2 * 128 + 128] = piece[:, :128]
        at = WIDE + 64 * k2
        target_ref[part, rows, at : at + 64] = piece[:, 128:]


def filter_kernel(
    place_ref, own_ref, pair_ref, lone_ref, straight_ref, mirrored_ref, main_ref, cross_ref
):
    device = place_ref[0]
    low, special = device < 16, device == 16
    scale = 0.5 / POINTS
    for part in range(2):
        sign = 1.0 if part == 0 else -1.0
        for j in range(3):
            straight = nt(straight_ref[...], own_ref[1 + j, part])
            mirrored = nt(mirrored_ref[...], pair_ref[3 - j, part])
            put_spectrum(main_ref, part, j, (straight + sign * mirrored) * scale)
        own = jnp.where(low, own_ref[4, part], own_ref[0, part])
        other = jnp.where(low, pair_ref[0, part], lone_ref[part])
        o, q = nt(straight_ref[...], own), nt(straight_ref[...], other)
        o_back = nt(mirrored_ref[...], own) * sign
        q_back = nt(mirrored_ref[...], other) * sign
        usual = (o + q_back) * scale
        put_spectrum(
            main_ref, part, 3, jnp.where(special, (o + o_back + q + q_back) * (0.5 * scale), usual)
        )
        put_spectrum(
            cross_ref,
            part,
            0,
            jnp.where(special, (q + q_back - o - o_back) * (0.5 * scale), 0.0 * usual),
        )


def eighth_turn(value, step, sign):
    re, im = value
    if step == 0:
        return value
    if step == 1:
        return (re + sign * im) * root_half, (im - sign * re) * root_half
    if step == 2:
        return sign * im, -sign * re
    return (sign * im - re) * root_half, (-sign * re - im) * root_half


def add(a, b):
    return a[0] + b[0], a[1] + b[1]


def sub(a, b):
    return a[0] - b[0], a[1] - b[1]


def four_points(x, sign):
    s, d = add(x[0], x[2]), sub(x[0], x[2])
    t, u = add(x[1], x[3]), eighth_turn(sub(x[1], x[3]), 2, sign)
    return [add(s, t), add(d, u), sub(s, t), sub(d, u)]


def eight_points(x, sign):
    even = four_points([add(x[m], x[m + 4]) for m in range(4)], sign)
    odd = four_points([eighth_turn(sub(x[m], x[m + 4]), m, sign) for m in range(4)], sign)
    return [part[q] for q in range(4) for part in (even, odd)]


def upper_lanes(like):
    return lax.broadcasted_iota(jnp.int32, like.shape, 1) >= 64


def halves(value):
    upper = upper_lanes(value)
    return pltpu.roll(value, 64, axis=1) + jnp.where(upper, -value, value)


def upper_turn(value, step, sign):
    upper = upper_lanes(value[0])
    return tuple(jnp.where(upper, b, a) for a, b in zip(value, eighth_turn(value, step, sign)))


def narrow_forward(x, sign):
    turned = [upper_turn((halves(re), halves(im)), m, sign) for m, (re, im) in enumerate(x)]
    return four_points(turned, sign)


def narrow_inverse(x, sign):
    turned = [upper_turn(v, m, sign) for m, v in enumerate(four_points(x, sign))]
    return [(halves(re), halves(im)) for re, im in turned]


def lane_blocks(re, im):
    return [(re[:, at : at + 128], im[:, at : at + 128]) for at in range(0, LANES, 128)]


def to_frequencies(re, im, cos, sin):
    x = lane_blocks(re * cos + im * sin, im * cos - re * sin)
    return eight_points(x[:SLAB], 1.0) + narrow_forward(x[SLAB:], 1.0)


def to_tokens_rows(blocks, cos, sin):
    y = eight_points(blocks[:SLAB], -1.0) + narrow_inverse(blocks[SLAB:], -1.0)
    re = jnp.concatenate([v[0] for v in y], axis=1)
    im = jnp.concatenate([v[1] for v in y], axis=1)
    return re * cos - im * sin, im * cos + re * sin


def row_body(saves, refs):
    place_ref, received_ref, fwd_ref, inv_ref, cos_ref, sin_ref, main_ref, cross_ref = refs[:8]
    if saves:
        message_ref, seen_ref, mixed_ref, ready_ref = refs[8:]
    else:
        seen_ref, message_ref, product_ref, mixed_ref, ready_ref = refs[8:]
    for at in range(0, LANES, 512):
        mixed_ref[:, at : at + 512] = nn(fwd_ref[...], received_ref[:, at : at + 512])

    def spectrum(group):
        at = pl.multiple_of(group * 16, 16)
        table = pl.ds(pl.multiple_of(lax.rem(group, 2) * 16, 16), 16)
        return to_frequencies(
            mixed_ref[pl.ds(at, 16), :],
            mixed_ref[pl.ds(160 + at, 16), :],
            cos_ref[table, :],
            sin_ref[table, :],
        )

    def save(group, blocks):
        at = pl.ds(pl.multiple_of(group * 16, 16), 16)
        for n, value in enumerate(blocks):
            for part in range(2):
                seen_ref[part, at, n * 128 : n * 128 + 128] = value[part].astype(BF16)

    def times(value, n, source_ref, at):
        k_re = source_ref[0, at, n * 128 : n * 128 + 128]
        k_im = source_ref[1, at, n * 128 : n * 128 + 128]
        re, im = value
        if saves:
            return re * k_re - im * k_im, im * k_re + re * k_im
        return re * k_re + im * k_im, im * k_re - re * k_im

    def store_back(group, blocks):
        table = pl.ds(pl.multiple_of(lax.rem(group, 2) * 16, 16), 16)
        re, im = to_tokens_rows(blocks, cos_ref[table, :], sin_ref[table, :])
        at = pl.multiple_of(group * 16, 16)
        ready_ref[pl.ds(at, 16), :] = re.astype(BF16)
        ready_ref[pl.ds(128 + at, 16), :] = im.astype(BF16)

    def seen(group, n):
        at = pl.ds(pl.multiple_of(group * 16, 16), 16)
        return tuple(seen_ref[part, at, n * 128 : n * 128 + 128].astype(F32) for part in range(2))

    def product(a, b, factor):
        re = (a[0] * b[0] + a[1] * b[1]) * factor
        return re, (b[1] * a[0] - b[0] * a[1]) * factor

    def put_product(group, n, value):
        at = pl.ds(pl.multiple_of(group * 16, 16), 16)
        for part in range(2):
            product_ref[part, at, n * 128 : n * 128 + 128] = value[part].astype(BF16)

    def plain(group, carry):
        at = pl.ds(pl.multiple_of(group * 16, 16), 16)
        values = spectrum(group)
        if saves:
            save(group, values)
        else:
            for n, value in enumerate(values):
                put_product(group, n, product(seen(group, n), value, 1.0 / POINTS))
        store_back(group, [times(v, n, main_ref, at) for n, v in enumerate(values)])
        return carry

    def packed(group, carry):
        at = pl.ds(pl.multiple_of(group * 16, 16), 16)
        cross_at = pl.ds(pl.multiple_of((group - 6) * 16, 16), 16)
        values, mirrors = spectrum(group), spectrum(group + 2)
        if saves:
            save(group, values)
            save(group + 2, mirrors)
        else:
            special = place_ref[0] == 16
            for n, (value, mirror) in enumerate(zip(values, mirrors)):
                first, first_mirror = seen(group, n), seen(group + 2, n)
                usual = product(first, value, 1.0 / POINTS)
                odd = product(sub(first, first_mirror), sub(value, mirror), 0.25 / POINTS)
                even = product(add(first, first_mirror), add(value, mirror), 0.25 / POINTS)
                put_product(group, n, [jnp.where(special, a, b) for a, b in zip(odd, usual)])
                put_product(group + 2, n, [jnp.where(special, a, b) for a, b in zip(even, usual)])
        store_back(
            group,
            [
                add(times(v, n, main_ref, at), times(m, n, cross_ref, cross_at))
                for n, (v, m) in enumerate(zip(values, mirrors))
            ],
        )
        return carry

    lax.fori_loop(0, 6, plain, 0)
    lax.fori_loop(6, 8, packed, 0)
    for at in range(0, LANES, 512):
        block = nn(inv_ref[...], ready_ref[:, at : at + 512])
        message_ref[:, at : at + 512] = block.astype(BF16)


def rows_forward_kernel(*refs):
    row_body(True, refs)


def rows_backward_kernel(*refs):
    row_body(False, refs)


def token_rows(received_ref, table_ref, place):
    for h in range(SLAB):
        place(h, 0, tn(received_ref[:, h * 128 : h * 128 + 128], table_ref[...]))
    for m in range(4):
        at = WIDE + 128 * m
        block = tn(received_ref[:, at : at + 128], table_ref[...])
        place(m, 128, block[:64])
        place(m + 4, 128, block[64:])


def tokens_kernel(received_ref, table_ref, filtered_ref, first_ref, last_ref):
    def place(h, channel, block):
        rows = block.astype(BF16)
        filtered_ref[h * CH + channel : h * CH + channel + block.shape[0]] = rows
        if h == 0:
            first_ref[channel : channel + block.shape[0]] = rows
        if h == SLAB - 1:
            last_ref[channel : channel + block.shape[0]] = rows

    token_rows(received_ref, table_ref, place)


def convolve(load, taps, put):
    lane = lax.broadcasted_iota(jnp.int32, (16, LEN), 1)
    window = [load(-1), load(0)]
    for h in range(SLAB):
        window.append(load(h + 1))
        sums = [sum(taps[3 * a + b] * window[a] for a in range(3)) for b in range(3)]
        left = jnp.where(lane == 0, 0.0, pltpu.roll(sums[0], 1, axis=1))
        right = jnp.where(lane == LEN - 1, 0.0, pltpu.roll(sums[2], LEN - 1, axis=1))
        put(h, sums[1] + left + right, window[1])
        window.pop(0)


def rows_at(h, start):
    return pl.ds(pl.multiple_of(h * CH + start, 16), 16)


def spread_taps(taps_ref, start, order):
    taps = taps_ref[pl.ds(start, 16), :]
    return [jnp.broadcast_to(taps[:, k : k + 1], (16, LEN)) for k in order]


def hidden_kernel(filtered_ref, above_ref, below_ref, taps_ref, signal_ref, hidden_ref):
    def chunk(index, carry):
        start = pl.multiple_of(index * 16, 16)

        def load(h):
            if h < 0:
                return above_ref[pl.ds(start, 16), :].astype(F32)
            if h == SLAB:
                return below_ref[pl.ds(start, 16), :].astype(F32)
            return filtered_ref[rows_at(h, start), :].astype(F32)

        def put(h, convolved, middle):
            at = rows_at(h, start)
            hidden_ref[at, :] = (signal_ref[at, :].astype(F32) + convolved).astype(BF16)

        convolve(load, spread_taps(taps_ref, start, range(9)), put)
        return carry

    lax.fori_loop(0, CH // 16, chunk, 0)


def gradient_columns_kernel(
    upstream_ref, mlp_ref, above_ref, below_ref, taps_ref, table_ref, message_ref, natural_ref, lanes_ref
):
    def chunk(index, carry):
        start = pl.multiple_of(index * 16, 16)

        def load(h):
            if h < 0:
                return above_ref[pl.ds(start, 16), :].astype(F32)
            if h == SLAB:
                return below_ref[pl.ds(start, 16), :].astype(F32)
            at = rows_at(h, start)
            return upstream_ref[at, :].astype(F32) + mlp_ref[at, :].astype(F32)

        def put(h, convolved, middle):
            natural_ref[rows_at(h, start), :] = convolved.astype(BF16)

        convolve(load, spread_taps(taps_ref, start, range(8, -1, -1)), put)
        return carry

    lax.fori_loop(0, CH // 16, chunk, 0)
    for h in range(SLAB):
        lanes_ref[h * 128 : h * 128 + 128] = natural_ref[h * CH : h * CH + 128]
        lanes_ref[narrow_at(h) : narrow_at(h) + 64] = natural_ref[h * CH + 128 : (h + 1) * CH]
    send_columns(table_ref, lanes_ref, message_ref)


def gelu_parts(pre_act):
    cumulative = 0.5 * (1.0 + lax.erf(pre_act * root_half))
    bell = density * jnp.exp(-0.5 * pre_act * pre_act)
    return pre_act * cumulative, cumulative + pre_act * bell


def mlp_kernel(
    hidden_ref,
    upstream_ref,
    gain_ref,
    unit_ref,
    mine_ref,
    other_ref,
    out_ref,
    grad_ref,
    gathered_ref,
    scaled_ref,
    dy_ref,
    normed_ref,
    inv_ref,
    out_sum_ref,
    grad_sum_ref,
):
    step = pl.program_id(0)

    def turn_in(source_ref, half):
        for src in range(CH_DEVICES):
            at = src * 2 * CH + half * CH
            gathered_ref[src * CH : (src + 1) * CH] = source_ref[at : at + CH]
        return nt(unit_ref[...], gathered_ref[...])

    @pl.when(step == 0)
    def _():
        for half in range(2):
            rows = slice(half * LEN, half * LEN + LEN)
            values = turn_in(hidden_ref, half)
            centred = values - jnp.mean(values, axis=1, keepdims=True)
            variance = jnp.mean(centred * centred, axis=1, keepdims=True)
            inv_std = lax.rsqrt(variance + norm_epsilon)
            normed = centred * inv_std
            normed_ref[rows] = normed
            inv_ref[rows] = jnp.broadcast_to(inv_std, (LEN, 128))
            scaled_ref[rows] = (normed * gain_ref[...]).astype(BF16)
            dy_ref[rows] = turn_in(upstream_ref, half).astype(BF16)
        out_sum_ref[...] = jnp.zeros_like(out_sum_ref)
        grad_sum_ref[...] = jnp.zeros_like(grad_sum_ref)

    for weights_ref in (mine_ref, other_ref):
        up, down = weights_ref[:, :ALL_CH], weights_ref[:, ALL_CH:]
        pre_act = nt(scaled_ref[...], up)
        grad_act = nt(dy_ref[...], down)
        activated, slope = gelu_parts(pre_act)
        out_sum_ref[...] += nn(activated.astype(BF16), down)
        grad_sum_ref[...] += nn((grad_act * slope).astype(BF16), up)

    def turn_out(values, half, target_ref):
        for block in range(3):
            piece = nt(unit_ref[...], values[:, block * LEN : (block + 1) * LEN])
            gathered_ref[block * LEN : (block + 1) * LEN] = piece.astype(BF16)
        for dst in range(CH_DEVICES):
            at = (dst * 2 + half) * CH
            target_ref[at : at + CH] = gathered_ref[dst * CH : (dst + 1) * CH]

    @pl.when(step == pl.num_programs(0) - 1)
    def _():
        for half in range(2):
            rows = slice(half * LEN, half * LEN + LEN)
            weighted = grad_sum_ref[rows] * gain_ref[...]
            normed = normed_ref[rows]
            first = jnp.mean(weighted, axis=1, keepdims=True)
            second = jnp.mean(weighted * normed, axis=1, keepdims=True)
            term = inv_ref[rows, 0:1] * (weighted - first - normed * second)
            turn_out(term.astype(BF16), half, grad_ref)
            turn_out(out_sum_ref[rows].astype(BF16), half, out_ref)


def mlp(hidden, upstream, gain, mine, other, block=256):
    tokens, units = 2 * LEN, CH_DEVICES * HALF_UNITS
    whole = pl.BlockSpec(memory_space=pltpu.VMEM)
    weights = pl.BlockSpec((block, 2 * ALL_CH), lambda i: (i, 0))
    return pl.pallas_call(
        mlp_kernel,
        name="mlp",
        grid=(units // block,),
        out_shape=(shape((LANES, LEN), BF16),) * 2,
        in_specs=[whole] * 4 + [weights] * 2,
        out_specs=(whole,) * 2,
        scratch_shapes=[
            pltpu.VMEM((ALL_CH, LEN), BF16),
            pltpu.VMEM((tokens, ALL_CH), BF16),
            pltpu.VMEM((tokens, ALL_CH), BF16),
            pltpu.VMEM((tokens, ALL_CH), F32),
            pltpu.VMEM((tokens, 128), F32),
            pltpu.VMEM((tokens, ALL_CH), F32),
            pltpu.VMEM((tokens, ALL_CH), F32),
        ],
        cost_estimate=pl.CostEstimate(
            flops=16 * tokens * units * ALL_CH,
            bytes_accessed=8 * units * ALL_CH + 8 * LANES * LEN,
            transcendentals=2 * tokens * units,
        ),
        compiler_params=pltpu.CompilerParams(vmem_limit_bytes=48 * MIB),
    )(hidden, upstream, gain, jnp.asarray(UNIT), mine, other)


def block_out_kernel(hidden_ref, sum_ref, out_ref, wide_ref):
    for h in range(SLAB):
        rows = slice(h * CH, (h + 1) * CH)
        total = hidden_ref[rows].astype(F32) + sum_ref[rows].astype(F32)
        put_eighth(wide_ref, h, total)
    out_ref[...] = take_wide(wide_ref).astype(BF16)


def image_kernel(received_ref, table_ref, upstream_ref, mlp_ref, out_ref, wide_ref):
    def place(h, channel, block):
        count = block.shape[0]
        rows = slice(h * CH + channel, h * CH + channel + count)
        total = block + upstream_ref[rows].astype(F32) + mlp_ref[rows].astype(F32)
        put_eighth(wide_ref, channel * SLAB + h, total)

    token_rows(received_ref, table_ref, place)
    out_ref[...] = take_wide(wide_ref)


def unturn_kernel(product_ref, straight_ref, mirrored_ref, own_ref, pair_ref, lone_ref, block_ref):
    def gather(part, column):
        rows = slice(column * 32, column * 32 + 32)
        for k2 in range(SLAB):
            to = slice(k2 * 32, k2 * 32 + 32)
            at = WIDE + 64 * k2
            block_ref[to, :128] = product_ref[part, rows, k2 * 128 : k2 * 128 + 128]
            block_ref[to, 128:] = product_ref[part, rows, at : at + 64]

    for part in range(2):
        sign = 1.0 if part == 0 else -1.0
        for j in range(4):
            gather(part, j)
            own_ref[j, part] = tn(block_ref[...], straight_ref[...]).astype(BF16)
            pair_ref[3 - j, part] = (tn(block_ref[...], mirrored_ref[...]) * sign).astype(BF16)
        gather(part, 4)
        lone_ref[part] = (tn(block_ref[...], mirrored_ref[...]) * sign).astype(BF16)


def grad_filter_kernel(place_ref, own_ref, pair_ref, lone_ref, out_ref, wide_ref):
    low = place_ref[0] < 16
    for part in range(2):
        parts = [jnp.where(low, lone_ref[part], own_ref[3, part])]
        parts += [own_ref[j, part] for j in range(3)]
        parts += [jnp.where(low, own_ref[3, part], pair_ref[0, part])]
        parts += [pair_ref[n, part] for n in range(1, 4)]
        for i, value in enumerate(parts):
            put_eighth(wide_ref, i, value.astype(F32))
        out_ref[part] = take_wide(wide_ref)


def to_peers(values, axis):
    return lax.all_to_all(values, axis, split_axis=0, concat_axis=0, tiled=True)


def halo(first, last):
    down = [(i, i + 1) for i in range(ROWS_DEVICES - 1)]
    up = [(i + 1, i) for i in range(ROWS_DEVICES - 1)]
    return lax.ppermute(last, "rows", down), lax.ppermute(first, "rows", up)


def on_device(tile_image, spectral_filter, conv_taps, norm_gain, up_weight, down_weight, upstream):
    device = lax.axis_index("rows")
    place = device.reshape(1).astype(jnp.int32)
    flat = (LANES, LEN)
    tables = [jnp.asarray(t) for t in (FORWARD_ROWS, INVERSE_ROWS, TWIDDLE_COS, TWIDDLE_SIN)]
    forward_columns, inverse_columns = jnp.asarray(FORWARD_COLUMNS), jnp.asarray(INVERSE_COLUMNS)
    straight, mirrored = jnp.asarray(STRAIGHT), jnp.asarray(MIRRORED)

    start = lax.rem(device, 2) * HALF_UNITS
    own_up = lax.dynamic_slice_in_dim(up_weight, start, HALF_UNITS, axis=1).T
    own_down = lax.dynamic_slice_in_dim(down_weight, start, HALF_UNITS, axis=0)
    mine = lax.all_gather(jnp.concatenate([own_up, own_down], axis=1), "ch", axis=0, tiled=True)
    other = lax.ppermute(mine, "rows", [(i, i ^ 1) for i in range(ROWS_DEVICES)])

    wide = pltpu.VMEM((2, LANES, 128), F32)
    lanes = pltpu.VMEM(flat, BF16)
    message, signal = kernel_call(
        columns_kernel,
        "columns",
        [shape((LEN, LANES), BF16), shape(flat, BF16)],
        [wide, lanes],
        [tile_image.reshape(flat), forward_columns],
        24,
        2 * LEN * LEN * LANES,
    )
    received = to_peers(message, "rows")
    (dy,) = kernel_call(
        unfold_kernel, "unfold", [shape(flat, BF16)], [wide], [upstream.reshape(flat)], 16
    )
    (own_filter,) = kernel_call(
        filter_split_kernel,
        "filter_split",
        [shape((SLAB, 2, CH, LEN), BF16)],
        [wide],
        [spectral_filter.reshape(2, LANES, LEN)],
        24,
    )
    opposite = [(i, ROWS_DEVICES - 1 - i) for i in range(ROWS_DEVICES)]
    lone_in = [(i, ROWS_DEVICES - i) for i in range(1, 16)] + [(0, 16)]
    pair_filter = lax.ppermute(own_filter[4:], "rows", opposite)
    lone_filter = lax.ppermute(own_filter[0], "rows", lone_in)
    main, cross = kernel_call(
        filter_kernel,
        "filter",
        [shape((2, 128, LANES), F32), shape((2, 32, LANES), F32)],
        [],
        [place, own_filter, pair_filter, lone_filter, straight, mirrored],
        32,
        2 * 14 * LEN * LEN * CH,
        smem=1,
    )
    dy_tokens = to_peers(dy, "ch")

    row_scratch = [pltpu.VMEM((320, LANES), F32), pltpu.VMEM((LEN, LANES), BF16)]
    message, seen = kernel_call(
        rows_forward_kernel,
        "rows_forward",
        [shape((LEN, LANES), BF16), shape((2, 160, LANES), BF16)],
        row_scratch,
        [place, received, *tables, main, cross],
        24,
        2 * 576 * LEN * LANES,
        smem=1,
    )
    received = to_peers(message, "rows")
    filtered, first, last = kernel_call(
        tokens_kernel,
        "tokens",
        [shape(flat, BF16), shape((CH, LEN), BF16), shape((CH, LEN), BF16)],
        [],
        [received, inverse_columns],
        24,
        2 * LEN * LEN * LANES,
    )
    above, below = halo(first, last)
    (hidden,) = kernel_call(
        hidden_kernel,
        "hidden",
        [shape(flat, BF16)],
        [],
        [filtered, above, below, conv_taps, signal],
        24,
    )
    hidden_tokens = to_peers(hidden, "ch")
    out_message, grad_message = mlp(
        hidden_tokens, dy_tokens, norm_gain.reshape(1, ALL_CH), mine, other
    )
    grad_mlp = to_peers(grad_message, "ch")
    edges = [
        (dy[at].astype(F32) + grad_mlp[at].astype(F32)).astype(BF16)
        for at in (slice(0, CH), slice(LANES - CH, LANES))
    ]
    above, below = halo(*edges)
    (message,) = kernel_call(
        gradient_columns_kernel,
        "gradient_columns",
        [shape((LEN, LANES), BF16)],
        [lanes, lanes],
        [dy, grad_mlp, above, below, conv_taps, forward_columns],
        24,
        2 * LEN * LEN * LANES,
    )
    received = to_peers(message, "rows")
    out_sum = to_peers(out_message, "ch")
    (block_out,) = kernel_call(
        block_out_kernel, "block_out", [shape(flat, BF16)], [wide], [hidden, out_sum], 24
    )
    message, products = kernel_call(
        rows_backward_kernel,
        "rows_backward",
        [shape((LEN, LANES), BF16), shape((2, 160, LANES), BF16)],
        row_scratch,
        [place, received, *tables, main, cross, seen],
        24,
        2 * 576 * LEN * LANES,
        smem=1,
    )
    received = to_peers(message, "rows")
    own, pair, lone = kernel_call(
        unturn_kernel,
        "unturn",
        [shape((4, 2, CH, LEN), BF16), shape((4, 2, CH, LEN), BF16), shape((2, CH, LEN), BF16)],
        [pltpu.VMEM((LEN, CH), BF16)],
        [products, straight, mirrored],
        24,
        2 * 18 * LEN * LEN * CH,
    )
    pair = lax.ppermute(pair, "rows", opposite)
    lone = lax.ppermute(lone, "rows", [(b, a) for a, b in lone_in])
    (grad_filter,) = kernel_call(
        grad_filter_kernel,
        "grad_filter",
        [shape((2, LANES, LEN), F32)],
        [wide],
        [place, own, pair, lone],
        24,
        smem=1,
    )
    (grad_image,) = kernel_call(
        image_kernel,
        "image",
        [shape(flat, F32)],
        [wide],
        [received, inverse_columns, dy, grad_mlp],
        24,
        2 * LEN * LEN * LANES,
    )
    slab = (CH, SLAB, LEN)
    return (
        block_out.reshape(slab),
        grad_image.reshape(slab),
        grad_filter.reshape(2, CH, SLAB, LEN),
    )


def solution(mesh):
    return jax.shard_map(
        on_device,
        mesh=mesh,
        in_specs=(
            P("ch", "rows", None),
            P(None, "ch", "rows", None),
            P("ch", None),
            P(),
            P(None, "ch"),
            P("ch", None),
            P("ch", "rows", None),
        ),
        out_specs=(P("ch", "rows", None), P("ch", "rows", None), P(None, "ch", "rows", None)),
        check_vma=False,
    )
```

time: 397 us -> 315 us (0.79); the launches traced: 390 us -> 313 us
  local copies, waits for them, and re-layouts: 109 us -> 30.3 us
  waiting for transfers between devices: 46.4 us -> 124 us
  matrix products: 75.1 us -> 0 us
  other arithmetic: 55.2 us -> 2.09 us
  Pallas kernels: 0 us -> 47.7 us
  starting transfers between devices: 42.2 us -> 58.5 us
  blocking collectives: 47.4 us -> 35.7 us
    dot_general x24 -> x0, matrix products: 58.6 us -> none  [contract(): jnp.einsum(form, left, right, precision=lax.Precision.HIGHEST, preferred_...]
    all_gather x1, waiting for transfers between devices: 0.01 us -> 56.1 us  [on_device(): lax.all_gather(jnp.concatenate([own_up, own_down], axis=1), 'ch', axis=0,...]
    pallas_call x0 -> x14, Pallas kernels: none -> 47.7 us  [the longest x13 31.5 us: kernel_call(): pl.pallas_call(body, name=name, out_shape=tuple(outs), in_specs=[scalar]...]
    convert_element_type x10 -> x1, other arithmetic: 35.8 us -> 0.99 us  [on_device(): (dy[at].astype(F32) + grad_mlp[at].astype(F32)).astype(BF16)]
    slice x22 -> x1, local copies, waits for them, and re-layouts: 28.7 us -> 0.93 us  [on_device(): pair_filter = lax.ppermute(own_filter[4:], 'rows', opposite)]
    convert_element_type x9 -> x0, local copies, waits for them, and re-layouts: 26.8 us -> none  [the longest x6 18.7 us: to_channels(): return lax.all_to_all(values.astype(jnp.bfloat16), 'ch', split_axis=0, co...]
    unnamed x4 -> x0, matrix products: 16.5 us -> none
    ppermute x4 -> x9, starting transfers between devices: 13.8 us -> 27.8 us  [the longest x4 12.6 us: halo(): return (lax.ppermute(last, 'rows', down), lax.ppermute(first, 'rows', up))]
  transfers between devices with their start and end apart: 11 -> 16, of which waited for: 8 -> 8; matrix products, arithmetic and copies ran while one was open for 36% -> 0% of each run, Pallas kernels for 0% -> 7%
where the time goes in v1:
time: 315 us; the launch traced here: 313 us
  waiting for transfers between devices  124 us (39%)
  starting transfers between devices  58.5 us (19%)
  Pallas kernels  47.7 us (15%)
  blocking collectives  35.7 us (11%)
  local copies, waits for them, and re-layouts  30.3 us (10%)
  between operations  14.4 us (5%)
    all_gather x1, waiting for transfers between devices, on_device(): lax.all_gather(jnp.concatenate([own_up, own_down], axis=1), 'ch', axis=0,...  56.1 us
    all_to_all x6, waiting for transfers between devices, to_peers(): return lax.all_to_all(values, axis, split_axis=0, concat_axis=0, tiled=True)  45.3 us
    all_to_all x2, blocking collectives, to_peers(): return lax.all_to_all(values, axis, split_axis=0, concat_axis=0, tiled=True)  35.7 us
    pallas_call x13, Pallas kernels, kernel_call(): pl.pallas_call(body, name=name, out_shape=tuple(outs), in_specs=[scalar]...  31.5 us
    all_to_all x6, starting transfers between devices, to_peers(): return lax.all_to_all(values, axis, split_axis=0, concat_axis=0, tiled=True)  30.6 us
    unnamed x86, local copies, waits for them, and re-layouts  29.3 us
    ppermute x1, waiting for transfers between devices, on_device(): lone_filter = lax.ppermute(own_filter[0], 'rows', lone_in)  17.1 us
    pallas_call x1, Pallas kernels, mlp(): pl.pallas_call(mlp_kernel, name='mlp', grid=(units // block,), out_shape=...  16.2 us
  transfers between devices with their start and end apart: 16, of which 8 were waited for; matrix products, arithmetic and copies ran while one was open for 0% of the time, Pallas kernels for 7%

profile of v1, /device:TPU:1, one launch (start us, length us, event | category | flops | bytes accessed | tf_op | source)
XLA Modules:
  0.0 313.0 jit_solution(10555692908085867963)
XLA Ops:
  10.0 56.1 %all-gather.2.cloned.1.call-done.mine_ref = bf16[1536,1536]{1,0:T(8,128)(2,1)} async-done(((bf16[384,1536]{1,0:T(8,128)(2,1)}), bf16[1536,1536]{1,0:T(8,128)(2,1)}) %all-gather.2.cloned.1.call-update) | async-done | bytes 4718608 | tf_op jit(solution)/shard_map/all_gather | solution.py:664
  70.5 4.7 %collective-permute-start = (bf16[4,2,192,256]{3,2,1,0:T(8,128)(2,1)}, bf16[4,2,192,256]{3,2,1,0:T(8,128)(2,1)}, u32[]{:S(2)}, u32[]{:S(2)}) collective-permute-start(bf16[4,2,192,256]{3,2,1,0:T(8,128)(2,1)} %slice.24), channel_id=1, source_target_pairs={{0,124},{4,120},{8,116},{12,112},{16,108},{20,104},{24,100},{28,96... | collective-permute-start | bytes 2359304 | tf_op jit(solution)/shard_map/ppermute | solution.py:692
  77.5 4.1 %all-to-all-start = ((bf16[32,8,1536]{2,1,0:T(8,128)(2,1)}), bf16[32,8,1536]{2,1,0:T(8,128)(2,1)S(1)}, u32[]{:S(2)}, u32[]{:S(2)}) async-start(bf16[32,8,1536]{2,1,0:T(8,128)(2,1)} %bitcast.40), calls=%async_computation | async-start | bytes 1572864 | tf_op jit(solution)/shard_map/all_to_all | solution.py:644
  81.6 6.8 %collective-permute-start.1 = (bf16[2,192,256]{2,1,0:T(8,128)(2,1)S(1)}, bf16[2,192,256]{2,1,0:T(8,128)(2,1)S(1)}, u32[]{:S(2)}, u32[]{:S(2)}) collective-permute-start(bf16[2,192,256]{2,1,0:T(8,128)(2,1)S(1)} %slice_bitcast_fusion), channel_id=1, source_target_pairs={{4,124},{8,120},{12,116},{16,112},{20,108},{24,104},{28,100},{32,9... | collective-permute-start | bytes 589832 | tf_op jit(solution)/shard_map/ppermute | solution.py:693
  88.5 17.1 %collective-permute-done.1.lone_ref = bf16[2,192,256]{2,1,0:T(8,128)(2,1)S(1)} collective-permute-done((bf16[2,192,256]{2,1,0:T(8,128)(2,1)S(1)}, bf16[2,192,256]{2,1,0:T(8,128)(2,1)S(1)}, u32[]{:S(2)}, u32[]{:S(2)}) %collective-permute-start.1) | collective-permute-done | bytes 196640 | tf_op jit(solution)/shard_map/ppermute | solution.py:693
  122.0 9.4 %all-to-all-start.1 = ((bf16[32,8,1536]{2,1,0:T(8,128)(2,1)}), bf16[32,8,1536]{2,1,0:T(8,128)(2,1)S(1)}, u32[]{:S(2)}, u32[]{:S(2)}) async-start(bf16[32,8,1536]{2,1,0:T(8,128)(2,1)} %bitcast.42), calls=%async_computation.1 | async-start | bytes 1572864 | tf_op jit(solution)/shard_map/all_to_all | solution.py:644
  132.7 12.9 %all-to-all-done.1 = bf16[32,8,1536]{2,1,0:T(8,128)(2,1)S(1)} async-done(((bf16[32,8,1536]{2,1,0:T(8,128)(2,1)}), bf16[32,8,1536]{2,1,0:T(8,128)(2,1)S(1)}, u32[]{:S(2)}, u32[]{:S(2)}) %all-to-all-start.1) | async-done | bytes 786464 | tf_op jit(solution)/shard_map/all_to_all | solution.py:644
  145.6 3.5 %all-to-all-start.3 = ((bf16[4,384,256]{2,1,0:T(8,128)(2,1)}), bf16[4,384,256]{2,1,0:T(8,128)(2,1)S(1)}, u32[]{:S(2)}, u32[]{:S(2)}) async-start(bf16[4,384,256]{2,1,0:T(8,128)(2,1)} %bitcast.11), calls=%async_computation.3 | async-start | bytes 1572864 | tf_op jit(solution)/shard_map/all_to_all | solution.py:644
  156.4 4.2 %collective-permute-done.3.below_ref = bf16[192,256]{1,0:T(8,128)(2,1)S(1)} collective-permute-done((bf16[192,256]{1,0:T(8,128)(2,1)}, bf16[192,256]{1,0:T(8,128)(2,1)S(1)}, u32[]{:S(2)}, u32[]{:S(2)}) %collective-permute-start.3) | collective-permute-done | bytes 98336 | tf_op jit(solution)/shard_map/ppermute | solution.py:650
  161.7 3.6 %hidden.1.hidden_ref = bf16[1536,256]{1,0:T(8,128)(2,1)} custom-call(bf16[1536,256]{1,0:T(8,128)(2,1)S(1)} %copy-done.24, bf16[192,256]{1,0:T(8,128)(2,1)S(1)} %collective-permute-done.2.above_ref, bf16[192,256]{1,0:T(8,128)(2,1)S(1)} %collective-permute-done.3.below_ref, f32[192,9]{1,0:T(8,128)S(1)} %copy.19.taps_ref, bf16[1536,256]{1,0:T(8,128)(2,1)S(1)} %copy-done.22), custom_call_target="tpu_custom_call" | custom-call | bytes 2562816 | tf_op jit(solution)/shard_map/hidden/pallas_call | solution.py:118
  165.3 4.3 %all-to-all-start.2 = ((bf16[4,384,256]{2,1,0:T(8,128)(2,1)}), bf16[4,384,256]{2,1,0:T(8,128)(2,1)S(1)}, u32[]{:S(2)}, u32[]{:S(2)}) async-start(bf16[4,384,256]{2,1,0:T(8,128)(2,1)} %bitcast.8), calls=%async_computation.2 | async-start | bytes 1572864 | tf_op jit(solution)/shard_map/all_to_all | solution.py:644
  169.6 10.6 %all-to-all-done.2 = bf16[4,384,256]{2,1,0:T(8,128)(2,1)S(1)} async-done(((bf16[4,384,256]{2,1,0:T(8,128)(2,1)}), bf16[4,384,256]{2,1,0:T(8,128)(2,1)S(1)}, u32[]{:S(2)}, u32[]{:S(2)}) %all-to-all-start.2) | async-done | bytes 786464 | tf_op jit(solution)/shard_map/all_to_all | solution.py:644
  180.2 16.2 %mlp.1 = (bf16[1536,256]{1,0:T(8,128)(2,1)S(1)}, bf16[1536,256]{1,0:T(8,128)(2,1)S(1)}) custom-call(bf16[1536,256]{1,0:T(8,128)(2,1)S(1)} %bitcast.41, bf16[1536,256]{1,0:T(8,128)(2,1)S(1)} %bitcast.38, f32[1,768]{1,0:T(1,128)S(1)} %reshape.50.gain_ref, bf16[256,256]{1,0:T(8,128)(2,1)S(1)} %copy-done.34, ...), custom_call_target="tpu_custom_call" | custom-call | flops 9663676416 | bytes 12582912 | tf_op jit(solution)/shard_map/mlp/pallas_call | solution.py:568
  196.4 14.2 %all_to_all.88 = bf16[4,384,256]{2,1,0:T(8,128)(2,1)S(1)} all-to-all(bf16[4,384,256]{2,1,0:T(8,128)(2,1)S(1)} %bitcast.43), channel_id=1, replica_groups=mesh['rows'=32,'ch'=4] {'ch'}, dimensions={0} | all-to-all | bytes 1572864 | tf_op jit(solution)/shard_map/all_to_all | solution.py:644
  213.5 6.3 %collective-permute-start.5 = (bf16[192,256]{1,0:T(8,128)(2,1)S(1)}, bf16[192,256]{1,0:T(8,128)(2,1)S(1)}, u32[]{:S(2)}, u32[]{:S(2)}) collective-permute-start(bf16[192,256]{1,0:T(8,128)(2,1)S(1)} %get-tuple-element.36), channel_id=1, source_target_pairs={{0,4},{4,8},{8,12},{12,16},{16,20},{20,24},{24,28},{28,32},{32,36}... | collective-permute-start | bytes 294920 | tf_op jit(solution)/shard_map/ppermute | solution.py:650
  221.5 4.2 %gradient_columns.1 = bf16[256,1536]{1,0:T(8,128)(2,1)S(1)} custom-call(bf16[1536,256]{1,0:T(8,128)(2,1)} %unfold.1.upstream_ref, bf16[1536,256]{1,0:T(8,128)(2,1)S(1)} %bitcast.27, bf16[192,256]{1,0:T(8,128)(2,1)S(1)} %collective-permute-done.5.above_ref, bf16[192,256]{1,0:T(8,128)(2,1)S(1)} %collective-permute-done.6.below_ref, ...), custom_call_target="tpu_custom_call" | custom-call | flops 201326592 | bytes 2693888 | tf_op jit(solution)/shard_map/gradient_columns/pallas_call | solution.py:118
  225.8 21.5 %all_to_all.89 = bf16[32,8,1536]{2,1,0:T(8,128)(2,1)} all-to-all(bf16[32,8,1536]{2,1,0:T(8,128)(2,1)S(1)} %bitcast.33), channel_id=1, replica_groups=mesh['rows'=32,'ch'=4] {'rows'}, dimensions={0} | all-to-all | bytes 1572864 | tf_op jit(solution)/shard_map/all_to_all | solution.py:644
  247.3 4.2 %all-to-all-start.4 = ((bf16[4,384,256]{2,1,0:T(8,128)(2,1)}), bf16[4,384,256]{2,1,0:T(8,128)(2,1)}, u32[]{:S(2)}, u32[]{:S(2)}) async-start(bf16[4,384,256]{2,1,0:T(8,128)(2,1)} %bitcast.37), calls=%async_computation.4 | async-start | bytes 1572864 | tf_op jit(solution)/shard_map/all_to_all | solution.py:644
  258.5 3.1 rows_backward.1
  267.3 5.2 %all-to-all-start.7 = ((bf16[32,8,1536]{2,1,0:T(8,128)(2,1)}), bf16[32,8,1536]{2,1,0:T(8,128)(2,1)S(1)}, u32[]{:S(2)}, u32[]{:S(2)}) async-start(bf16[32,8,1536]{2,1,0:T(8,128)(2,1)} %bitcast.39), calls=%async_computation.7 | async-start | bytes 1572864 | tf_op jit(solution)/shard_map/all_to_all | solution.py:644
  273.8 2.8 block_out.1
  276.6 21.9 %all-to-all-done.7 = bf16[32,8,1536]{2,1,0:T(8,128)(2,1)S(1)} async-done(((bf16[32,8,1536]{2,1,0:T(8,128)(2,1)}), bf16[32,8,1536]{2,1,0:T(8,128)(2,1)S(1)}, u32[]{:S(2)}, u32[]{:S(2)}) %all-to-all-start.7) | async-done | bytes 786464 | tf_op jit(solution)/shard_map/all_to_all | solution.py:644
  299.3 2.9 image.1
  302.2 3.9 %grad_filter.1 = f32[2,1536,256]{2,1,0:T(8,128)} custom-call(s32[1]{0:T(128)} %bitcast.place_ref.refs_0_, bf16[4,2,192,256]{3,2,1,0:T(8,128)(2,1)S(1)} %get-tuple-element.32.own_ref, bf16[4,2,192,256]{3,2,1,0:T(8,128)(2,1)} %collective-permute-done.7.pair_ref, bf16[2,192,256]{2,1,0:T(8,128)(2,1)} %collective-permute-done.8.lone_ref), custom_call_target="tpu_custom_call" | custom-call | bytes 4915204 | tf_op jit(solution)/shard_map/grad_filter/pallas_call | solution.py:118
  (118 shorter events, 55.0 us)
Async XLA Ops:
  7.2 58.9 %all-gather.2.cloned.1.call-start = ((), (), s32[]{:S(2)}) async-start(), calls=%async_computation.8 | async-start | bytes 5898240 | tf_op jit(solution)/shard_map/all_gather | solution.py:664
  66.1 114.1 %collective-permute-start.4 = (bf16[1536,1536]{1,0:T(8,128)(2,1)}, bf16[1536,1536]{1,0:T(8,128)(2,1)}, u32[]{:S(2)}, u32[]{:S(2)}) collective-permute-start(bf16[1536,1536]{1,0:T(8,128)(2,1)} %all-gather.2.cloned.1.call-done.mine_ref), channel_id=1, source_target_pairs={{0,4},{4,0},{8,12},{12,8},{16,20},{20,16},{24,28},{28,24},{32,36},... | collective-permute-start | bytes 14155784 | tf_op jit(solution)/shard_map/ppermute | solution.py:665
  70.5 35.1 %collective-permute-start = (bf16[4,2,192,256]{3,2,1,0:T(8,128)(2,1)}, bf16[4,2,192,256]{3,2,1,0:T(8,128)(2,1)}, u32[]{:S(2)}, u32[]{:S(2)}) collective-permute-start(bf16[4,2,192,256]{3,2,1,0:T(8,128)(2,1)} %slice.24), channel_id=1, source_target_pairs={{0,124},{4,120},{8,116},{12,112},{16,108},{20,104},{24,100},{28,96... | collective-permute-start | bytes 2359304 | tf_op jit(solution)/shard_map/ppermute | solution.py:692
  77.5 33.9 %all-to-all-start = ((bf16[32,8,1536]{2,1,0:T(8,128)(2,1)}), bf16[32,8,1536]{2,1,0:T(8,128)(2,1)S(1)}, u32[]{:S(2)}, u32[]{:S(2)}) async-start(bf16[32,8,1536]{2,1,0:T(8,128)(2,1)} %bitcast.40), calls=%async_computation | async-start | bytes 1572864 | tf_op jit(solution)/shard_map/all_to_all | solution.py:644
  81.6 23.9 %collective-permute-start.1 = (bf16[2,192,256]{2,1,0:T(8,128)(2,1)S(1)}, bf16[2,192,256]{2,1,0:T(8,128)(2,1)S(1)}, u32[]{:S(2)}, u32[]{:S(2)}) collective-permute-start(bf16[2,192,256]{2,1,0:T(8,128)(2,1)S(1)} %slice_bitcast_fusion), channel_id=1, source_target_pairs={{4,124},{8,120},{12,116},{16,112},{20,108},{24,104},{28,100},{32,9... | collective-permute-start | bytes 589832 | tf_op jit(solution)/shard_map/ppermute | solution.py:693
  122.0 9.4 %copy-start.16 = (bf16[192,8,256]{2,1,0:T(8,128)(2,1)S(1)}, bf16[192,8,256]{2,1,0:T(8,128)(2,1)}, u32[]{:S(2)}) copy-start(bf16[192,8,256]{2,1,0:T(8,128)(2,1)} %param.22) | copy-start | bytes 2359300
  122.0 23.6 %all-to-all-start.1 = ((bf16[32,8,1536]{2,1,0:T(8,128)(2,1)}), bf16[32,8,1536]{2,1,0:T(8,128)(2,1)S(1)}, u32[]{:S(2)}, u32[]{:S(2)}) async-start(bf16[32,8,1536]{2,1,0:T(8,128)(2,1)} %bitcast.42), calls=%async_computation.1 | async-start | bytes 1572864 | tf_op jit(solution)/shard_map/all_to_all | solution.py:644
  132.7 23.6 %copy-start.40 = (f32[192,9]{0,1:T(8,128)S(1)}, f32[192,9]{0,1:T(8,128)}, u32[]{:S(2)}) copy-start(f32[192,9]{0,1:T(8,128)} %param.18) | copy-start | bytes 20740
  132.7 27.9 %copy-start.22 = (bf16[1536,256]{1,0:T(8,128)(2,1)S(1)}, bf16[1536,256]{1,0:T(8,128)(2,1)}, u32[]{:S(2)}) copy-start(bf16[1536,256]{1,0:T(8,128)(2,1)} %copy-done.21) | copy-start | bytes 2359300
  145.6 19.7 %all-to-all-start.3 = ((bf16[4,384,256]{2,1,0:T(8,128)(2,1)}), bf16[4,384,256]{2,1,0:T(8,128)(2,1)S(1)}, u32[]{:S(2)}, u32[]{:S(2)}) async-start(bf16[4,384,256]{2,1,0:T(8,128)(2,1)} %bitcast.11), calls=%async_computation.3 | async-start | bytes 1572864 | tf_op jit(solution)/shard_map/all_to_all | solution.py:644
  151.9 4.5 %collective-permute-start.2 = (bf16[192,256]{1,0:T(8,128)(2,1)}, bf16[192,256]{1,0:T(8,128)(2,1)S(1)}, u32[]{:S(2)}, u32[]{:S(2)}) collective-permute-start(bf16[192,256]{1,0:T(8,128)(2,1)} %get-tuple-element.24), channel_id=1, source_target_pairs={{0,4},{4,8},{8,12},{12,16},{16,20},{20,24},{24,28},{28,32},{32,36}... | collective-permute-start | bytes 294920 | tf_op jit(solution)/shard_map/ppermute | solution.py:650
  154.1 6.4 %collective-permute-start.3 = (bf16[192,256]{1,0:T(8,128)(2,1)}, bf16[192,256]{1,0:T(8,128)(2,1)S(1)}, u32[]{:S(2)}, u32[]{:S(2)}) collective-permute-start(bf16[192,256]{1,0:T(8,128)(2,1)} %get-tuple-element.25), channel_id=1, source_target_pairs={{4,0},{8,4},{12,8},{16,12},{20,16},{24,20},{28,24},{32,28},{36,32}... | collective-permute-start | bytes 294920 | tf_op jit(solution)/shard_map/ppermute | solution.py:650
  161.7 7.9 %copy-start.41 = (f32[768]{0:T(1024)S(1)}, f32[768]{0:T(1024)}, u32[]{:S(2)}) copy-start(f32[768]{0:T(1024)} %param.19) | copy-start | bytes 9220
  165.3 14.9 %copy-start.34 = (bf16[256,256]{1,0:T(8,128)(2,1)S(1)}, bf16[256,256]{1,0:T(8,128)(2,1)}, u32[]{:S(2)}) copy-start(bf16[256,256]{1,0:T(8,128)(2,1)} %constant.38.clone.straight_ref.unit_ref) | copy-start | bytes 393220
  165.3 14.9 %all-to-all-start.2 = ((bf16[4,384,256]{2,1,0:T(8,128)(2,1)}), bf16[4,384,256]{2,1,0:T(8,128)(2,1)S(1)}, u32[]{:S(2)}, u32[]{:S(2)}) async-start(bf16[4,384,256]{2,1,0:T(8,128)(2,1)} %bitcast.8), calls=%async_computation.2 | async-start | bytes 1572864 | tf_op jit(solution)/shard_map/all_to_all | solution.py:644
  196.4 29.4 %copy-start.17 = (bf16[1536,256]{1,0:T(8,128)(2,1)}, bf16[1536,256]{1,0:T(8,128)(2,1)S(1)}, u32[]{:S(2)}) copy-start(bf16[1536,256]{1,0:T(8,128)(2,1)S(1)} %get-tuple-element.27) | copy-start | bytes 2359300
  196.4 25.1 %copy-start.32 = (bf16[256,256]{1,0:T(8,128)(2,1)S(1)}, bf16[256,256]{1,0:T(8,128)(2,1)}, u32[]{:S(2)}) copy-start(bf16[256,256]{1,0:T(8,128)(2,1)} %constant.36.clone.table_ref) | copy-start | bytes 393220
  211.6 8.6 %collective-permute-start.6 = (bf16[192,256]{1,0:T(8,128)(2,1)S(1)}, bf16[192,256]{1,0:T(8,128)(2,1)S(1)}, u32[]{:S(2)}, u32[]{:S(2)}) collective-permute-start(bf16[192,256]{1,0:T(8,128)(2,1)S(1)} %get-tuple-element.35), channel_id=1, source_target_pairs={{4,0},{8,4},{12,8},{16,12},{20,16},{24,20},{28,24},{32,28},{36,32}... | collective-permute-start | bytes 294920 | tf_op jit(solution)/shard_map/ppermute | solution.py:650
  213.5 8.0 %collective-permute-start.5 = (bf16[192,256]{1,0:T(8,128)(2,1)S(1)}, bf16[192,256]{1,0:T(8,128)(2,1)S(1)}, u32[]{:S(2)}, u32[]{:S(2)}) collective-permute-start(bf16[192,256]{1,0:T(8,128)(2,1)S(1)} %get-tuple-element.36), channel_id=1, source_target_pairs={{0,4},{4,8},{8,12},{12,16},{16,20},{20,24},{24,28},{28,32},{32,36}... | collective-permute-start | bytes 294920 | tf_op jit(solution)/shard_map/ppermute | solution.py:650
  225.8 25.7 %copy-start.3 = (f32[2,128,1536]{2,1,0:T(8,128)S(1)}, f32[2,128,1536]{2,1,0:T(8,128)}, u32[]{:S(2)}) copy-start(f32[2,128,1536]{2,1,0:T(8,128)} %copy-done.1) | copy-start | bytes 4718596
  247.3 20.0 %all-to-all-start.4 = ((bf16[4,384,256]{2,1,0:T(8,128)(2,1)}), bf16[4,384,256]{2,1,0:T(8,128)(2,1)}, u32[]{:S(2)}, u32[]{:S(2)}) async-start(bf16[4,384,256]{2,1,0:T(8,128)(2,1)} %bitcast.37), calls=%async_computation.4 | async-start | bytes 1572864 | tf_op jit(solution)/shard_map/all_to_all | solution.py:644
  265.6 36.7 %collective-permute-start.7 = (bf16[4,2,192,256]{3,2,1,0:T(8,128)(2,1)}, bf16[4,2,192,256]{3,2,1,0:T(8,128)(2,1)}, u32[]{:S(2)}, u32[]{:S(2)}) collective-permute-start(bf16[4,2,192,256]{3,2,1,0:T(8,128)(2,1)} %get-tuple-element.33), channel_id=1, source_target_pairs={{0,124},{4,120},{8,116},{12,112},{16,108},{20,104},{24,100},{28,96... | collective-permute-start | bytes 2359304 | tf_op jit(solution)/shard_map/ppermute | solution.py:780
  267.3 31.1 %all-to-all-start.7 = ((bf16[32,8,1536]{2,1,0:T(8,128)(2,1)}), bf16[32,8,1536]{2,1,0:T(8,128)(2,1)S(1)}, u32[]{:S(2)}, u32[]{:S(2)}) async-start(bf16[32,8,1536]{2,1,0:T(8,128)(2,1)} %bitcast.39), calls=%async_computation.7 | async-start | bytes 1572864 | tf_op jit(solution)/shard_map/all_to_all | solution.py:644
  272.5 29.8 %collective-permute-start.8 = (bf16[2,192,256]{2,1,0:T(8,128)(2,1)}, bf16[2,192,256]{2,1,0:T(8,128)(2,1)}, u32[]{:S(2)}, u32[]{:S(2)}) collective-permute-start(bf16[2,192,256]{2,1,0:T(8,128)(2,1)} %copy-done.38), channel_id=1, source_target_pairs={{124,4},{120,8},{116,12},{112,16},{108,20},{104,24},{100,28},{96,3... | collective-permute-start | bytes 589832 | tf_op jit(solution)/shard_map/ppermute | solution.py:781
  (34 other events, 49.9 us)
Sparse Core Ops, SparseCore 0:
  10.3 55.7 all-gather.1

commit v2 on v1

--- a/solution.py
+++ b/solution.py
@@ -23,13 +23,20 @@
 WIDE = SLAB * 128
 POINTS = LEN * LEN
 HALF_UNITS = 384
+UNITS = 3072
+ROWS = ("y", "z", "core")
+SENT = (SLAB + 2) * CH
 F32 = jnp.float32
 BF16 = jnp.bfloat16
 MIB = 1 << 20
 
 
+def wide_at(h):
+    return {-1: LANES, SLAB: LANES + 128}.get(h, 128 * h)
+
+
 def narrow_at(h):
-    return WIDE + 64 * (2 * (h % 4) + h // 4)
+    return {-1: LANES + 256, SLAB: LANES + 320}.get(h, WIDE + 64 * (2 * (h % 4) + h // 4))
 
 
 def columns_of(device):
@@ -110,19 +117,25 @@
     return lax.dot_general(a, b, (((0,), (0,)), ((), ())), preferred_element_type=F32)
 
 
-def kernel_call(body, name, outs, scratch, operands, vmem, flops=0, smem=0):
-    whole = pl.BlockSpec(memory_space=pltpu.VMEM)
+def whole_block(dims):
+    return pl.BlockSpec(dims, lambda *_: (0,) * len(dims), pipeline_mode=pl.Buffered(1))
+
+
+def kernel_call(body, name, outs, scratch, operands, vmem, flops=0, smem=0, hint=0):
     scalar = pl.BlockSpec(memory_space=pltpu.SMEM)
     moved = sum(a.size * a.dtype.itemsize for a in operands)
     moved += sum(o.size * np.dtype(o.dtype).itemsize for o in outs)
     return pl.pallas_call(
         body,
         name=name,
+        grid=(1,),
         out_shape=tuple(outs),
-        in_specs=[scalar] * smem + [whole] * (len(operands) - smem),
-        out_specs=tuple(whole for _ in outs),
+        in_specs=[scalar] * smem + [whole_block(a.shape) for a in operands[smem:]],
+        out_specs=tuple(whole_block(o.shape) for o in outs),
         scratch_shapes=scratch,
-        cost_estimate=pl.CostEstimate(flops=flops, bytes_accessed=moved, transcendentals=0),
+        cost_estimate=pl.CostEstimate(
+            flops=flops + hint * 10**9, bytes_accessed=moved, transcendentals=0
+        ),
         compiler_params=pltpu.CompilerParams(vmem_limit_bytes=vmem * MIB),
     )(*operands)
 
@@ -165,20 +178,28 @@
 
 
 def send_columns(table_ref, lanes_ref, message_ref):
-    for at in range(0, LANES, 512):
-        message_ref[:, at : at + 512] = nt(table_ref[...], lanes_ref[at : at + 512]).astype(BF16)
-
-
-def unfold_kernel(source_ref, kept_ref, wide_ref):
+    for at in range(0, lanes_ref.shape[0], 384):
+        message_ref[:, at : at + 384] = nt(table_ref[...], lanes_ref[at : at + 384]).astype(BF16)
+
+
+def unfold_kernel(channel_ref, source_ref, kept_ref, *refs):
+    *turned_refs, wide_ref = refs
     for h, rows in unfold_rows(source_ref, wide_ref):
         kept_ref[h * CH : (h + 1) * CH] = rows
-
-
-def filter_split_kernel(filter_ref, turned_ref, wide_ref):
+    for turn, turned_ref in enumerate(turned_refs):
+        peer = lax.rem(channel_ref[0] + turn, CH_DEVICES)
+        for half in range(2):
+            rows = every_eighth(wide_ref, peer * 2 + half)
+            turned_ref[half * CH : half * CH + CH] = rows.astype(BF16)
+
+
+def filter_split_kernel(filter_ref, head_ref, tail_ref, lone_ref, wide_ref):
     for part in range(2):
         fill_wide(wide_ref, filter_ref[part])
-        for i in range(SLAB):
-            turned_ref[i, part] = every_eighth(wide_ref, i).astype(BF16)
+        for i in range(4):
+            tail_ref[i, part] = every_eighth(wide_ref, 4 + i).astype(BF16)
+            head_ref[i, part] = every_eighth(wide_ref, i).astype(BF16)
+        lone_ref[part] = head_ref[0, part]
 
 
 def put_spectrum(target_ref, part, column, block):
@@ -191,7 +212,7 @@
 
 
 def filter_kernel(
-    place_ref, own_ref, pair_ref, lone_ref, straight_ref, mirrored_ref, main_ref, cross_ref
+    place_ref, head_ref, tail_ref, pair_ref, lone_ref, straight_ref, mirrored_ref, main_ref, cross_ref
 ):
     device = place_ref[0]
     low, special = device < 16, device == 16
@@ -199,10 +220,10 @@
     for part in range(2):
         sign = 1.0 if part == 0 else -1.0
         for j in range(3):
-            straight = nt(straight_ref[...], own_ref[1 + j, part])
+            straight = nt(straight_ref[...], head_ref[1 + j, part])
             mirrored = nt(mirrored_ref[...], pair_ref[3 - j, part])
             put_spectrum(main_ref, part, j, (straight + sign * mirrored) * scale)
-        own = jnp.where(low, own_ref[4, part], own_ref[0, part])
+        own = jnp.where(low, tail_ref[0, part], head_ref[0, part])
         other = jnp.where(low, pair_ref[0, part], lone_ref[part])
         o, q = nt(straight_ref[...], own), nt(straight_ref[...], other)
         o_back = nt(mirrored_ref[...], own) * sign
@@ -290,14 +311,33 @@
     return re * cos - im * sin, im * cos + re * sin
 
 
+def moved_rows(block, step):
+    empty = jnp.zeros((SLAB, block.shape[1]), block.dtype)
+    if step > 0:
+        return jnp.concatenate([empty, block[:-SLAB]], axis=0)
+    return jnp.concatenate([block[SLAB:], empty], axis=0)
+
+
 def row_body(saves, refs):
     place_ref, received_ref, fwd_ref, inv_ref, cos_ref, sin_ref, main_ref, cross_ref = refs[:8]
     if saves:
         message_ref, seen_ref, mixed_ref, ready_ref = refs[8:]
     else:
         seen_ref, message_ref, product_ref, mixed_ref, ready_ref = refs[8:]
+
+    def joined(at, width, edge, step):
+        rows = received_ref[:, at : at + width].astype(F32)
+        moved = moved_rows(received_ref[:, edge : edge + width].astype(F32), step)
+        return nn(fwd_ref[...], (rows + moved).astype(BF16))
+
     for at in range(0, LANES, 512):
         mixed_ref[:, at : at + 512] = nn(fwd_ref[...], received_ref[:, at : at + 512])
+    if not saves:
+        for h, edge, step in ((0, SLAB, 1), (SLAB - 1, -1, -1)):
+            at = wide_at(h)
+            mixed_ref[:, at : at + 128] = joined(at, 128, wide_at(edge), step)
+            at = narrow_at(h)
+            mixed_ref[:, at : at + 64] = joined(at, 64, narrow_at(edge), step)
 
     def spectrum(group):
         at = pl.multiple_of(group * 16, 16)
@@ -384,6 +424,13 @@
     for at in range(0, LANES, 512):
         block = nn(inv_ref[...], ready_ref[:, at : at + 512])
         message_ref[:, at : at + 512] = block.astype(BF16)
+        if saves:
+            for h, edge, step in ((0, SLAB, -1), (SLAB - 1, -1, 1)):
+                for place, width in ((wide_at, 128), (narrow_at, 64)):
+                    start = place(h) - at
+                    if 0 <= start < 512:
+                        moved = moved_rows(block[:, start : start + width], step)
+                        message_ref[:, place(edge) : place(edge) + width] = moved.astype(BF16)
 
 
 def rows_forward_kernel(*refs):
@@ -404,28 +451,34 @@
         place(m + 4, 128, block[64:])
 
 
-def tokens_kernel(received_ref, table_ref, filtered_ref, first_ref, last_ref):
-    def place(h, channel, block):
-        rows = block.astype(BF16)
-        filtered_ref[h * CH + channel : h * CH + channel + block.shape[0]] = rows
-        if h == 0:
-            first_ref[channel : channel + block.shape[0]] = rows
-        if h == SLAB - 1:
-            last_ref[channel : channel + block.shape[0]] = rows
-
-    token_rows(received_ref, table_ref, place)
-
-
-def convolve(load, taps, put):
+def convolve(load, rows, taps, put):
     lane = lax.broadcasted_iota(jnp.int32, (16, LEN), 1)
-    window = [load(-1), load(0)]
-    for h in range(SLAB):
+    window = [load(rows[0] - 1), load(rows[0])]
+    for h in rows:
         window.append(load(h + 1))
-        sums = [sum(taps[3 * a + b] * window[a] for a in range(3)) for b in range(3)]
+        sums = []
+        for b in range(3):
+            terms = [taps[3 * a + b] * w for a, w in enumerate(window) if w is not None]
+            sums.append(sum(terms[1:], terms[0]))
         left = jnp.where(lane == 0, 0.0, pltpu.roll(sums[0], 1, axis=1))
         right = jnp.where(lane == LEN - 1, 0.0, pltpu.roll(sums[2], LEN - 1, axis=1))
-        put(h, sums[1] + left + right, window[1])
+        put(h, sums[1] + left + right)
         window.pop(0)
+
+
+def every_chunk(body):
+    def wide(index, carry):
+        at = pl.multiple_of(index * 16, 16)
+        body(at, lambda h: pl.ds(pl.multiple_of(wide_at(h) + at, 16), 16))
+        return carry
+
+    def last(index, carry):
+        at = pl.multiple_of(index * 16, 16)
+        body(at + 128, lambda h: pl.ds(pl.multiple_of(narrow_at(h) + at, 16), 16))
+        return carry
+
+    lax.fori_loop(0, 8, wide, 0)
+    lax.fori_loop(0, 4, last, 0)
 
 
 def rows_at(h, start):
@@ -433,55 +486,44 @@
 
 
 def spread_taps(taps_ref, start, order):
-    taps = taps_ref[pl.ds(start, 16), :]
+    taps = taps_ref[pl.ds(pl.multiple_of(start, 16), 16), :]
     return [jnp.broadcast_to(taps[:, k : k + 1], (16, LEN)) for k in order]
 
 
-def hidden_kernel(filtered_ref, above_ref, below_ref, taps_ref, signal_ref, hidden_ref):
-    def chunk(index, carry):
-        start = pl.multiple_of(index * 16, 16)
-
+def hidden_kernel(received_ref, table_ref, taps_ref, signal_ref, hidden_ref, filtered_ref):
+    for at in range(0, SENT, 128):
+        block = tn(received_ref[:, at : at + 128], table_ref[...])
+        filtered_ref[at : at + 128] = block.astype(BF16)
+
+    def chunk(start, place):
         def load(h):
-            if h < 0:
-                return above_ref[pl.ds(start, 16), :].astype(F32)
-            if h == SLAB:
-                return below_ref[pl.ds(start, 16), :].astype(F32)
-            return filtered_ref[rows_at(h, start), :].astype(F32)
-
-        def put(h, convolved, middle):
+            return filtered_ref[place(h), :].astype(F32)
+
+        def put(h, convolved):
             at = rows_at(h, start)
             hidden_ref[at, :] = (signal_ref[at, :].astype(F32) + convolved).astype(BF16)
 
-        convolve(load, spread_taps(taps_ref, start, range(9)), put)
-        return carry
-
-    lax.fori_loop(0, CH // 16, chunk, 0)
-
-
-def gradient_columns_kernel(
-    upstream_ref, mlp_ref, above_ref, below_ref, taps_ref, table_ref, message_ref, natural_ref, lanes_ref
-):
-    def chunk(index, carry):
-        start = pl.multiple_of(index * 16, 16)
-
+        convolve(load, range(SLAB), spread_taps(taps_ref, start, range(9)), put)
+
+    every_chunk(chunk)
+
+
+def gradient_columns_kernel(upstream_ref, mlp_ref, taps_ref, table_ref, message_ref, lanes_ref):
+    def chunk(start, place):
         def load(h):
-            if h < 0:
-                return above_ref[pl.ds(start, 16), :].astype(F32)
-            if h == SLAB:
-                return below_ref[pl.ds(start, 16), :].astype(F32)
+            if h < 0 or h >= SLAB:
+                return None
             at = rows_at(h, start)
             return upstream_ref[at, :].astype(F32) + mlp_ref[at, :].astype(F32)
 
-        def put(h, convolved, middle):
-            natural_ref[rows_at(h, start), :] = convolved.astype(BF16)
-
-        convolve(load, spread_taps(taps_ref, start, range(8, -1, -1)), put)
-        return carry
-
-    lax.fori_loop(0, CH // 16, chunk, 0)
-    for h in range(SLAB):
-        lanes_ref[h * 128 : h * 128 + 128] = natural_ref[h * CH : h * CH + 128]
-        lanes_ref[narrow_at(h) : narrow_at(h) + 64] = natural_ref[h * CH + 128 : (h + 1) * CH]
+        def put(h, convolved):
+            lanes_ref[place(h), :] = convolved.astype(BF16)
+
+        convolve(
+            load, range(-1, SLAB + 1), spread_taps(taps_ref, start, range(8, -1, -1)), put
+        )
+
+    every_chunk(chunk)
     send_columns(table_ref, lanes_ref, message_ref)
 
 
@@ -492,14 +534,22 @@
 
 
 def mlp_kernel(
+    channel_ref,
     hidden_ref,
-    upstream_ref,
+    own_dy_ref,
+    dy_one_ref,
+    dy_two_ref,
+    dy_three_ref,
     gain_ref,
     unit_ref,
     mine_ref,
     other_ref,
-    out_ref,
+    out_own_ref,
+    out_one_ref,
+    out_two_ref,
+    out_three_ref,
     grad_ref,
+    parts_ref,
     gathered_ref,
     scaled_ref,
     dy_ref,
@@ -509,18 +559,26 @@
     grad_sum_ref,
 ):
     step = pl.program_id(0)
-
-    def turn_in(source_ref, half):
+    channel = channel_ref[0]
+
+    def turn_in(half):
         for src in range(CH_DEVICES):
             at = src * 2 * CH + half * CH
-            gathered_ref[src * CH : (src + 1) * CH] = source_ref[at : at + CH]
+            gathered_ref[src * CH : (src + 1) * CH] = hidden_ref[at : at + CH]
+        return nt(unit_ref[...], gathered_ref[...])
+
+    def turn_in_dy(half):
+        for src in range(CH_DEVICES):
+            gathered_ref[src * CH : (src + 1) * CH] = parts_ref[src, half * CH : half * CH + CH]
         return nt(unit_ref[...], gathered_ref[...])
 
     @pl.when(step == 0)
     def _():
+        for turn, source_ref in enumerate((own_dy_ref, dy_one_ref, dy_two_ref, dy_three_ref)):
+            parts_ref[lax.rem(channel + CH_DEVICES - turn, CH_DEVICES)] = source_ref[...]
         for half in range(2):
             rows = slice(half * LEN, half * LEN + LEN)
-            values = turn_in(hidden_ref, half)
+            values = turn_in(half)
             centred = values - jnp.mean(values, axis=1, keepdims=True)
             variance = jnp.mean(centred * centred, axis=1, keepdims=True)
             inv_std = lax.rsqrt(variance + norm_epsilon)
@@ -528,7 +586,7 @@
             normed_ref[rows] = normed
             inv_ref[rows] = jnp.broadcast_to(inv_std, (LEN, 128))
             scaled_ref[rows] = (normed * gain_ref[...]).astype(BF16)
-            dy_ref[rows] = turn_in(upstream_ref, half).astype(BF16)
+            dy_ref[rows] = turn_in_dy(half).astype(BF16)
         out_sum_ref[...] = jnp.zeros_like(out_sum_ref)
         grad_sum_ref[...] = jnp.zeros_like(grad_sum_ref)
 
@@ -540,13 +598,19 @@
         out_sum_ref[...] += nn(activated.astype(BF16), down)
         grad_sum_ref[...] += nn((grad_act * slope).astype(BF16), up)
 
-    def turn_out(values, half, target_ref):
+    def turn_out(values, half, put):
         for block in range(3):
             piece = nt(unit_ref[...], values[:, block * LEN : (block + 1) * LEN])
             gathered_ref[block * LEN : (block + 1) * LEN] = piece.astype(BF16)
         for dst in range(CH_DEVICES):
-            at = (dst * 2 + half) * CH
-            target_ref[at : at + CH] = gathered_ref[dst * CH : (dst + 1) * CH]
+            put(dst, half, gathered_ref[dst * CH : (dst + 1) * CH])
+
+    def put_grad(dst, half, rows):
+        at = (dst * 2 + half) * CH
+        grad_ref[at : at + CH] = rows
+
+    def put_out(dst, half, rows):
+        parts_ref[dst, half * CH : half * CH + CH] = rows
 
     @pl.when(step == pl.num_programs(0) - 1)
     def _():
@@ -557,22 +621,35 @@
             first = jnp.mean(weighted, axis=1, keepdims=True)
             second = jnp.mean(weighted * normed, axis=1, keepdims=True)
             term = inv_ref[rows, 0:1] * (weighted - first - normed * second)
-            turn_out(term.astype(BF16), half, grad_ref)
-            turn_out(out_sum_ref[rows].astype(BF16), half, out_ref)
-
-
-def mlp(hidden, upstream, gain, mine, other, block=256):
-    tokens, units = 2 * LEN, CH_DEVICES * HALF_UNITS
-    whole = pl.BlockSpec(memory_space=pltpu.VMEM)
-    weights = pl.BlockSpec((block, 2 * ALL_CH), lambda i: (i, 0))
+            turn_out(term.astype(BF16), half, put_grad)
+            turn_out(out_sum_ref[rows].astype(BF16), half, put_out)
+        for turn, out_ref in enumerate((out_own_ref, out_one_ref, out_two_ref, out_three_ref)):
+            out_ref[...] = parts_ref[lax.rem(channel + turn, CH_DEVICES)]
+
+
+def mlp(channel, hidden, dy_parts, gain, weights, block=256):
+    tokens, steps = 2 * LEN, UNITS // 2 // block
+    part = whole_block((2 * CH, LEN))
     return pl.pallas_call(
         mlp_kernel,
         name="mlp",
-        grid=(units // block,),
-        out_shape=(shape((LANES, LEN), BF16),) * 2,
-        in_specs=[whole] * 4 + [weights] * 2,
-        out_specs=(whole,) * 2,
+        grid=(steps,),
+        out_shape=(*(shape((2 * CH, LEN), BF16),) * CH_DEVICES, shape((LANES, LEN), BF16)),
+        in_specs=[
+            pl.BlockSpec(memory_space=pltpu.SMEM),
+            whole_block((LANES, LEN)),
+            part,
+            part,
+            part,
+            part,
+            whole_block((1, ALL_CH)),
+            whole_block((LEN, LEN)),
+            pl.BlockSpec((block, 2 * ALL_CH), lambda i: (i, 0)),
+            pl.BlockSpec((block, 2 * ALL_CH), lambda i: (i + steps, 0)),
+        ],
+        out_specs=(part, part, part, part, whole_block((LANES, LEN))),
         scratch_shapes=[
+            pltpu.VMEM((CH_DEVICES, 2 * CH, LEN), BF16),
             pltpu.VMEM((ALL_CH, LEN), BF16),
             pltpu.VMEM((tokens, ALL_CH), BF16),
             pltpu.VMEM((tokens, ALL_CH), BF16),
@@ -582,19 +659,22 @@
             pltpu.VMEM((tokens, ALL_CH), F32),
         ],
         cost_estimate=pl.CostEstimate(
-            flops=16 * tokens * units * ALL_CH,
-            bytes_accessed=8 * units * ALL_CH + 8 * LANES * LEN,
-            transcendentals=2 * tokens * units,
+            flops=8 * tokens * UNITS * ALL_CH,
+            bytes_accessed=4 * UNITS * ALL_CH + 8 * LANES * LEN,
+            transcendentals=2 * tokens * UNITS,
         ),
-        compiler_params=pltpu.CompilerParams(vmem_limit_bytes=48 * MIB),
-    )(hidden, upstream, gain, jnp.asarray(UNIT), mine, other)
-
-
-def block_out_kernel(hidden_ref, sum_ref, out_ref, wide_ref):
-    for h in range(SLAB):
-        rows = slice(h * CH, (h + 1) * CH)
-        total = hidden_ref[rows].astype(F32) + sum_ref[rows].astype(F32)
-        put_eighth(wide_ref, h, total)
+        compiler_params=pltpu.CompilerParams(vmem_limit_bytes=28 * MIB),
+    )(channel, hidden, *dy_parts, gain, jnp.asarray(UNIT), weights, weights)
+
+
+def block_out_kernel(channel_ref, hidden_ref, own_ref, one_ref, two_ref, three_ref, out_ref, wide_ref):
+    for turn, sum_ref in enumerate((own_ref, one_ref, two_ref, three_ref)):
+        src = lax.rem(channel_ref[0] + CH_DEVICES - turn, CH_DEVICES)
+        for half in range(2):
+            rows = pl.ds(pl.multiple_of((src * 2 + half) * CH, 64), CH)
+            total = hidden_ref[rows, :].astype(F32)
+            total += sum_ref[half * CH : half * CH + CH].astype(F32)
+            put_eighth(wide_ref, src * 2 + half, total)
     out_ref[...] = take_wide(wide_ref).astype(BF16)
 
 
@@ -644,118 +724,123 @@
     return lax.all_to_all(values, axis, split_axis=0, concat_axis=0, tiled=True)
 
 
-def halo(first, last):
-    down = [(i, i + 1) for i in range(ROWS_DEVICES - 1)]
-    up = [(i + 1, i) for i in range(ROWS_DEVICES - 1)]
-    return lax.ppermute(last, "rows", down), lax.ppermute(first, "rows", up)
+def turned_exchange(parts):
+    received = [parts[0]]
+    for turn in range(1, CH_DEVICES):
+        pairs = [(i, (i + turn) % CH_DEVICES) for i in range(CH_DEVICES)]
+        received.append(lax.ppermute(parts[turn], "ch", pairs))
+    return received
+
+
+def after(value, earlier):
+    return lax.optimization_barrier((value, earlier))
 
 
 def on_device(tile_image, spectral_filter, conv_taps, norm_gain, up_weight, down_weight, upstream):
-    device = lax.axis_index("rows")
+    device = lax.axis_index(ROWS)
     place = device.reshape(1).astype(jnp.int32)
+    channel = lax.axis_index("ch").reshape(1).astype(jnp.int32)
     flat = (LANES, LEN)
     tables = [jnp.asarray(t) for t in (FORWARD_ROWS, INVERSE_ROWS, TWIDDLE_COS, TWIDDLE_SIN)]
     forward_columns, inverse_columns = jnp.asarray(FORWARD_COLUMNS), jnp.asarray(INVERSE_COLUMNS)
     straight, mirrored = jnp.asarray(STRAIGHT), jnp.asarray(MIRRORED)
 
-    start = lax.rem(device, 2) * HALF_UNITS
-    own_up = lax.dynamic_slice_in_dim(up_weight, start, HALF_UNITS, axis=1).T
-    own_down = lax.dynamic_slice_in_dim(down_weight, start, HALF_UNITS, axis=0)
-    mine = lax.all_gather(jnp.concatenate([own_up, own_down], axis=1), "ch", axis=0, tiled=True)
-    other = lax.ppermute(mine, "rows", [(i, i ^ 1) for i in range(ROWS_DEVICES)])
-
     wide = pltpu.VMEM((2, LANES, 128), F32)
-    lanes = pltpu.VMEM(flat, BF16)
+    head, tail, lone = kernel_call(
+        filter_split_kernel,
+        "filter_split",
+        [shape((4, 2, CH, LEN), BF16), shape((4, 2, CH, LEN), BF16), shape((2, CH, LEN), BF16)],
+        [wide],
+        [spectral_filter.reshape(2, LANES, LEN)],
+        16,
+    )
+    opposite = [(i, ROWS_DEVICES - 1 - i) for i in range(ROWS_DEVICES)]
+    lone_in = [(i, ROWS_DEVICES - i) for i in range(1, 16)] + [(0, 16)]
+    pair_filter = lax.ppermute(tail, ROWS, opposite)
+    lone_filter = lax.ppermute(lone, ROWS, lone_in)
     message, signal = kernel_call(
         columns_kernel,
         "columns",
         [shape((LEN, LANES), BF16), shape(flat, BF16)],
-        [wide, lanes],
+        [wide, pltpu.VMEM(flat, BF16)],
         [tile_image.reshape(flat), forward_columns],
-        24,
+        16,
         2 * LEN * LEN * LANES,
     )
-    received = to_peers(message, "rows")
-    (dy,) = kernel_call(
-        unfold_kernel, "unfold", [shape(flat, BF16)], [wide], [upstream.reshape(flat)], 16
-    )
-    (own_filter,) = kernel_call(
-        filter_split_kernel,
-        "filter_split",
-        [shape((SLAB, 2, CH, LEN), BF16)],
+    received = to_peers(message, ROWS)
+
+    (up_own, down_own, upstream_rows), _ = after(
+        (up_weight, down_weight, upstream.reshape(flat)), message
+    )
+    start = lax.axis_index("core") * HALF_UNITS
+    own_up = lax.dynamic_slice_in_dim(up_own, start, HALF_UNITS, axis=1).T
+    own_down = lax.dynamic_slice_in_dim(down_own, start, HALF_UNITS, axis=0)
+    pack = jnp.concatenate([own_up, own_down], axis=1)
+    weights = lax.all_gather(pack, ("core", "ch"), axis=0, tiled=True)
+    dy, *dy_turned = kernel_call(
+        unfold_kernel,
+        "unfold",
+        [shape(flat, BF16)] + [shape((2 * CH, LEN), BF16)] * CH_DEVICES,
         [wide],
-        [spectral_filter.reshape(2, LANES, LEN)],
-        24,
-    )
-    opposite = [(i, ROWS_DEVICES - 1 - i) for i in range(ROWS_DEVICES)]
-    lone_in = [(i, ROWS_DEVICES - i) for i in range(1, 16)] + [(0, 16)]
-    pair_filter = lax.ppermute(own_filter[4:], "rows", opposite)
-    lone_filter = lax.ppermute(own_filter[0], "rows", lone_in)
+        [channel, upstream_rows],
+        16,
+        smem=1,
+        hint=6,
+    )
+    dy_parts = turned_exchange(dy_turned)
     main, cross = kernel_call(
         filter_kernel,
         "filter",
         [shape((2, 128, LANES), F32), shape((2, 32, LANES), F32)],
         [],
-        [place, own_filter, pair_filter, lone_filter, straight, mirrored],
-        32,
+        [place, head, tail, pair_filter, lone_filter, straight, mirrored],
+        16,
         2 * 14 * LEN * LEN * CH,
         smem=1,
-    )
-    dy_tokens = to_peers(dy, "ch")
+        hint=6,
+    )
+    received, dy_parts = after(received, dy_parts)
 
     row_scratch = [pltpu.VMEM((320, LANES), F32), pltpu.VMEM((LEN, LANES), BF16)]
     message, seen = kernel_call(
         rows_forward_kernel,
         "rows_forward",
-        [shape((LEN, LANES), BF16), shape((2, 160, LANES), BF16)],
+        [shape((LEN, SENT), BF16), shape((2, 160, LANES), BF16)],
         row_scratch,
         [place, received, *tables, main, cross],
-        24,
+        20,
         2 * 576 * LEN * LANES,
         smem=1,
     )
-    received = to_peers(message, "rows")
-    filtered, first, last = kernel_call(
-        tokens_kernel,
-        "tokens",
-        [shape(flat, BF16), shape((CH, LEN), BF16), shape((CH, LEN), BF16)],
-        [],
-        [received, inverse_columns],
-        24,
-        2 * LEN * LEN * LANES,
-    )
-    above, below = halo(first, last)
+    received = to_peers(message, ROWS)
     (hidden,) = kernel_call(
         hidden_kernel,
         "hidden",
         [shape(flat, BF16)],
-        [],
-        [filtered, above, below, conv_taps, signal],
-        24,
+        [pltpu.VMEM((SENT, LEN), BF16)],
+        [received, inverse_columns, conv_taps, signal],
+        16,
+        2 * LEN * LEN * SENT,
     )
     hidden_tokens = to_peers(hidden, "ch")
-    out_message, grad_message = mlp(
-        hidden_tokens, dy_tokens, norm_gain.reshape(1, ALL_CH), mine, other
+    *out_turned, grad_message = mlp(
+        channel, hidden_tokens, dy_parts, norm_gain.reshape(1, ALL_CH), weights
     )
     grad_mlp = to_peers(grad_message, "ch")
-    edges = [
-        (dy[at].astype(F32) + grad_mlp[at].astype(F32)).astype(BF16)
-        for at in (slice(0, CH), slice(LANES - CH, LANES))
-    ]
-    above, below = halo(*edges)
     (message,) = kernel_call(
         gradient_columns_kernel,
         "gradient_columns",
-        [shape((LEN, LANES), BF16)],
-        [lanes, lanes],
-        [dy, grad_mlp, above, below, conv_taps, forward_columns],
-        24,
-        2 * LEN * LEN * LANES,
-    )
-    received = to_peers(message, "rows")
-    out_sum = to_peers(out_message, "ch")
+        [shape((LEN, SENT), BF16)],
+        [pltpu.VMEM((SENT, LEN), BF16)],
+        [dy, grad_mlp, conv_taps, forward_columns],
+        16,
+        2 * LEN * LEN * SENT,
+    )
+    out_turned, message = after(out_turned, message)
+    received = to_peers(message, ROWS)
+    out_parts = turned_exchange(out_turned)
     (block_out,) = kernel_call(
-        block_out_kernel, "block_out", [shape(flat, BF16)], [wide], [hidden, out_sum], 24
+        block_out_kernel, "block_out", [shape(flat, BF16)], [wide], [channel, hidden, *out_parts], 16, smem=1
     )
     message, products = kernel_call(
         rows_backward_kernel,
@@ -763,29 +848,30 @@
         [shape((LEN, LANES), BF16), shape((2, 160, LANES), BF16)],
         row_scratch,
         [place, received, *tables, main, cross, seen],
-        24,
+        20,
         2 * 576 * LEN * LANES,
         smem=1,
     )
-    received = to_peers(message, "rows")
+    received = to_peers(message, ROWS)
     own, pair, lone = kernel_call(
         unturn_kernel,
         "unturn",
         [shape((4, 2, CH, LEN), BF16), shape((4, 2, CH, LEN), BF16), shape((2, CH, LEN), BF16)],
         [pltpu.VMEM((LEN, CH), BF16)],
         [products, straight, mirrored],
-        24,
+        16,
         2 * 18 * LEN * LEN * CH,
-    )
-    pair = lax.ppermute(pair, "rows", opposite)
-    lone = lax.ppermute(lone, "rows", [(b, a) for a, b in lone_in])
+        hint=12,
+    )
+    pair = lax.ppermute(pair, ROWS, opposite)
+    lone = lax.ppermute(lone, ROWS, [(b, a) for a, b in lone_in])
     (grad_filter,) = kernel_call(
         grad_filter_kernel,
         "grad_filter",
         [shape((2, LANES, LEN), F32)],
         [wide],
         [place, own, pair, lone],
-        24,
+        16,
         smem=1,
     )
     (grad_image,) = kernel_call(
@@ -794,7 +880,7 @@
         [shape(flat, F32)],
         [wide],
         [received, inverse_columns, dy, grad_mlp],
-        24,
+        16,
         2 * LEN * LEN * LANES,
     )
     slab = (CH, SLAB, LEN)
@@ -806,18 +892,13 @@
 
 
 def solution(mesh):
+    devices = mesh.devices.reshape(4, 4, 2, CH_DEVICES)
+    token = P("ch", ROWS, None)
+    frequency = P(None, "ch", ROWS, None)
     return jax.shard_map(
         on_device,
-        mesh=mesh,
-        in_specs=(
-            P("ch", "rows", None),
-            P(None, "ch", "rows", None),
-            P("ch", None),
-            P(),
-            P(None, "ch"),
-            P("ch", None),
-            P("ch", "rows", None),
-        ),
-        out_specs=(P("ch", "rows", None), P("ch", "rows", None), P(None, "ch", "rows", None)),
+        mesh=jax.sharding.Mesh(devices, (*ROWS, "ch")),
+        in_specs=(token, frequency, P("ch", None), P(), P(None, "ch"), P("ch", None), token),
+        out_specs=(token, token, frequency),
         check_vma=False,
     )

time: 315 us -> 236 us (0.75)
  waiting for transfers between devices: 124 us -> 58.4 us
  starting transfers between devices: 58.5 us -> 45.4 us
    all_gather x1, waiting for transfers between devices: 56.1 us -> 0.01 us  [on_device(): weights = lax.all_gather(pack, ('core', 'ch'), axis=0, tiled=True)]
    all_to_all x6 -> x4, starting transfers between devices: 30.6 us -> 20.3 us  [to_peers(): return lax.all_to_all(values, axis, split_axis=0, concat_axis=0, tiled=True)]
    all_to_all x6 -> x4, waiting for transfers between devices: 45.3 us -> 38.2 us  [to_peers(): return lax.all_to_all(values, axis, split_axis=0, concat_axis=0, tiled=True)]
    ppermute x9 -> x10, starting transfers between devices: 27.8 us -> 25.1 us  [the longest x6 7.66 us: turned_exchange(): received.append(lax.ppermute(parts[turn], 'ch', pairs))]
    ppermute x9 -> x10, waiting for transfers between devices: 22.9 us -> 20.2 us  [the longest x6 17.9 us: turned_exchange(): received.append(lax.ppermute(parts[turn], 'ch', pairs))]
    unnamed x86 -> x111, local copies, waits for them, and re-layouts: 29.3 us -> 30.1 us
    pallas_call x14 -> x13, Pallas kernels: 47.7 us -> 47.8 us  [the longest x12 32 us: kernel_call(): pl.pallas_call(body, name=name, grid=(1,), out_shape=tuple(outs), in_spec...]
  transfers between devices with their start and end apart: 16 -> 15, of which waited for: 8 -> 10; matrix products, arithmetic and copies ran while one was open for 0% -> 0% of each run, Pallas kernels for 7% -> 7%
where the time goes in v2:
time: 236 us; the launch traced here: 234 us
  waiting for transfers between devices  58.4 us (25%)
  Pallas kernels  47.8 us (20%)
  starting transfers between devices  45.4 us (19%)
  blocking collectives  35.5 us (15%)
  local copies, waits for them, and re-layouts  31.8 us (13%)
  between operations  14.4 us (6%)
    all_to_all x4, waiting for transfers between devices, to_peers(): return lax.all_to_all(values, axis, split_axis=0, concat_axis=0, tiled=True)  38.2 us
    all_to_all x2, blocking collectives, to_peers(): return lax.all_to_all(values, axis, split_axis=0, concat_axis=0, tiled=True)  35.5 us
    pallas_call x12, Pallas kernels, kernel_call(): pl.pallas_call(body, name=name, grid=(1,), out_shape=tuple(outs), in_spec...  32 us
    unnamed x111, local copies, waits for them, and re-layouts  30.1 us
    all_to_all x4, starting transfers between devices, to_peers(): return lax.all_to_all(values, axis, split_axis=0, concat_axis=0, tiled=True)  20.3 us
    ppermute x6, waiting for transfers between devices, turned_exchange(): received.append(lax.ppermute(parts[turn], 'ch', pairs))  17.9 us
    pallas_call x1, Pallas kernels, mlp(): pl.pallas_call(mlp_kernel, name='mlp', grid=(steps,), out_shape=(*(shape(...  15.8 us
    ppermute x6, starting transfers between devices, turned_exchange(): received.append(lax.ppermute(parts[turn], 'ch', pairs))  7.66 us
  transfers between devices with their start and end apart: 15, of which 10 were waited for; matrix products, arithmetic and copies ran while one was open for 0% of the time, Pallas kernels for 7%

profile of v2, /device:TPU:1, one launch (start us, length us, event | category | flops | bytes accessed | tf_op | source)
XLA Modules:
  0.0 234.3 jit_solution(17420712208921435219)
XLA Ops:
  18.8 7.6 %collective-permute-start.3 = (bf16[4,2,192,256]{3,2,1,0:T(8,128)(2,1)S(1)}, bf16[4,2,192,256]{3,2,1,0:T(8,128)(2,1)}, u32[]{:S(2)}, u32[]{:S(2)}) collective-permute-start(bf16[4,2,192,256]{3,2,1,0:T(8,128)(2,1)S(1)} %get-tuple-element.48.tail_ref), channel_id=1, source_target_pairs={{0,124},{4,120},{8,116},{12,112},{16,108},{20,104},{24,100},{28,96... | collective-permute-start | bytes 2359304 | tf_op jit(solution)/shard_map/ppermute | solution.py:759
  26.4 3.7 %all-to-all-start = ((bf16[32,8,1536]{2,1,0:T(8,128)(2,1)}), bf16[32,8,1536]{2,1,0:T(8,128)(2,1)S(1)}, u32[]{:S(2)}, u32[]{:S(2)}) async-start(bf16[32,8,1536]{2,1,0:T(8,128)(2,1)} %bitcast.3), calls=%async_computation | async-start | bytes 1572864 | tf_op jit(solution)/shard_map/all_to_all | solution.py:724
  34.4 2.5 %collective-permute-start.1 = (bf16[384,256]{1,0:T(8,128)(2,1)}, bf16[384,256]{1,0:T(8,128)(2,1)S(1)}, u32[]{:S(2)}, u32[]{:S(2)}) collective-permute-start(bf16[384,256]{1,0:T(8,128)(2,1)} %get-tuple-element.44), channel_id=1, source_target_pairs={{0,2},{1,3},{2,0},{3,1},{4,6},{5,7},{6,4},{7,5},{8,10},{9,11},{10,... | collective-permute-start | bytes 589832 | tf_op jit(solution)/shard_map/ppermute | solution.py:731
  38.1 6.5 %collective-permute-start.4 = (bf16[2,192,256]{2,1,0:T(8,128)(2,1)}, bf16[2,192,256]{2,1,0:T(8,128)(2,1)S(1)}, u32[]{:S(2)}, u32[]{:S(2)}) collective-permute-start(bf16[2,192,256]{2,1,0:T(8,128)(2,1)} %get-tuple-element.49), channel_id=1, source_target_pairs={{4,124},{8,120},{12,116},{16,112},{20,108},{24,104},{28,100},{32,9... | collective-permute-start | bytes 589832 | tf_op jit(solution)/shard_map/ppermute | solution.py:760
  46.4 8.7 %collective-permute-done.1.dy_two_ref = bf16[384,256]{1,0:T(8,128)(2,1)S(1)} collective-permute-done((bf16[384,256]{1,0:T(8,128)(2,1)}, bf16[384,256]{1,0:T(8,128)(2,1)S(1)}, u32[]{:S(2)}, u32[]{:S(2)}) %collective-permute-start.1) | collective-permute-done | bytes 196640 | tf_op jit(solution)/shard_map/ppermute | solution.py:731
  66.0 2.7 %rows_forward.1 = (bf16[256,1920]{1,0:T(8,128)(2,1)S(1)}, bf16[2,160,1536]{2,1,0:T(8,128)(2,1)S(1)}) custom-call(s32[1]{0:T(128)} %bitcast.1.place_ref.refs_0_, bf16[256,1536]{1,0:T(8,128)(2,1)S(1)} %bitcast.27, bf16[320,256]{1,0:T(8,128)(2,1)S(1)} %copy-done.22, bf16[256,256]{1,0:T(8,128)(2,1)S(1)} %copy-done.26, f32[32,1536]{1,0:T(8,128)S(1)} %copy-done.14, ...), custom_call_target="tpu_custom_call" | custom-call | flops 452984832 | bytes 5406724 | tf_op jit(solution)/shard_map/rows_forward/pallas_call | solution.py:128
  70.6 7.6 %all-to-all-start.1 = ((bf16[32,8,1920]{2,1,0:T(8,128)(2,1)}), bf16[32,8,1920]{2,1,0:T(8,128)(2,1)}, u32[]{:S(2)}, u32[]{:S(2)}) async-start(bf16[32,8,1920]{2,1,0:T(8,128)(2,1)} %bitcast.29), calls=%async_computation.1 | async-start | bytes 1966080 | tf_op jit(solution)/shard_map/all_to_all | solution.py:724
  78.3 16.1 %all-to-all-done.1 = bf16[32,8,1920]{2,1,0:T(8,128)(2,1)} async-done(((bf16[32,8,1920]{2,1,0:T(8,128)(2,1)}), bf16[32,8,1920]{2,1,0:T(8,128)(2,1)}, u32[]{:S(2)}, u32[]{:S(2)}) %all-to-all-start.1) | async-done | bytes 983072 | tf_op jit(solution)/shard_map/all_to_all | solution.py:724
  95.6 5.3 %hidden.1.hidden_ref = bf16[1536,256]{1,0:T(8,128)(2,1)} custom-call(bf16[256,1920]{1,0:T(8,128)(2,1)} %bitcast.8.received_ref, bf16[256,256]{1,0:T(8,128)(2,1)S(1)} %copy-done.24, f32[192,9]{1,0:T(8,128)S(1)} %copy.19.taps_ref, bf16[1536,256]{1,0:T(8,128)(2,1)S(1)} %copy-done.21), custom_call_target="tpu_custom_call" | custom-call | flops 251658240 | bytes 2693888 | tf_op jit(solution)/shard_map/hidden/pallas_call | solution.py:128
  100.9 4.0 %all-to-all-start.2 = ((bf16[4,384,256]{2,1,0:T(8,128)(2,1)}), bf16[4,384,256]{2,1,0:T(8,128)(2,1)S(1)}, u32[]{:S(2)}, u32[]{:S(2)}) async-start(bf16[4,384,256]{2,1,0:T(8,128)(2,1)} %bitcast.9), calls=%async_computation.2 | async-start | bytes 1572864 | tf_op jit(solution)/shard_map/all_to_all | solution.py:724
  104.8 12.0 %all-to-all-done.2 = bf16[4,384,256]{2,1,0:T(8,128)(2,1)S(1)} async-done(((bf16[4,384,256]{2,1,0:T(8,128)(2,1)}), bf16[4,384,256]{2,1,0:T(8,128)(2,1)S(1)}, u32[]{:S(2)}, u32[]{:S(2)}) %all-to-all-start.2) | async-done | bytes 786464 | tf_op jit(solution)/shard_map/all_to_all | solution.py:724
  116.8 3.7 %copy-done.32 = bf16[3072,1536]{1,0:T(8,128)(2,1)S(1)} copy-done((bf16[3072,1536]{1,0:T(8,128)(2,1)S(1)}, bf16[3072,1536]{1,0:T(8,128)(2,1)}, u32[]{:S(2)}) %copy-start.32) | copy-done | bytes 9437208
  125.1 15.8 %mlp.1 = (bf16[384,256]{1,0:T(8,128)(2,1)S(1)}, bf16[384,256]{1,0:T(8,128)(2,1)}, bf16[384,256]{1,0:T(8,128)(2,1)}, bf16[384,256]{1,0:T(8,128)(2,1)}, bf16[1536,256]{1,0:T(8,128)(2,1)S(1)}) custom-call(s32[1]{0:T(128)} %bitcast.channel_ref, bf16[1536,256]{1,0:T(8,128)(2,1)S(1)} %bitcast.32, bf16[384,256]{1,0:T(8,128)(2,1)S(1)} %copy-done.52, ...), custom_call_target="tpu_custom_call" | custom-call | flops 9663676416 | bytes 12582912 | tf_op jit(solution)/shard_map/mlp/pallas_call | solution.py:633
  140.9 13.3 %all_to_all.67 = bf16[4,384,256]{2,1,0:T(8,128)(2,1)S(1)} all-to-all(bf16[4,384,256]{2,1,0:T(8,128)(2,1)S(1)} %bitcast.33), channel_id=1, replica_groups=mesh['y'=4,'z'=4,'core'=2,'ch'=4] {'ch'}, dimensions={0} | all-to-all | bytes 1572864 | tf_op jit(solution)/shard_map/all_to_all | solution.py:724
  154.3 3.4 %gradient_columns.1 = bf16[256,1920]{1,0:T(8,128)(2,1)S(1)} custom-call(bf16[1536,256]{1,0:T(8,128)(2,1)S(1)} %copy-done.3, bf16[1536,256]{1,0:T(8,128)(2,1)S(1)} %bitcast.22, f32[192,9]{1,0:T(8,128)S(1)} %copy-done.11, bf16[256,256]{1,0:T(8,128)(2,1)S(1)} %copy-done.29), custom_call_target="tpu_custom_call" | custom-call | flops 251658240 | bytes 2693888 | tf_op jit(solution)/shard_map/gradient_columns/pallas_call | solution.py:128
  157.8 22.2 %all_to_all.68 = bf16[32,8,1920]{2,1,0:T(8,128)(2,1)S(1)} all-to-all(bf16[32,8,1920]{2,1,0:T(8,128)(2,1)S(1)} %bitcast.25), channel_id=1, replica_groups=mesh['y'=4,'z'=4,'core'=2,'ch'=4] {'y','z','core'}, dimensions={0} | all-to-all | bytes 1966080 | tf_op jit(solution)/shard_map/all_to_all | solution.py:724
  180.0 3.3 %rows_backward.1 = (bf16[256,1536]{1,0:T(8,128)(2,1)S(1)}, bf16[2,160,1536]{2,1,0:T(8,128)(2,1)S(1)}) custom-call(s32[1]{0:T(128)} %bitcast.1.place_ref.refs_0_, bf16[256,1920]{1,0:T(8,128)(2,1)S(1)} %bitcast.24, bf16[320,256]{1,0:T(8,128)(2,1)S(1)} %copy-done.23, bf16[256,256]{1,0:T(8,128)(2,1)S(1)} %copy-done.27, f32[32,1536]{1,0:T(8,128)S(1)} %copy-done.15, ...), custom_call_target="tpu_custom_call" | custom-call | flops 452984832 | bytes 6389764 | tf_op jit(solution)/shard_map/rows_backward/pallas_call | solution.py:128
  183.3 2.4 %unturn.1 = (bf16[4,2,192,256]{3,2,1,0:T(8,128)(2,1)S(1)}, bf16[4,2,192,256]{3,2,1,0:T(8,128)(2,1)}, bf16[2,192,256]{2,1,0:T(8,128)(2,1)S(1)}) custom-call(bf16[2,160,1536]{2,1,0:T(8,128)(2,1)S(1)} %get-tuple-element.73.product_ref, bf16[256,256]{1,0:T(8,128)(2,1)S(1)} %copy-done.48, bf16[256,256]{1,0:T(8,128)(2,1)S(1)} %copy-done.50), custom_call_target="tpu_custom_call" | custom-call | flops 12452984832 | bytes 3014656 | tf_op jit(solution)/shard_map/unturn/pallas_call | solution.py:128
  189.3 5.0 %all-to-all-start.5 = ((bf16[32,8,1536]{2,1,0:T(8,128)(2,1)}), bf16[32,8,1536]{2,1,0:T(8,128)(2,1)S(1)}, u32[]{:S(2)}, u32[]{:S(2)}) async-start(bf16[32,8,1536]{2,1,0:T(8,128)(2,1)} %bitcast.31), calls=%async_computation.5 | async-start | bytes 1572864 | tf_op jit(solution)/shard_map/all_to_all | solution.py:724
  198.5 4.2 %collective-permute-done.5.one_ref = bf16[384,256]{1,0:T(8,128)(2,1)S(1)} collective-permute-done((bf16[384,256]{1,0:T(8,128)(2,1)}, bf16[384,256]{1,0:T(8,128)(2,1)S(1)}, u32[]{:S(2)}, u32[]{:S(2)}) %collective-permute-start.5) | collective-permute-done | bytes 196640 | tf_op jit(solution)/shard_map/ppermute | solution.py:731
  202.7 3.1 %collective-permute-done.6.two_ref = bf16[384,256]{1,0:T(8,128)(2,1)S(1)} collective-permute-done((bf16[384,256]{1,0:T(8,128)(2,1)}, bf16[384,256]{1,0:T(8,128)(2,1)S(1)}, u32[]{:S(2)}, u32[]{:S(2)}) %collective-permute-start.6) | collective-permute-done | bytes 196640 | tf_op jit(solution)/shard_map/ppermute | solution.py:731
  207.6 2.4 %block_out.1 = bf16[1536,256]{1,0:T(8,128)(2,1)} custom-call(s32[1]{0:T(128)} %bitcast.channel_ref, bf16[1536,256]{1,0:T(8,128)(2,1)} %hidden.1.hidden_ref, bf16[384,256]{1,0:T(8,128)(2,1)S(1)} %copy-done.31, bf16[384,256]{1,0:T(8,128)(2,1)S(1)} %collective-permute-done.5.one_ref, bf16[384,256]{1,0:T(8,128)(2,1)S(1)} %collective-permute-done.6.two_ref, ...), custom_call_target="tpu_custom_call" | custom-call | bytes 2359300 | tf_op jit(solution)/shard_map/block_out/pallas_call | solution.py:128
  210.0 10.1 %all-to-all-done.5 = bf16[32,8,1536]{2,1,0:T(8,128)(2,1)S(1)} async-done(((bf16[32,8,1536]{2,1,0:T(8,128)(2,1)}), bf16[32,8,1536]{2,1,0:T(8,128)(2,1)S(1)}, u32[]{:S(2)}, u32[]{:S(2)}) %all-to-all-start.5) | async-done | bytes 786464 | tf_op jit(solution)/shard_map/all_to_all | solution.py:724
  223.6 3.9 %grad_filter.1 = f32[2,1536,256]{2,1,0:T(8,128)} custom-call(s32[1]{0:T(128)} %bitcast.1.place_ref.refs_0_, bf16[4,2,192,256]{3,2,1,0:T(8,128)(2,1)S(1)} %copy-done.17, bf16[4,2,192,256]{3,2,1,0:T(8,128)(2,1)} %collective-permute-done.8.pair_ref, bf16[2,192,256]{2,1,0:T(8,128)(2,1)} %collective-permute-done.9.lone_ref), custom_call_target="tpu_custom_call" | custom-call | bytes 4915204 | tf_op jit(solution)/shard_map/grad_filter/pallas_call | solution.py:128
  (138 shorter events, 50.5 us)
Async XLA Ops:
  7.2 109.6 %all-gather.2.cloned.1.call-start = ((), (), s32[]{:S(2)}) async-start(), calls=%async_computation.6 | async-start | bytes 10616832 | tf_op jit(solution)/shard_map/all_gather | solution.py:779
  18.8 39.8 %collective-permute-start.3 = (bf16[4,2,192,256]{3,2,1,0:T(8,128)(2,1)S(1)}, bf16[4,2,192,256]{3,2,1,0:T(8,128)(2,1)}, u32[]{:S(2)}, u32[]{:S(2)}) collective-permute-start(bf16[4,2,192,256]{3,2,1,0:T(8,128)(2,1)S(1)} %get-tuple-element.48.tail_ref), channel_id=1, source_target_pairs={{0,124},{4,120},{8,116},{12,112},{16,108},{20,104},{24,100},{28,96... | collective-permute-start | bytes 2359304 | tf_op jit(solution)/shard_map/ppermute | solution.py:759
  26.4 29.9 %all-to-all-start = ((bf16[32,8,1536]{2,1,0:T(8,128)(2,1)}), bf16[32,8,1536]{2,1,0:T(8,128)(2,1)S(1)}, u32[]{:S(2)}, u32[]{:S(2)}) async-start(bf16[32,8,1536]{2,1,0:T(8,128)(2,1)} %bitcast.3), calls=%async_computation | async-start | bytes 1572864 | tf_op jit(solution)/shard_map/all_to_all | solution.py:724
  33.2 12.5 %collective-permute-start = (bf16[384,256]{1,0:T(8,128)(2,1)}, bf16[384,256]{1,0:T(8,128)(2,1)S(1)}, u32[]{:S(2)}, u32[]{:S(2)}) collective-permute-start(bf16[384,256]{1,0:T(8,128)(2,1)} %get-tuple-element.43), channel_id=1, source_target_pairs={{0,1},{1,2},{2,3},{3,0},{4,5},{5,6},{6,7},{7,4},{8,9},{9,10},{10,1... | collective-permute-start | bytes 589832 | tf_op jit(solution)/shard_map/ppermute | solution.py:731
  34.4 20.6 %collective-permute-start.1 = (bf16[384,256]{1,0:T(8,128)(2,1)}, bf16[384,256]{1,0:T(8,128)(2,1)S(1)}, u32[]{:S(2)}, u32[]{:S(2)}) collective-permute-start(bf16[384,256]{1,0:T(8,128)(2,1)} %get-tuple-element.44), channel_id=1, source_target_pairs={{0,2},{1,3},{2,0},{3,1},{4,6},{5,7},{6,4},{7,5},{8,10},{9,11},{10,... | collective-permute-start | bytes 589832 | tf_op jit(solution)/shard_map/ppermute | solution.py:731
  36.9 18.8 %collective-permute-start.2 = (bf16[384,256]{1,0:T(8,128)(2,1)}, bf16[384,256]{1,0:T(8,128)(2,1)S(1)}, u32[]{:S(2)}, u32[]{:S(2)}) collective-permute-start(bf16[384,256]{1,0:T(8,128)(2,1)} %get-tuple-element.45), channel_id=1, source_target_pairs={{0,3},{1,0},{2,1},{3,2},{4,7},{5,4},{6,5},{7,6},{8,11},{9,8},{10,9... | collective-permute-start | bytes 589832 | tf_op jit(solution)/shard_map/ppermute | solution.py:731
  38.1 19.9 %collective-permute-start.4 = (bf16[2,192,256]{2,1,0:T(8,128)(2,1)}, bf16[2,192,256]{2,1,0:T(8,128)(2,1)S(1)}, u32[]{:S(2)}, u32[]{:S(2)}) collective-permute-start(bf16[2,192,256]{2,1,0:T(8,128)(2,1)} %get-tuple-element.49), channel_id=1, source_target_pairs={{4,124},{8,120},{12,116},{16,112},{20,108},{24,104},{28,100},{32,9... | collective-permute-start | bytes 589832 | tf_op jit(solution)/shard_map/ppermute | solution.py:760
  70.6 23.9 %copy-start.24 = (bf16[256,256]{1,0:T(8,128)(2,1)S(1)}, bf16[256,256]{1,0:T(8,128)(2,1)}, u32[]{:S(2)}) copy-start(bf16[256,256]{1,0:T(8,128)(2,1)} %constant.47.clone.table_ref) | copy-start | bytes 393220
  70.6 23.9 %all-to-all-start.1 = ((bf16[32,8,1920]{2,1,0:T(8,128)(2,1)}), bf16[32,8,1920]{2,1,0:T(8,128)(2,1)}, u32[]{:S(2)}, u32[]{:S(2)}) async-start(bf16[32,8,1920]{2,1,0:T(8,128)(2,1)} %bitcast.29), calls=%async_computation.1 | async-start | bytes 1966080 | tf_op jit(solution)/shard_map/all_to_all | solution.py:724
  78.3 22.5 %copy-start.10 = (f32[192,9]{1,0:T(8,128)}, f32[192,9]{1,0:T(8,128)S(1)}, u32[]{:S(2)}) copy-start(f32[192,9]{1,0:T(8,128)S(1)} %copy.19.taps_ref) | copy-start | bytes 20740
  100.9 15.9 %all-to-all-start.2 = ((bf16[4,384,256]{2,1,0:T(8,128)(2,1)}), bf16[4,384,256]{2,1,0:T(8,128)(2,1)S(1)}, u32[]{:S(2)}, u32[]{:S(2)}) async-start(bf16[4,384,256]{2,1,0:T(8,128)(2,1)} %bitcast.9), calls=%async_computation.2 | async-start | bytes 1572864 | tf_op jit(solution)/shard_map/all_to_all | solution.py:724
  154.2 25.7 %copy-start.27 = (bf16[256,256]{1,0:T(8,128)(2,1)S(1)}, bf16[256,256]{1,0:T(8,128)(2,1)}, u32[]{:S(2)}) copy-start(bf16[256,256]{1,0:T(8,128)(2,1)} %constant.43.clone.refs_3_) | copy-start | bytes 393220
  157.7 22.2 %copy-start.6 = (f32[2,32,1536]{2,1,0:T(8,128)S(1)}, f32[2,32,1536]{2,1,0:T(8,128)}, u32[]{:S(2)}) copy-start(f32[2,32,1536]{2,1,0:T(8,128)} %copy-done.5) | copy-start | bytes 1179652
  157.7 22.2 %copy-start.8 = (bf16[2,160,1536]{2,1,0:T(8,128)(2,1)S(1)}, bf16[2,160,1536]{2,1,0:T(8,128)(2,1)}, u32[]{:S(2)}) copy-start(bf16[2,160,1536]{2,1,0:T(8,128)(2,1)} %copy-done.7) | copy-start | bytes 2949124
  157.7 22.2 %copy-start.13 = (f32[32,1536]{1,0:T(8,128)S(1)}, f32[32,1536]{1,0:T(8,128)}, u32[]{:S(2)}) copy-start(f32[32,1536]{1,0:T(8,128)} %constant.45.clone.refs_5_) | copy-start | bytes 589828
  157.7 22.2 %copy-start.15 = (f32[32,1536]{1,0:T(8,128)S(1)}, f32[32,1536]{1,0:T(8,128)}, u32[]{:S(2)}) copy-start(f32[32,1536]{1,0:T(8,128)} %constant.44.clone.refs_4_) | copy-start | bytes 589828
  157.8 22.2 %copy-start.23 = (bf16[320,256]{1,0:T(8,128)(2,1)S(1)}, bf16[320,256]{1,0:T(8,128)(2,1)}, u32[]{:S(2)}) copy-start(bf16[320,256]{1,0:T(8,128)(2,1)} %constant.42.clone.refs_2_) | copy-start | bytes 491524
  187.4 36.2 %collective-permute-start.8 = (bf16[4,2,192,256]{3,2,1,0:T(8,128)(2,1)}, bf16[4,2,192,256]{3,2,1,0:T(8,128)(2,1)}, u32[]{:S(2)}, u32[]{:S(2)}) collective-permute-start(bf16[4,2,192,256]{3,2,1,0:T(8,128)(2,1)} %get-tuple-element.75), channel_id=1, source_target_pairs={{0,124},{4,120},{8,116},{12,112},{16,108},{20,104},{24,100},{28,96... | collective-permute-start | bytes 2359304 | tf_op jit(solution)/shard_map/ppermute | solution.py:866
  189.3 30.9 %all-to-all-start.5 = ((bf16[32,8,1536]{2,1,0:T(8,128)(2,1)}), bf16[32,8,1536]{2,1,0:T(8,128)(2,1)S(1)}, u32[]{:S(2)}, u32[]{:S(2)}) async-start(bf16[32,8,1536]{2,1,0:T(8,128)(2,1)} %bitcast.31), calls=%async_computation.5 | async-start | bytes 1572864 | tf_op jit(solution)/shard_map/all_to_all | solution.py:724
  194.3 8.5 %collective-permute-start.5 = (bf16[384,256]{1,0:T(8,128)(2,1)}, bf16[384,256]{1,0:T(8,128)(2,1)S(1)}, u32[]{:S(2)}, u32[]{:S(2)}) collective-permute-start(bf16[384,256]{1,0:T(8,128)(2,1)} %get-tuple-element.67), channel_id=1, source_target_pairs={{0,1},{1,2},{2,3},{3,0},{4,5},{5,6},{6,7},{7,4},{8,9},{9,10},{10,1... | collective-permute-start | bytes 589832 | tf_op jit(solution)/shard_map/ppermute | solution.py:731
  194.6 11.2 %collective-permute-start.6 = (bf16[384,256]{1,0:T(8,128)(2,1)}, bf16[384,256]{1,0:T(8,128)(2,1)S(1)}, u32[]{:S(2)}, u32[]{:S(2)}) collective-permute-start(bf16[384,256]{1,0:T(8,128)(2,1)} %get-tuple-element.68), channel_id=1, source_target_pairs={{0,2},{1,3},{2,0},{3,1},{4,6},{5,7},{6,4},{7,5},{8,10},{9,11},{10,... | collective-permute-start | bytes 589832 | tf_op jit(solution)/shard_map/ppermute | solution.py:731
  196.4 10.3 %collective-permute-start.7 = (bf16[384,256]{1,0:T(8,128)(2,1)}, bf16[384,256]{1,0:T(8,128)(2,1)S(1)}, u32[]{:S(2)}, u32[]{:S(2)}) collective-permute-start(bf16[384,256]{1,0:T(8,128)(2,1)} %get-tuple-element.69), channel_id=1, source_target_pairs={{0,3},{1,0},{2,1},{3,2},{4,7},{5,4},{6,5},{7,6},{8,11},{9,8},{10,9... | collective-permute-start | bytes 589832 | tf_op jit(solution)/shard_map/ppermute | solution.py:731
  197.1 23.1 %copy-start.4 = (bf16[1536,256]{1,0:T(8,128)(2,1)S(1)}, bf16[1536,256]{1,0:T(8,128)(2,1)}, u32[]{:S(2)}) copy-start(bf16[1536,256]{1,0:T(8,128)(2,1)} %copy-done.2) | copy-start | bytes 2359300
  197.1 26.5 %collective-permute-start.9 = (bf16[2,192,256]{2,1,0:T(8,128)(2,1)}, bf16[2,192,256]{2,1,0:T(8,128)(2,1)}, u32[]{:S(2)}, u32[]{:S(2)}) collective-permute-start(bf16[2,192,256]{2,1,0:T(8,128)(2,1)} %copy-done.44), channel_id=1, source_target_pairs={{124,4},{120,8},{116,12},{112,16},{108,20},{104,24},{100,28},{96,3... | collective-permute-start | bytes 589832 | tf_op jit(solution)/shard_map/ppermute | solution.py:867
  (46 other events, 148.6 us)
Sparse Core Ops, SparseCore 0:
  14.6 66.1 all-gather.1

commit v3 on v2

--- a/solution.py
+++ b/solution.py
@@ -1,5 +1,3 @@
-import functools
-
 import jax
 import jax.numpy as jnp
 import ml_dtypes
@@ -23,6 +21,7 @@
 WIDE = SLAB * 128
 POINTS = LEN * LEN
 HALF_UNITS = 384
+MESSAGE = 2 * LEN
 UNITS = 3072
 ROWS = ("y", "z", "core")
 SENT = (SLAB + 2) * CH
@@ -39,41 +38,25 @@
     return {-1: LANES + 256, SLAB: LANES + 320}.get(h, WIDE + 64 * (2 * (h % 4) + h // 4))
 
 
-def columns_of(device):
-    base = SLAB * device
-    return [base + 1, base + 2, base + 3, base + 4 if device < 16 else base]
-
-
 def column_tables():
-    w = np.arange(LEN)
-    forward, inverse = np.zeros((LEN, LEN)), np.zeros((LEN, LEN))
-    for device in range(ROWS_DEVICES):
-        for j, kw in enumerate(columns_of(device)):
-            turn = 2 * np.pi * (kw * w % LEN) / LEN
-            re, im = SLAB * device + j, SLAB * device + 4 + j
-            if device == 16 and j == 3:
-                forward[re] = inverse[re] = 1.0
-                forward[im] = inverse[im] = np.where(w % 2 == 0, 1.0, -1.0)
-            else:
-                forward[re], forward[im] = np.cos(turn), -np.sin(turn)
-                inverse[re], inverse[im] = 2 * np.cos(turn), -2 * np.sin(turn)
-    return forward, inverse
+    w, kw = np.arange(LEN)[None, :], np.arange(LEN)[:, None]
+    turn = (2 * np.pi * (kw * w % LEN) / LEN).reshape(ROWS_DEVICES, SLAB, LEN)
+    both = np.stack([np.cos(turn), -np.sin(turn)], axis=1)
+    return both.reshape(MESSAGE, LEN)
 
 
 def row_tables():
     k1, src = np.arange(32)[:, None], np.arange(32)[None, :]
     turn = 2 * np.pi * (k1 * src % 32) / 32
     cos, sin = np.cos(turn), np.sin(turn)
-    forward = np.zeros((2, 5, 32, 32, 2, 4))
-    inverse = np.zeros((32, 2, 4, 2, 4, 32))
-    for j in range(4):
+    forward = np.zeros((2, SLAB, 32, 32, 2, SLAB))
+    inverse = np.zeros((32, 2, SLAB, 2, SLAB, 32))
+    for j in range(SLAB):
         forward[0, j, :, :, 0, j], forward[0, j, :, :, 1, j] = cos, sin
         forward[1, j, :, :, 0, j], forward[1, j, :, :, 1, j] = -sin, cos
         inverse[:, 0, j, 0, j, :], inverse[:, 0, j, 1, j, :] = cos.T, -sin.T
         inverse[:, 1, j, 0, j, :], inverse[:, 1, j, 1, j, :] = sin.T, cos.T
-    forward[0, 4, :, :, 0, 3], forward[0, 4, :, :, 1, 3] = cos, -sin
-    forward[1, 4, :, :, 0, 3], forward[1, 4, :, :, 1, 3] = -sin, -cos
-    return forward.reshape(320, 256), inverse.reshape(256, 256)
+    return forward.reshape(MESSAGE, MESSAGE), inverse.reshape(MESSAGE, MESSAGE)
 
 
 def twiddle_tables():
@@ -85,23 +68,21 @@
     return np.cos(turn), np.sin(turn)
 
 
-def turn_tables():
+def turn_table():
     k2, k1 = np.divmod(np.arange(LEN), 32)
-    kh = k1 + 32 * k2
-    straight, mirrored = np.zeros((LEN, LEN)), np.zeros((LEN, LEN))
-    straight[np.arange(LEN), kh] = 1.0
-    mirrored[np.arange(LEN), -kh % LEN] = 1.0
-    return straight, mirrored
+    straight = np.zeros((LEN, LEN))
+    straight[np.arange(LEN), k1 + 32 * k2] = 1.0
+    return straight
 
 
 def narrow(table):
     return np.asarray(table, np.float64).astype(ml_dtypes.bfloat16)
 
 
-FORWARD_COLUMNS, INVERSE_COLUMNS = (narrow(t) for t in column_tables())
+COLUMNS = narrow(column_tables())
 FORWARD_ROWS, INVERSE_ROWS = (narrow(t) for t in row_tables())
 TWIDDLE_COS, TWIDDLE_SIN = (t.astype(np.float32) for t in twiddle_tables())
-STRAIGHT, MIRRORED = (narrow(t) for t in turn_tables())
+STRAIGHT = narrow(turn_table())
 UNIT = narrow(np.eye(LEN))
 
 
@@ -193,15 +174,6 @@
             turned_ref[half * CH : half * CH + CH] = rows.astype(BF16)
 
 
-def filter_split_kernel(filter_ref, head_ref, tail_ref, lone_ref, wide_ref):
-    for part in range(2):
-        fill_wide(wide_ref, filter_ref[part])
-        for i in range(4):
-            tail_ref[i, part] = every_eighth(wide_ref, 4 + i).astype(BF16)
-            head_ref[i, part] = every_eighth(wide_ref, i).astype(BF16)
-        lone_ref[part] = head_ref[0, part]
-
-
 def put_spectrum(target_ref, part, column, block):
     rows = slice(column * 32, column * 32 + 32)
     for k2 in range(SLAB):
@@ -211,33 +183,12 @@
         target_ref[part, rows, at : at + 64] = piece[:, 128:]
 
 
-def filter_kernel(
-    place_ref, head_ref, tail_ref, pair_ref, lone_ref, straight_ref, mirrored_ref, main_ref, cross_ref
-):
-    device = place_ref[0]
-    low, special = device < 16, device == 16
-    scale = 0.5 / POINTS
+def filter_kernel(filter_ref, straight_ref, main_ref, wide_ref):
     for part in range(2):
-        sign = 1.0 if part == 0 else -1.0
-        for j in range(3):
-            straight = nt(straight_ref[...], head_ref[1 + j, part])
-            mirrored = nt(mirrored_ref[...], pair_ref[3 - j, part])
-            put_spectrum(main_ref, part, j, (straight + sign * mirrored) * scale)
-        own = jnp.where(low, tail_ref[0, part], head_ref[0, part])
-        other = jnp.where(low, pair_ref[0, part], lone_ref[part])
-        o, q = nt(straight_ref[...], own), nt(straight_ref[...], other)
-        o_back = nt(mirrored_ref[...], own) * sign
-        q_back = nt(mirrored_ref[...], other) * sign
-        usual = (o + q_back) * scale
-        put_spectrum(
-            main_ref, part, 3, jnp.where(special, (o + o_back + q + q_back) * (0.5 * scale), usual)
-        )
-        put_spectrum(
-            cross_ref,
-            part,
-            0,
-            jnp.where(special, (q + q_back - o - o_back) * (0.5 * scale), 0.0 * usual),
-        )
+        fill_wide(wide_ref, filter_ref[part])
+        for j in range(SLAB):
+            turned = nt(straight_ref[...], every_eighth(wide_ref, j).astype(BF16))
+            put_spectrum(main_ref, part, j, (turned * (1.0 / POINTS)).astype(BF16))
 
 
 def eighth_turn(value, step, sign):
@@ -312,18 +263,19 @@
 
 
 def moved_rows(block, step):
-    empty = jnp.zeros((SLAB, block.shape[1]), block.dtype)
+    rows = 2 * SLAB
+    empty = jnp.zeros((rows, block.shape[1]), block.dtype)
     if step > 0:
-        return jnp.concatenate([empty, block[:-SLAB]], axis=0)
-    return jnp.concatenate([block[SLAB:], empty], axis=0)
+        return jnp.concatenate([empty, block[:-rows]], axis=0)
+    return jnp.concatenate([block[rows:], empty], axis=0)
 
 
 def row_body(saves, refs):
-    place_ref, received_ref, fwd_ref, inv_ref, cos_ref, sin_ref, main_ref, cross_ref = refs[:8]
+    received_ref, fwd_ref, inv_ref, cos_ref, sin_ref, main_ref = refs[:6]
     if saves:
-        message_ref, seen_ref, mixed_ref, ready_ref = refs[8:]
+        message_ref, seen_ref, mixed_ref, ready_ref = refs[6:]
     else:
-        seen_ref, message_ref, product_ref, mixed_ref, ready_ref = refs[8:]
+        seen_ref, message_ref, product_ref, mixed_ref, ready_ref = refs[6:]
 
     def joined(at, width, edge, step):
         rows = received_ref[:, at : at + width].astype(F32)
@@ -339,88 +291,32 @@
             at = narrow_at(h)
             mixed_ref[:, at : at + 64] = joined(at, 64, narrow_at(edge), step)
 
-    def spectrum(group):
-        at = pl.multiple_of(group * 16, 16)
-        table = pl.ds(pl.multiple_of(lax.rem(group, 2) * 16, 16), 16)
-        return to_frequencies(
-            mixed_ref[pl.ds(at, 16), :],
-            mixed_ref[pl.ds(160 + at, 16), :],
-            cos_ref[table, :],
-            sin_ref[table, :],
-        )
-
-    def save(group, blocks):
-        at = pl.ds(pl.multiple_of(group * 16, 16), 16)
-        for n, value in enumerate(blocks):
-            for part in range(2):
-                seen_ref[part, at, n * 128 : n * 128 + 128] = value[part].astype(BF16)
-
-    def times(value, n, source_ref, at):
-        k_re = source_ref[0, at, n * 128 : n * 128 + 128]
-        k_im = source_ref[1, at, n * 128 : n * 128 + 128]
-        re, im = value
-        if saves:
-            return re * k_re - im * k_im, im * k_re + re * k_im
-        return re * k_re + im * k_im, im * k_re - re * k_im
-
-    def store_back(group, blocks):
-        table = pl.ds(pl.multiple_of(lax.rem(group, 2) * 16, 16), 16)
-        re, im = to_tokens_rows(blocks, cos_ref[table, :], sin_ref[table, :])
-        at = pl.multiple_of(group * 16, 16)
-        ready_ref[pl.ds(at, 16), :] = re.astype(BF16)
-        ready_ref[pl.ds(128 + at, 16), :] = im.astype(BF16)
-
-    def seen(group, n):
-        at = pl.ds(pl.multiple_of(group * 16, 16), 16)
-        return tuple(seen_ref[part, at, n * 128 : n * 128 + 128].astype(F32) for part in range(2))
-
-    def product(a, b, factor):
-        re = (a[0] * b[0] + a[1] * b[1]) * factor
-        return re, (b[1] * a[0] - b[0] * a[1]) * factor
-
-    def put_product(group, n, value):
-        at = pl.ds(pl.multiple_of(group * 16, 16), 16)
-        for part in range(2):
-            product_ref[part, at, n * 128 : n * 128 + 128] = value[part].astype(BF16)
-
-    def plain(group, carry):
-        at = pl.ds(pl.multiple_of(group * 16, 16), 16)
-        values = spectrum(group)
-        if saves:
-            save(group, values)
-        else:
-            for n, value in enumerate(values):
-                put_product(group, n, product(seen(group, n), value, 1.0 / POINTS))
-        store_back(group, [times(v, n, main_ref, at) for n, v in enumerate(values)])
+    def group(index, carry):
+        at = pl.ds(pl.multiple_of(index * 16, 16), 16)
+        at_im = pl.ds(pl.multiple_of(LEN + index * 16, 16), 16)
+        table = pl.ds(pl.multiple_of(lax.rem(index, 2) * 16, 16), 16)
+        cos, sin = cos_ref[table, :], sin_ref[table, :]
+        values = to_frequencies(mixed_ref[at, :], mixed_ref[at_im, :], cos, sin)
+        filtered = []
+        for n, (re, im) in enumerate(values):
+            lanes = slice(n * 128, n * 128 + 128)
+            k_re, k_im = main_ref[0, at, lanes].astype(F32), main_ref[1, at, lanes].astype(F32)
+            if saves:
+                seen_ref[0, at, lanes], seen_ref[1, at, lanes] = re.astype(BF16), im.astype(BF16)
+                filtered.append((re * k_re - im * k_im, im * k_re + re * k_im))
+            else:
+                x_re, x_im = seen_ref[0, at, lanes].astype(F32), seen_ref[1, at, lanes].astype(F32)
+                product_re = (x_re * re + x_im * im) * (1.0 / POINTS)
+                product_im = (im * x_re - re * x_im) * (1.0 / POINTS)
+                product_ref[0, at, lanes] = product_re.astype(BF16)
+                product_ref[1, at, lanes] = product_im.astype(BF16)
+                filtered.append((re * k_re + im * k_im, im * k_re - re * k_im))
+        re, im = to_tokens_rows(filtered, cos, sin)
+        ready_ref[at, :] = re.astype(BF16)
+        ready_ref[at_im, :] = im.astype(BF16)
         return carry
 
-    def packed(group, carry):
-        at = pl.ds(pl.multiple_of(group * 16, 16), 16)
-        cross_at = pl.ds(pl.multiple_of((group - 6) * 16, 16), 16)
-        values, mirrors = spectrum(group), spectrum(group + 2)
-        if saves:
-            save(group, values)
-            save(group + 2, mirrors)
-        else:
-            special = place_ref[0] == 16
-            for n, (value, mirror) in enumerate(zip(values, mirrors)):
-                first, first_mirror = seen(group, n), seen(group + 2, n)
-                usual = product(first, value, 1.0 / POINTS)
-                odd = product(sub(first, first_mirror), sub(value, mirror), 0.25 / POINTS)
-                even = product(add(first, first_mirror), add(value, mirror), 0.25 / POINTS)
-                put_product(group, n, [jnp.where(special, a, b) for a, b in zip(odd, usual)])
-                put_product(group + 2, n, [jnp.where(special, a, b) for a, b in zip(even, usual)])
-        store_back(
-            group,
-            [
-                add(times(v, n, main_ref, at), times(m, n, cross_ref, cross_at))
-                for n, (v, m) in enumerate(zip(values, mirrors))
-            ],
-        )
-        return carry
-
-    lax.fori_loop(0, 6, plain, 0)
-    lax.fori_loop(6, 8, packed, 0)
+    lax.fori_loop(0, 16, group, 0)
     for at in range(0, LANES, 512):
         block = nn(inv_ref[...], ready_ref[:, at : at + 512])
         message_ref[:, at : at + 512] = block.astype(BF16)
@@ -663,7 +559,7 @@
             bytes_accessed=4 * UNITS * ALL_CH + 8 * LANES * LEN,
             transcendentals=2 * tokens * UNITS,
         ),
-        compiler_params=pltpu.CompilerParams(vmem_limit_bytes=28 * MIB),
+        compiler_params=pltpu.CompilerParams(vmem_limit_bytes=48 * MIB),
     )(channel, hidden, *dy_parts, gain, jnp.asarray(UNIT), weights, weights)
 
 
@@ -689,34 +585,16 @@
     out_ref[...] = take_wide(wide_ref)
 
 
-def unturn_kernel(product_ref, straight_ref, mirrored_ref, own_ref, pair_ref, lone_ref, block_ref):
-    def gather(part, column):
-        rows = slice(column * 32, column * 32 + 32)
-        for k2 in range(SLAB):
-            to = slice(k2 * 32, k2 * 32 + 32)
-            at = WIDE + 64 * k2
-            block_ref[to, :128] = product_ref[part, rows, k2 * 128 : k2 * 128 + 128]
-            block_ref[to, 128:] = product_ref[part, rows, at : at + 64]
-
+def grad_filter_kernel(product_ref, straight_ref, out_ref, block_ref, wide_ref):
     for part in range(2):
-        sign = 1.0 if part == 0 else -1.0
-        for j in range(4):
-            gather(part, j)
-            own_ref[j, part] = tn(block_ref[...], straight_ref[...]).astype(BF16)
-            pair_ref[3 - j, part] = (tn(block_ref[...], mirrored_ref[...]) * sign).astype(BF16)
-        gather(part, 4)
-        lone_ref[part] = (tn(block_ref[...], mirrored_ref[...]) * sign).astype(BF16)
-
-
-def grad_filter_kernel(place_ref, own_ref, pair_ref, lone_ref, out_ref, wide_ref):
-    low = place_ref[0] < 16
-    for part in range(2):
-        parts = [jnp.where(low, lone_ref[part], own_ref[3, part])]
-        parts += [own_ref[j, part] for j in range(3)]
-        parts += [jnp.where(low, own_ref[3, part], pair_ref[0, part])]
-        parts += [pair_ref[n, part] for n in range(1, 4)]
-        for i, value in enumerate(parts):
-            put_eighth(wide_ref, i, value.astype(F32))
+        for j in range(SLAB):
+            rows = slice(j * 32, j * 32 + 32)
+            for k2 in range(SLAB):
+                to = slice(k2 * 32, k2 * 32 + 32)
+                at = WIDE + 64 * k2
+                block_ref[to, :128] = product_ref[part, rows, k2 * 128 : k2 * 128 + 128]
+                block_ref[to, 128:] = product_ref[part, rows, at : at + 64]
+            put_eighth(wide_ref, j, tn(block_ref[...], straight_ref[...]))
         out_ref[part] = take_wide(wide_ref)
 
 
@@ -737,46 +615,25 @@
 
 
 def on_device(tile_image, spectral_filter, conv_taps, norm_gain, up_weight, down_weight, upstream):
-    device = lax.axis_index(ROWS)
-    place = device.reshape(1).astype(jnp.int32)
     channel = lax.axis_index("ch").reshape(1).astype(jnp.int32)
     flat = (LANES, LEN)
     tables = [jnp.asarray(t) for t in (FORWARD_ROWS, INVERSE_ROWS, TWIDDLE_COS, TWIDDLE_SIN)]
-    forward_columns, inverse_columns = jnp.asarray(FORWARD_COLUMNS), jnp.asarray(INVERSE_COLUMNS)
-    straight, mirrored = jnp.asarray(STRAIGHT), jnp.asarray(MIRRORED)
-
+    columns, straight = jnp.asarray(COLUMNS), jnp.asarray(STRAIGHT)
     wide = pltpu.VMEM((2, LANES, 128), F32)
-    head, tail, lone = kernel_call(
-        filter_split_kernel,
-        "filter_split",
-        [shape((4, 2, CH, LEN), BF16), shape((4, 2, CH, LEN), BF16), shape((2, CH, LEN), BF16)],
-        [wide],
-        [spectral_filter.reshape(2, LANES, LEN)],
-        16,
-    )
-    opposite = [(i, ROWS_DEVICES - 1 - i) for i in range(ROWS_DEVICES)]
-    lone_in = [(i, ROWS_DEVICES - i) for i in range(1, 16)] + [(0, 16)]
-    pair_filter = lax.ppermute(tail, ROWS, opposite)
-    lone_filter = lax.ppermute(lone, ROWS, lone_in)
     message, signal = kernel_call(
         columns_kernel,
         "columns",
-        [shape((LEN, LANES), BF16), shape(flat, BF16)],
+        [shape((MESSAGE, LANES), BF16), shape(flat, BF16)],
         [wide, pltpu.VMEM(flat, BF16)],
-        [tile_image.reshape(flat), forward_columns],
+        [tile_image.reshape(flat), columns],
         16,
-        2 * LEN * LEN * LANES,
+        2 * MESSAGE * LEN * LANES,
     )
     received = to_peers(message, ROWS)
 
-    (up_own, down_own, upstream_rows), _ = after(
-        (up_weight, down_weight, upstream.reshape(flat)), message
-    )
-    start = lax.axis_index("core") * HALF_UNITS
-    own_up = lax.dynamic_slice_in_dim(up_own, start, HALF_UNITS, axis=1).T
-    own_down = lax.dynamic_slice_in_dim(down_own, start, HALF_UNITS, axis=0)
-    pack = jnp.concatenate([own_up, own_down], axis=1)
-    weights = lax.all_gather(pack, ("core", "ch"), axis=0, tiled=True)
+    (upstream_rows, filter_rows), _ = after(
+        (upstream.reshape(flat), spectral_filter.reshape(2, LANES, LEN)), message
+    )
     dy, *dy_turned = kernel_call(
         unfold_kernel,
         "unfold",
@@ -787,30 +644,34 @@
         smem=1,
         hint=6,
     )
+    (up_own, down_own), _ = after((up_weight, down_weight), dy_turned)
+    start = lax.axis_index("core") * HALF_UNITS
+    own_up = lax.dynamic_slice_in_dim(up_own, start, HALF_UNITS, axis=1).T
+    own_down = lax.dynamic_slice_in_dim(down_own, start, HALF_UNITS, axis=0)
+    pack = jnp.concatenate([own_up, own_down], axis=1)
+    weights = lax.all_gather(pack, ("core", "ch"), axis=0, tiled=True)
     dy_parts = turned_exchange(dy_turned)
-    main, cross = kernel_call(
+    (main,) = kernel_call(
         filter_kernel,
         "filter",
-        [shape((2, 128, LANES), F32), shape((2, 32, LANES), F32)],
-        [],
-        [place, head, tail, pair_filter, lone_filter, straight, mirrored],
+        [shape((2, LEN, LANES), BF16)],
+        [wide],
+        [filter_rows, straight],
         16,
-        2 * 14 * LEN * LEN * CH,
-        smem=1,
+        2 * 16 * LEN * LEN * CH,
         hint=6,
     )
-    received, dy_parts = after(received, dy_parts)
-
-    row_scratch = [pltpu.VMEM((320, LANES), F32), pltpu.VMEM((LEN, LANES), BF16)]
+    received, dy_parts, main = lax.optimization_barrier((received, dy_parts, main))
+    row_scratch = [pltpu.VMEM((MESSAGE, LANES), F32), pltpu.VMEM((MESSAGE, LANES), BF16)]
+    row_flops = 4 * MESSAGE * MESSAGE * LANES
     message, seen = kernel_call(
         rows_forward_kernel,
         "rows_forward",
-        [shape((LEN, SENT), BF16), shape((2, 160, LANES), BF16)],
+        [shape((MESSAGE, SENT), BF16), shape((2, LEN, LANES), BF16)],
         row_scratch,
-        [place, received, *tables, main, cross],
+        [received, *tables, main],
         20,
-        2 * 576 * LEN * LANES,
-        smem=1,
+        row_flops,
     )
     received = to_peers(message, ROWS)
     (hidden,) = kernel_call(
@@ -818,9 +679,9 @@
         "hidden",
         [shape(flat, BF16)],
         [pltpu.VMEM((SENT, LEN), BF16)],
-        [received, inverse_columns, conv_taps, signal],
+        [received, columns, conv_taps, signal],
         16,
-        2 * LEN * LEN * SENT,
+        2 * MESSAGE * LEN * SENT,
     )
     hidden_tokens = to_peers(hidden, "ch")
     *out_turned, grad_message = mlp(
@@ -830,58 +691,46 @@
     (message,) = kernel_call(
         gradient_columns_kernel,
         "gradient_columns",
-        [shape((LEN, SENT), BF16)],
+        [shape((MESSAGE, SENT), BF16)],
         [pltpu.VMEM((SENT, LEN), BF16)],
-        [dy, grad_mlp, conv_taps, forward_columns],
+        [dy, grad_mlp, conv_taps, columns],
         16,
-        2 * LEN * LEN * SENT,
+        2 * MESSAGE * LEN * SENT,
     )
     out_turned, message = after(out_turned, message)
+    received = to_peers(message, ROWS)
+    message, products = kernel_call(
+        rows_backward_kernel,
+        "rows_backward",
+        [shape((MESSAGE, LANES), BF16), shape((2, LEN, LANES), BF16)],
+        row_scratch,
+        [received, *tables, main, seen],
+        20,
+        row_flops,
+    )
     received = to_peers(message, ROWS)
     out_parts = turned_exchange(out_turned)
     (block_out,) = kernel_call(
-        block_out_kernel, "block_out", [shape(flat, BF16)], [wide], [channel, hidden, *out_parts], 16, smem=1
-    )
-    message, products = kernel_call(
-        rows_backward_kernel,
-        "rows_backward",
-        [shape((LEN, LANES), BF16), shape((2, 160, LANES), BF16)],
-        row_scratch,
-        [place, received, *tables, main, cross, seen],
-        20,
-        2 * 576 * LEN * LANES,
-        smem=1,
-    )
-    received = to_peers(message, ROWS)
-    own, pair, lone = kernel_call(
-        unturn_kernel,
-        "unturn",
-        [shape((4, 2, CH, LEN), BF16), shape((4, 2, CH, LEN), BF16), shape((2, CH, LEN), BF16)],
-        [pltpu.VMEM((LEN, CH), BF16)],
-        [products, straight, mirrored],
-        16,
-        2 * 18 * LEN * LEN * CH,
-        hint=12,
-    )
-    pair = lax.ppermute(pair, ROWS, opposite)
-    lone = lax.ppermute(lone, ROWS, [(b, a) for a, b in lone_in])
+        block_out_kernel, "block_out", [shape(flat, BF16)], [wide], [channel, hidden, *out_parts], 16, smem=1, hint=6
+    )
     (grad_filter,) = kernel_call(
         grad_filter_kernel,
         "grad_filter",
         [shape((2, LANES, LEN), F32)],
-        [wide],
-        [place, own, pair, lone],
+        [pltpu.VMEM((LEN, CH), BF16), wide],
+        [products, straight],
         16,
-        smem=1,
+        2 * 16 * LEN * LEN * CH,
+        hint=12,
     )
     (grad_image,) = kernel_call(
         image_kernel,
         "image",
         [shape(flat, F32)],
         [wide],
-        [received, inverse_columns, dy, grad_mlp],
+        [received, columns, dy, grad_mlp],
         16,
-        2 * LEN * LEN * LANES,
+        2 * MESSAGE * LEN * LANES,
     )
     slab = (CH, SLAB, LEN)
     return (

time: 236 us -> 242 us (1.025)
  waiting for transfers between devices: 58.4 us -> 87.5 us
  blocking collectives: 35.5 us -> 12.5 us
  starting transfers between devices: 45.4 us -> 39.2 us
  local copies, waits for them, and re-layouts: 31.8 us -> 37.6 us
    all_to_all x4 -> x5, waiting for transfers between devices: 38.2 us -> 81.6 us  [to_peers(): return lax.all_to_all(values, axis, split_axis=0, concat_axis=0, tiled=True)]
    all_to_all x2 -> x1, blocking collectives: 35.5 us -> 12.5 us  [to_peers(): return lax.all_to_all(values, axis, split_axis=0, concat_axis=0, tiled=True)]
    ppermute x4 -> x0, starting transfers between devices: 17.4 us -> none  [the longest x1 7.6 us: on_device(): pair_filter = lax.ppermute(tail, ROWS, opposite)]
    ppermute x6, waiting for transfers between devices: 17.9 us -> 5.9 us  [turned_exchange(): received.append(lax.ppermute(parts[turn], 'ch', pairs))]
    all_to_all x4 -> x5, starting transfers between devices: 20.3 us -> 31.5 us  [to_peers(): return lax.all_to_all(values, axis, split_axis=0, concat_axis=0, tiled=True)]
    unnamed x111 -> x113, local copies, waits for them, and re-layouts: 30.1 us -> 36.8 us
    pallas_call x12 -> x10, Pallas kernels: 32 us -> 31.3 us  [kernel_call(): pl.pallas_call(body, name=name, grid=(1,), out_shape=tuple(outs), in_spec...]
  transfers between devices with their start and end apart: 15 -> 12, of which waited for: 10 -> 6; matrix products, arithmetic and copies ran while one was open for 0% -> 0% of each run, Pallas kernels for 7% -> 10%
where the time goes in v3:
time: 242 us; the launch traced here: 240 us
  waiting for transfers between devices  87.5 us (36%)
  Pallas kernels  47.8 us (20%)
  starting transfers between devices  39.2 us (16%)
  local copies, waits for them, and re-layouts  37.6 us (16%)
  between operations  14.4 us (6%)
  blocking collectives  12.5 us (5%)
    all_to_all x5, waiting for transfers between devices, to_peers(): return lax.all_to_all(values, axis, split_axis=0, concat_axis=0, tiled=True)  81.6 us
    unnamed x113, local copies, waits for them, and re-layouts  36.8 us
    all_to_all x5, starting transfers between devices, to_peers(): return lax.all_to_all(values, axis, split_axis=0, concat_axis=0, tiled=True)  31.5 us
    pallas_call x10, Pallas kernels, kernel_call(): pl.pallas_call(body, name=name, grid=(1,), out_shape=tuple(outs), in_spec...  31.3 us
    pallas_call x1, Pallas kernels, mlp(): pl.pallas_call(mlp_kernel, name='mlp', grid=(steps,), out_shape=(*(shape(...  16.5 us
    all_to_all x1, blocking collectives, to_peers(): return lax.all_to_all(values, axis, split_axis=0, concat_axis=0, tiled=True)  12.5 us
    ppermute x6, starting transfers between devices, turned_exchange(): received.append(lax.ppermute(parts[turn], 'ch', pairs))  7.72 us
    ppermute x6, waiting for transfers between devices, turned_exchange(): received.append(lax.ppermute(parts[turn], 'ch', pairs))  5.9 us
  transfers between devices with their start and end apart: 12, of which 6 were waited for; matrix products, arithmetic and copies ran while one was open for 0% of the time, Pallas kernels for 10%

profile of v3, /device:TPU:1, one launch (start us, length us, event | category | flops | bytes accessed | tf_op | source)
XLA Modules:
  0.0 240.3 jit_solution(1965025241910765774)
XLA Ops:
  9.4 2.0 columns.1
  19.7 9.6 %all-to-all-start = ((bf16[32,16,1536]{2,1,0:T(8,128)(2,1)}), bf16[32,16,1536]{2,1,0:T(8,128)(2,1)S(1)}, u32[]{:S(2)}, u32[]{:S(2)}) async-start(bf16[32,16,1536]{2,1,0:T(8,128)(2,1)} %bitcast.2), calls=%async_computation | async-start | bytes 3145728 | tf_op jit(solution)/shard_map/all_to_all | solution.py:602
  30.7 2.5 %collective-permute-start.1 = (bf16[384,256]{1,0:T(8,128)(2,1)}, bf16[384,256]{1,0:T(8,128)(2,1)S(1)}, u32[]{:S(2)}, u32[]{:S(2)}) collective-permute-start(bf16[384,256]{1,0:T(8,128)(2,1)} %copy-done.39), channel_id=1, source_target_pairs={{0,2},{1,3},{2,0},{3,1},{4,6},{5,7},{6,4},{7,5},{8,10},{9,11},{10,... | collective-permute-start | bytes 589832 | tf_op jit(solution)/shard_map/ppermute | solution.py:609
  34.3 2.6 %copy-done.29 = f32[2,192,8,256]{3,2,1,0:T(8,128)S(1)} copy-done((f32[2,192,8,256]{3,2,1,0:T(8,128)S(1)}, f32[2,192,8,256]{3,2,1,0:T(8,128)}, u32[]{:S(2)}) %copy-start.29) | copy-done | bytes 3145752
  40.7 5.9 %collective-permute-done.1.dy_two_ref = bf16[384,256]{1,0:T(8,128)(2,1)S(1)} collective-permute-done((bf16[384,256]{1,0:T(8,128)(2,1)}, bf16[384,256]{1,0:T(8,128)(2,1)S(1)}, u32[]{:S(2)}, u32[]{:S(2)}) %collective-permute-start.1) | collective-permute-done | bytes 196640 | tf_op jit(solution)/shard_map/ppermute | solution.py:609
  48.0 4.0 %all-to-all-done = bf16[32,16,1536]{2,1,0:T(8,128)(2,1)S(1)} async-done(((bf16[32,16,1536]{2,1,0:T(8,128)(2,1)}), bf16[32,16,1536]{2,1,0:T(8,128)(2,1)S(1)}, u32[]{:S(2)}, u32[]{:S(2)}) %all-to-all-start) | async-done | bytes 1572896 | tf_op jit(solution)/shard_map/all_to_all | solution.py:602
  55.5 5.5 %rows_forward.1 = (bf16[512,1920]{1,0:T(8,128)(2,1)S(1)}, bf16[2,256,1536]{2,1,0:T(8,128)(2,1)S(1)}) custom-call(bf16[512,1536]{1,0:T(8,128)(2,1)S(1)} %bitcast.29, bf16[512,512]{1,0:T(8,128)(2,1)S(1)} %copy-done.21, bf16[512,512]{1,0:T(8,128)(2,1)S(1)} %copy-done.23, f32[32,1536]{1,0:T(8,128)S(1)} %copy-done.25, f32[32,1536]{1,0:T(8,128)S(1)} %copy-done.27, ...), custom_call_target="tpu_custom_call" | custom-call | flops 1610612736 | bytes 8126464 | tf_op jit(solution)/shard_map/rows_forward/pallas_call | solution.py:109
  63.4 5.6 %all-to-all-start.1 = ((bf16[32,16,1920]{2,1,0:T(8,128)(2,1)}), bf16[32,16,1920]{2,1,0:T(8,128)(2,1)S(1)}, u32[]{:S(2)}, u32[]{:S(2)}) async-start(bf16[32,16,1920]{2,1,0:T(8,128)(2,1)} %bitcast.28), calls=%async_computation.1 | async-start | bytes 3932160 | tf_op jit(solution)/shard_map/all_to_all | solution.py:602
  69.1 26.8 %all-to-all-done.1 = bf16[32,16,1920]{2,1,0:T(8,128)(2,1)S(1)} async-done(((bf16[32,16,1920]{2,1,0:T(8,128)(2,1)}), bf16[32,16,1920]{2,1,0:T(8,128)(2,1)S(1)}, u32[]{:S(2)}, u32[]{:S(2)}) %all-to-all-start.1) | async-done | bytes 1966112 | tf_op jit(solution)/shard_map/all_to_all | solution.py:602
  97.0 3.4 %hidden.1.hidden_ref = bf16[1536,256]{1,0:T(8,128)(2,1)S(1)} custom-call(bf16[512,1920]{1,0:T(8,128)(2,1)S(1)} %bitcast.23, bf16[512,256]{1,0:T(8,128)(2,1)S(1)} %copy-done.10, f32[192,9]{1,0:T(8,128)S(1)} %copy.17.taps_ref, bf16[1536,256]{1,0:T(8,128)(2,1)S(1)} %copy-done.20), custom_call_target="tpu_custom_call" | custom-call | flops 503316480 | bytes 3808000 | tf_op jit(solution)/shard_map/hidden/pallas_call | solution.py:109
  101.4 4.1 %all-to-all-start.2 = ((bf16[4,384,256]{2,1,0:T(8,128)(2,1)}), bf16[4,384,256]{2,1,0:T(8,128)(2,1)S(1)}, u32[]{:S(2)}, u32[]{:S(2)}) async-start(bf16[4,384,256]{2,1,0:T(8,128)(2,1)} %bitcast.27), calls=%async_computation.2 | async-start | bytes 1572864 | tf_op jit(solution)/shard_map/all_to_all | solution.py:602
  105.5 11.2 %all-to-all-done.2 = bf16[4,384,256]{2,1,0:T(8,128)(2,1)S(1)} async-done(((bf16[4,384,256]{2,1,0:T(8,128)(2,1)}), bf16[4,384,256]{2,1,0:T(8,128)(2,1)S(1)}, u32[]{:S(2)}, u32[]{:S(2)}) %all-to-all-start.2) | async-done | bytes 786464 | tf_op jit(solution)/shard_map/all_to_all | solution.py:602
  119.5 16.5 %mlp.1 = (bf16[384,256]{1,0:T(8,128)(2,1)S(1)}, bf16[384,256]{1,0:T(8,128)(2,1)S(1)}, bf16[384,256]{1,0:T(8,128)(2,1)S(1)}, bf16[384,256]{1,0:T(8,128)(2,1)S(1)}, bf16[1536,256]{1,0:T(8,128)(2,1)S(1)}) custom-call(s32[1]{0:T(128)} %bitcast.channel_ref, bf16[1536,256]{1,0:T(8,128)(2,1)S(1)} %bitcast.31, bf16[384,256]{1,0:T(8,128)(2,1)S(1)} %copy-done.50, ...), custom_call_target="tpu_custom_call" | custom-call | flops 9663676416 | bytes 12582912 | tf_op jit(solution)/shard_map/mlp/pallas_call | solution.py:529
  136.1 12.5 %all_to_all.67 = bf16[4,384,256]{2,1,0:T(8,128)(2,1)S(1)} all-to-all(bf16[4,384,256]{2,1,0:T(8,128)(2,1)S(1)} %bitcast.32), channel_id=1, replica_groups=mesh['y'=4,'z'=4,'core'=2,'ch'=4] {'ch'}, dimensions={0} | all-to-all | bytes 1572864 | tf_op jit(solution)/shard_map/all_to_all | solution.py:602
  148.6 3.8 %gradient_columns.1 = bf16[512,1920]{1,0:T(8,128)(2,1)S(1)} custom-call(bf16[1536,256]{1,0:T(8,128)(2,1)S(1)} %copy-done.5, bf16[1536,256]{1,0:T(8,128)(2,1)S(1)} %bitcast.24, f32[192,9]{1,0:T(8,128)S(1)} %copy.17.taps_ref, bf16[512,256]{1,0:T(8,128)(2,1)S(1)} %copy-done.10), custom_call_target="tpu_custom_call" | custom-call | flops 503316480 | bytes 3808000 | tf_op jit(solution)/shard_map/gradient_columns/pallas_call | solution.py:109
  153.7 7.6 %all-to-all-start.4 = ((bf16[32,16,1920]{2,1,0:T(8,128)(2,1)}), bf16[32,16,1920]{2,1,0:T(8,128)(2,1)S(1)}, u32[]{:S(2)}, u32[]{:S(2)}) async-start(bf16[32,16,1920]{2,1,0:T(8,128)(2,1)} %bitcast.22), calls=%async_computation.4 | async-start | bytes 3932160 | tf_op jit(solution)/shard_map/all_to_all | solution.py:602
  161.7 1.8 collective-permute-start.4
  164.1 24.1 %all-to-all-done.4 = bf16[32,16,1920]{2,1,0:T(8,128)(2,1)S(1)} async-done(((bf16[32,16,1920]{2,1,0:T(8,128)(2,1)}), bf16[32,16,1920]{2,1,0:T(8,128)(2,1)S(1)}, u32[]{:S(2)}, u32[]{:S(2)}) %all-to-all-start.4) | async-done | bytes 1966112 | tf_op jit(solution)/shard_map/all_to_all | solution.py:602
  193.1 6.7 %rows_backward.1 = (bf16[512,1536]{1,0:T(8,128)(2,1)S(1)}, bf16[2,256,1536]{2,1,0:T(8,128)(2,1)S(1)}) custom-call(bf16[512,1920]{1,0:T(8,128)(2,1)S(1)} %bitcast.21, bf16[512,512]{1,0:T(8,128)(2,1)S(1)} %copy-done.22, bf16[512,512]{1,0:T(8,128)(2,1)S(1)} %copy-done.24, f32[32,1536]{1,0:T(8,128)S(1)} %copy-done.26, f32[32,1536]{1,0:T(8,128)S(1)} %copy-done.28, ...), custom_call_target="tpu_custom_call" | custom-call | flops 1610612736 | bytes 9699328 | tf_op jit(solution)/shard_map/rows_backward/pallas_call | solution.py:109
  202.1 4.6 %all-to-all-start.5 = ((bf16[32,16,1536]{2,1,0:T(8,128)(2,1)}), bf16[32,16,1536]{2,1,0:T(8,128)(2,1)S(1)}, u32[]{:S(2)}, u32[]{:S(2)}) async-start(bf16[32,16,1536]{2,1,0:T(8,128)(2,1)} %bitcast.30), calls=%async_computation.5 | async-start | bytes 3145728 | tf_op jit(solution)/shard_map/all_to_all | solution.py:602
  207.8 2.4 %block_out.1 = bf16[1536,256]{1,0:T(8,128)(2,1)} custom-call(s32[1]{0:T(128)} %bitcast.channel_ref, bf16[1536,256]{1,0:T(8,128)(2,1)S(1)} %copy-done.8, bf16[384,256]{1,0:T(8,128)(2,1)S(1)} %copy-done.52, bf16[384,256]{1,0:T(8,128)(2,1)} %collective-permute-done.3.one_ref, bf16[384,256]{1,0:T(8,128)(2,1)} %collective-permute-done.4.two_ref, ...), custom_call_target="tpu_custom_call" | custom-call | flops 6000000000 | bytes 2359300 | tf_op jit(solution)/shard_map/block_out/pallas_call | solution.py:109
  210.2 3.7 %grad_filter.1 = f32[2,1536,256]{2,1,0:T(8,128)} custom-call(bf16[2,256,1536]{2,1,0:T(8,128)(2,1)S(1)} %copy-done.31, bf16[256,256]{1,0:T(8,128)(2,1)S(1)} %copy-done.48), custom_call_target="tpu_custom_call" | custom-call | flops 12402653184 | bytes 4849664 | tf_op jit(solution)/shard_map/grad_filter/pallas_call | solution.py:109
  213.9 15.5 %all-to-all-done.5 = bf16[32,16,1536]{2,1,0:T(8,128)(2,1)S(1)} async-done(((bf16[32,16,1536]{2,1,0:T(8,128)(2,1)}), bf16[32,16,1536]{2,1,0:T(8,128)(2,1)S(1)}, u32[]{:S(2)}, u32[]{:S(2)}) %all-to-all-start.5) | async-done | bytes 1572896 | tf_op jit(solution)/shard_map/all_to_all | solution.py:602
  231.5 1.9 image.1
  (131 shorter events, 41.7 us)
Async XLA Ops:
  7.2 109.5 %all-gather.2.cloned.1.call-start = ((), (), s32[]{:S(2)}) async-start(), calls=%async_computation.6 | async-start | bytes 10616832 | tf_op jit(solution)/shard_map/all_gather | solution.py:652
  19.7 32.3 %all-to-all-start = ((bf16[32,16,1536]{2,1,0:T(8,128)(2,1)}), bf16[32,16,1536]{2,1,0:T(8,128)(2,1)S(1)}, u32[]{:S(2)}, u32[]{:S(2)}) async-start(bf16[32,16,1536]{2,1,0:T(8,128)(2,1)} %bitcast.2), calls=%async_computation | async-start | bytes 3145728 | tf_op jit(solution)/shard_map/all_to_all | solution.py:602
  29.4 22.7 %copy-start.21 = (bf16[512,512]{1,0:T(8,128)(2,1)S(1)}, bf16[512,512]{1,0:T(8,128)(2,1)}, u32[]{:S(2)}) copy-start(bf16[512,512]{1,0:T(8,128)(2,1)} %constant.27.clone.refs_1_) | copy-start | bytes 1572868
  29.4 22.7 %copy-start.25 = (f32[32,1536]{1,0:T(8,128)S(1)}, f32[32,1536]{1,0:T(8,128)}, u32[]{:S(2)}) copy-start(f32[32,1536]{1,0:T(8,128)} %constant.29.clone.refs_3_) | copy-start | bytes 589828
  29.4 10.7 %collective-permute-start = (bf16[384,256]{1,0:T(8,128)(2,1)}, bf16[384,256]{1,0:T(8,128)(2,1)S(1)}, u32[]{:S(2)}, u32[]{:S(2)}) collective-permute-start(bf16[384,256]{1,0:T(8,128)(2,1)} %copy-done.43), channel_id=1, source_target_pairs={{0,1},{1,2},{2,3},{3,0},{4,5},{5,6},{6,7},{7,4},{8,9},{9,10},{10,1... | collective-permute-start | bytes 589832 | tf_op jit(solution)/shard_map/ppermute | solution.py:609
  30.7 16.0 %collective-permute-start.1 = (bf16[384,256]{1,0:T(8,128)(2,1)}, bf16[384,256]{1,0:T(8,128)(2,1)S(1)}, u32[]{:S(2)}, u32[]{:S(2)}) collective-permute-start(bf16[384,256]{1,0:T(8,128)(2,1)} %copy-done.39), channel_id=1, source_target_pairs={{0,2},{1,3},{2,0},{3,1},{4,6},{5,7},{6,4},{7,5},{8,10},{9,11},{10,... | collective-permute-start | bytes 589832 | tf_op jit(solution)/shard_map/ppermute | solution.py:609
  33.1 14.2 %collective-permute-start.2 = (bf16[384,256]{1,0:T(8,128)(2,1)}, bf16[384,256]{1,0:T(8,128)(2,1)S(1)}, u32[]{:S(2)}, u32[]{:S(2)}) collective-permute-start(bf16[384,256]{1,0:T(8,128)(2,1)} %copy-done.36), channel_id=1, source_target_pairs={{0,3},{1,0},{2,1},{3,2},{4,7},{5,4},{6,5},{7,6},{8,11},{9,8},{10,9... | collective-permute-start | bytes 589832 | tf_op jit(solution)/shard_map/ppermute | solution.py:609
  63.4 32.5 %copy-start.10 = (bf16[512,256]{1,0:T(8,128)(2,1)S(1)}, bf16[512,256]{1,0:T(8,128)(2,1)}, u32[]{:S(2)}) copy-start(bf16[512,256]{1,0:T(8,128)(2,1)} %constant.31.clone.table_ref) | copy-start | bytes 786436
  63.4 32.5 %all-to-all-start.1 = ((bf16[32,16,1920]{2,1,0:T(8,128)(2,1)}), bf16[32,16,1920]{2,1,0:T(8,128)(2,1)S(1)}, u32[]{:S(2)}, u32[]{:S(2)}) async-start(bf16[32,16,1920]{2,1,0:T(8,128)(2,1)} %bitcast.28), calls=%async_computation.1 | async-start | bytes 3932160 | tf_op jit(solution)/shard_map/all_to_all | solution.py:602
  101.4 15.4 %copy-start.35 = (bf16[384,256]{1,0:T(8,128)(2,1)S(1)}, bf16[384,256]{1,0:T(8,128)(2,1)}, u32[]{:S(2)}) copy-start(bf16[384,256]{1,0:T(8,128)(2,1)} %copy-done.34) | copy-start | bytes 589828
  101.4 15.4 %copy-start.47 = (bf16[256,256]{1,0:T(8,128)(2,1)S(1)}, bf16[256,256]{1,0:T(8,128)(2,1)}, u32[]{:S(2)}) copy-start(bf16[256,256]{1,0:T(8,128)(2,1)} %constant.32.clone.straight_ref.unit_ref) | copy-start | bytes 393220
  101.4 15.3 %all-to-all-start.2 = ((bf16[4,384,256]{2,1,0:T(8,128)(2,1)}), bf16[4,384,256]{2,1,0:T(8,128)(2,1)S(1)}, u32[]{:S(2)}, u32[]{:S(2)}) async-start(bf16[4,384,256]{2,1,0:T(8,128)(2,1)} %bitcast.27), calls=%async_computation.2 | async-start | bytes 1572864 | tf_op jit(solution)/shard_map/all_to_all | solution.py:602
  136.0 16.4 %copy-start.42 = (bf16[384,256]{1,0:T(8,128)(2,1)}, bf16[384,256]{1,0:T(8,128)(2,1)S(1)}, u32[]{:S(2)}) copy-start(bf16[384,256]{1,0:T(8,128)(2,1)S(1)} %get-tuple-element.60) | copy-start | bytes 589828
  136.0 16.4 %copy-start.44 = (bf16[384,256]{1,0:T(8,128)(2,1)}, bf16[384,256]{1,0:T(8,128)(2,1)S(1)}, u32[]{:S(2)}) copy-start(bf16[384,256]{1,0:T(8,128)(2,1)S(1)} %get-tuple-element.59) | copy-start | bytes 589828
  136.0 16.4 %copy-start.45 = (bf16[384,256]{1,0:T(8,128)(2,1)}, bf16[384,256]{1,0:T(8,128)(2,1)S(1)}, u32[]{:S(2)}) copy-start(bf16[384,256]{1,0:T(8,128)(2,1)S(1)} %get-tuple-element.58) | copy-start | bytes 589828
  136.1 16.4 %copy-start.51 = (bf16[384,256]{1,0:T(8,128)(2,1)}, bf16[384,256]{1,0:T(8,128)(2,1)S(1)}, u32[]{:S(2)}) copy-start(bf16[384,256]{1,0:T(8,128)(2,1)S(1)} %get-tuple-element.57.own_ref) | copy-start | bytes 589828
  153.7 34.5 %copy-start.26 = (f32[32,1536]{1,0:T(8,128)S(1)}, f32[32,1536]{1,0:T(8,128)}, u32[]{:S(2)}) copy-start(f32[32,1536]{1,0:T(8,128)} %constant.29.clone.refs_3_) | copy-start | bytes 589828
  153.7 34.5 %copy-start.28 = (f32[32,1536]{1,0:T(8,128)S(1)}, f32[32,1536]{1,0:T(8,128)}, u32[]{:S(2)}) copy-start(f32[32,1536]{1,0:T(8,128)} %constant.30.clone.refs_4_) | copy-start | bytes 589828
  153.7 34.5 %all-to-all-start.4 = ((bf16[32,16,1920]{2,1,0:T(8,128)(2,1)}), bf16[32,16,1920]{2,1,0:T(8,128)(2,1)S(1)}, u32[]{:S(2)}, u32[]{:S(2)}) async-start(bf16[32,16,1920]{2,1,0:T(8,128)(2,1)} %bitcast.22), calls=%async_computation.4 | async-start | bytes 3932160 | tf_op jit(solution)/shard_map/all_to_all | solution.py:602
  161.3 45.4 %collective-permute-start.3 = (bf16[384,256]{1,0:T(8,128)(2,1)}, bf16[384,256]{1,0:T(8,128)(2,1)}, u32[]{:S(2)}, u32[]{:S(2)}) collective-permute-start(bf16[384,256]{1,0:T(8,128)(2,1)} %copy-done.45), channel_id=1, source_target_pairs={{0,1},{1,2},{2,3},{3,0},{4,5},{5,6},{6,7},{7,4},{8,9},{9,10},{10,1... | collective-permute-start | bytes 589832 | tf_op jit(solution)/shard_map/ppermute | solution.py:609
  161.7 45.0 %collective-permute-start.4 = (bf16[384,256]{1,0:T(8,128)(2,1)}, bf16[384,256]{1,0:T(8,128)(2,1)}, u32[]{:S(2)}, u32[]{:S(2)}) collective-permute-start(bf16[384,256]{1,0:T(8,128)(2,1)} %copy-done.44), channel_id=1, source_target_pairs={{0,2},{1,3},{2,0},{3,1},{4,6},{5,7},{6,4},{7,5},{8,10},{9,11},{10,... | collective-permute-start | bytes 589832 | tf_op jit(solution)/shard_map/ppermute | solution.py:609
  163.4 43.3 %collective-permute-start.5 = (bf16[384,256]{1,0:T(8,128)(2,1)}, bf16[384,256]{1,0:T(8,128)(2,1)}, u32[]{:S(2)}, u32[]{:S(2)}) collective-permute-start(bf16[384,256]{1,0:T(8,128)(2,1)} %copy-done.42), channel_id=1, source_target_pairs={{0,3},{1,0},{2,1},{3,2},{4,7},{5,4},{6,5},{7,6},{8,11},{9,8},{10,9... | collective-permute-start | bytes 589832 | tf_op jit(solution)/shard_map/ppermute | solution.py:609
  202.1 27.4 %all-to-all-start.5 = ((bf16[32,16,1536]{2,1,0:T(8,128)(2,1)}), bf16[32,16,1536]{2,1,0:T(8,128)(2,1)S(1)}, u32[]{:S(2)}, u32[]{:S(2)}) async-start(bf16[32,16,1536]{2,1,0:T(8,128)(2,1)} %bitcast.30), calls=%async_computation.5 | async-start | bytes 3145728 | tf_op jit(solution)/shard_map/all_to_all | solution.py:602
  210.2 19.2 %copy-start.3 = (bf16[4,384,256]{2,1,0:T(8,128)(2,1)S(1)}, bf16[4,384,256]{2,1,0:T(8,128)(2,1)}, u32[]{:S(2)}) copy-start(bf16[4,384,256]{2,1,0:T(8,128)(2,1)} %copy-done.2) | copy-start | bytes 2359300
  (44 other events, 90.2 us)
Sparse Core Ops, SparseCore 0:
  19.9 62.4 all-gather.1

commit v4 on v3

--- a/solution.py
+++ b/solution.py
@@ -102,7 +102,7 @@
     return pl.BlockSpec(dims, lambda *_: (0,) * len(dims), pipeline_mode=pl.Buffered(1))
 
 
-def kernel_call(body, name, outs, scratch, operands, vmem, flops=0, smem=0, hint=0):
+def kernel_call(body, name, outs, scratch, operands, vmem, flops=0, smem=0, beside=False):
     scalar = pl.BlockSpec(memory_space=pltpu.SMEM)
     moved = sum(a.size * a.dtype.itemsize for a in operands)
     moved += sum(o.size * np.dtype(o.dtype).itemsize for o in outs)
@@ -115,7 +115,9 @@
         out_specs=tuple(whole_block(o.shape) for o in outs),
         scratch_shapes=scratch,
         cost_estimate=pl.CostEstimate(
-            flops=flops + hint * 10**9, bytes_accessed=moved, transcendentals=0
+            flops=0 if beside else flops,
+            bytes_accessed=1024 if beside else moved,
+            transcendentals=0,
         ),
         compiler_params=pltpu.CompilerParams(vmem_limit_bytes=vmem * MIB),
     )(*operands)
@@ -614,6 +616,11 @@
     return lax.optimization_barrier((value, earlier))
 
 
+def fenced(values, axis, live):
+    values, live = lax.optimization_barrier((values, live))
+    return lax.optimization_barrier((to_peers(values, axis), live))
+
+
 def on_device(tile_image, spectral_filter, conv_taps, norm_gain, up_weight, down_weight, upstream):
     channel = lax.axis_index("ch").reshape(1).astype(jnp.int32)
     flat = (LANES, LEN)
@@ -642,7 +649,7 @@
         [channel, upstream_rows],
         16,
         smem=1,
-        hint=6,
+        beside=True,
     )
     (up_own, down_own), _ = after((up_weight, down_weight), dy_turned)
     start = lax.axis_index("core") * HALF_UNITS
@@ -659,7 +666,7 @@
         [filter_rows, straight],
         16,
         2 * 16 * LEN * LEN * CH,
-        hint=6,
+        beside=True,
     )
     received, dy_parts, main = lax.optimization_barrier((received, dy_parts, main))
     row_scratch = [pltpu.VMEM((MESSAGE, LANES), F32), pltpu.VMEM((MESSAGE, LANES), BF16)]
@@ -673,7 +680,9 @@
         20,
         row_flops,
     )
-    received = to_peers(message, ROWS)
+    live = (seen, main, signal, dy, dy_parts, conv_taps, norm_gain)
+    received, live = fenced(message, ROWS, live)
+    seen, main, signal, dy, dy_parts, conv_taps, norm_gain = live
     (hidden,) = kernel_call(
         hidden_kernel,
         "hidden",
@@ -683,11 +692,12 @@
         16,
         2 * MESSAGE * LEN * SENT,
     )
-    hidden_tokens = to_peers(hidden, "ch")
-    *out_turned, grad_message = mlp(
-        channel, hidden_tokens, dy_parts, norm_gain.reshape(1, ALL_CH), weights
-    )
-    grad_mlp = to_peers(grad_message, "ch")
+    live = (seen, main, dy, dy_parts, conv_taps, norm_gain.reshape(1, ALL_CH), hidden)
+    hidden_tokens, live = fenced(hidden, "ch", live)
+    seen, main, dy, dy_parts, conv_taps, gain_row, hidden = live
+    *out_turned, grad_message = mlp(channel, hidden_tokens, dy_parts, gain_row, weights)
+    grad_mlp, live = fenced(grad_message, "ch", (seen, main, dy, out_turned, conv_taps, hidden))
+    seen, main, dy, out_turned, conv_taps, hidden = live
     (message,) = kernel_call(
         gradient_columns_kernel,
         "gradient_columns",
@@ -697,8 +707,9 @@
         16,
         2 * MESSAGE * LEN * SENT,
     )
-    out_turned, message = after(out_turned, message)
-    received = to_peers(message, ROWS)
+    live = (seen, main, dy, out_turned, grad_mlp, hidden)
+    received, live = fenced(message, ROWS, live)
+    seen, main, dy, out_turned, grad_mlp, hidden = live
     message, products = kernel_call(
         rows_backward_kernel,
         "rows_backward",
@@ -708,10 +719,13 @@
         20,
         row_flops,
     )
+    (dy, out_turned, grad_mlp, hidden, products), message = after(
+        (dy, out_turned, grad_mlp, hidden, products), message
+    )
     received = to_peers(message, ROWS)
     out_parts = turned_exchange(out_turned)
     (block_out,) = kernel_call(
-        block_out_kernel, "block_out", [shape(flat, BF16)], [wide], [channel, hidden, *out_parts], 16, smem=1, hint=6
+        block_out_kernel, "block_out", [shape(flat, BF16)], [wide], [channel, hidden, *out_parts], 16, smem=1, beside=True
     )
     (grad_filter,) = kernel_call(
         grad_filter_kernel,
@@ -721,7 +735,7 @@
         [products, straight],
         16,
         2 * 16 * LEN * LEN * CH,
-        hint=12,
+        beside=True,
     )
     (grad_image,) = kernel_call(
         image_kernel,

time: 242 us -> 230 us (0.950)
  blocking collectives: 12.5 us -> 94.3 us
  waiting for transfers between devices: 87.5 us -> 24.5 us
  starting transfers between devices: 39.2 us -> 21.5 us
  local copies, waits for them, and re-layouts: 37.6 us -> 24.2 us
    all_to_all x1 -> x4, blocking collectives: 12.5 us -> 94.3 us  [to_peers(): return lax.all_to_all(values, axis, split_axis=0, concat_axis=0, tiled=True)]
    all_to_all x5 -> x2, waiting for transfers between devices: 81.6 us -> 13.2 us  [to_peers(): return lax.all_to_all(values, axis, split_axis=0, concat_axis=0, tiled=True)]
    all_to_all x5 -> x2, starting transfers between devices: 31.5 us -> 13.8 us  [to_peers(): return lax.all_to_all(values, axis, split_axis=0, concat_axis=0, tiled=True)]
    unnamed x113 -> x96, local copies, waits for them, and re-layouts: 36.8 us -> 21.9 us
    ppermute x6, waiting for transfers between devices: 5.9 us -> 11.3 us  [turned_exchange(): received.append(lax.ppermute(parts[turn], 'ch', pairs))]
  transfers between devices with their start and end apart: 12 -> 9, of which waited for: 6 -> 5; matrix products, arithmetic and copies ran while one was open for 0% -> 1% of each run, Pallas kernels for 10% -> 7%
where the time goes in v4:
time: 230 us; the launch traced here: 229 us
  blocking collectives  94.3 us (41%)
  Pallas kernels  48.8 us (21%)
  waiting for transfers between devices  24.5 us (11%)
  local copies, waits for them, and re-layouts  24.2 us (11%)
  starting transfers between devices  21.5 us (9%)
  between operations  14.4 us (6%)
    all_to_all x4, blocking collectives, to_peers(): return lax.all_to_all(values, axis, split_axis=0, concat_axis=0, tiled=True)  94.3 us
    pallas_call x10, Pallas kernels, kernel_call(): pl.pallas_call(body, name=name, grid=(1,), out_shape=tuple(outs), in_spec...  32.4 us
    unnamed x96, local copies, waits for them, and re-layouts  21.9 us
    pallas_call x1, Pallas kernels, mlp(): pl.pallas_call(mlp_kernel, name='mlp', grid=(steps,), out_shape=(*(shape(...  16.5 us
    all_to_all x2, starting transfers between devices, to_peers(): return lax.all_to_all(values, axis, split_axis=0, concat_axis=0, tiled=True)  13.8 us
    all_to_all x2, waiting for transfers between devices, to_peers(): return lax.all_to_all(values, axis, split_axis=0, concat_axis=0, tiled=True)  13.2 us
    ppermute x6, waiting for transfers between devices, turned_exchange(): received.append(lax.ppermute(parts[turn], 'ch', pairs))  11.3 us
    ppermute x6, starting transfers between devices, turned_exchange(): received.append(lax.ppermute(parts[turn], 'ch', pairs))  7.72 us
  transfers between devices with their start and end apart: 9, of which 5 were waited for; matrix products, arithmetic and copies ran while one was open for 1% of the time, Pallas kernels for 7%

profile of v4, /device:TPU:1, one launch (start us, length us, event | category | flops | bytes accessed | tf_op | source)
XLA Modules:
  0.0 229.0 jit_solution(14502529494631364996)
XLA Ops:
  9.4 2.0 columns.1
  12.3 1.4 unfold.1
  17.2 9.8 %all-to-all-start = ((bf16[32,16,1536]{2,1,0:T(8,128)(2,1)}), bf16[32,16,1536]{2,1,0:T(8,128)(2,1)}, u32[]{:S(2)}, u32[]{:S(2)}) async-start(bf16[32,16,1536]{2,1,0:T(8,128)(2,1)} %bitcast.2), calls=%async_computation | async-start | bytes 3145728 | tf_op jit(solution)/shard_map/all_to_all | solution.py:604
  28.3 2.4 %collective-permute-start.1 = (bf16[384,256]{1,0:T(8,128)(2,1)}, bf16[384,256]{1,0:T(8,128)(2,1)S(1)}, u32[]{:S(2)}, u32[]{:S(2)}) collective-permute-start(bf16[384,256]{1,0:T(8,128)(2,1)} %get-tuple-element.126), channel_id=1, source_target_pairs={{0,2},{1,3},{2,0},{3,1},{4,6},{5,7},{6,4},{7,5},{8,10},{9,11},{10,... | collective-permute-start | bytes 589832 | tf_op jit(solution)/shard_map/ppermute | solution.py:611
  31.9 2.6 %copy-done.5 = f32[2,192,8,256]{3,2,1,0:T(8,128)S(1)} copy-done((f32[2,192,8,256]{3,2,1,0:T(8,128)S(1)}, f32[2,192,8,256]{3,2,1,0:T(8,128)}, u32[]{:S(2)}) %copy-start.5) | copy-done | bytes 3145752
  36.5 7.8 %collective-permute-done.1.dy_two_ref = bf16[384,256]{1,0:T(8,128)(2,1)S(1)} collective-permute-done((bf16[384,256]{1,0:T(8,128)(2,1)}, bf16[384,256]{1,0:T(8,128)(2,1)S(1)}, u32[]{:S(2)}, u32[]{:S(2)}) %collective-permute-start.1) | collective-permute-done | bytes 196640 | tf_op jit(solution)/shard_map/ppermute | solution.py:611
  45.6 4.2 %all-to-all-done = bf16[32,16,1536]{2,1,0:T(8,128)(2,1)} async-done(((bf16[32,16,1536]{2,1,0:T(8,128)(2,1)}), bf16[32,16,1536]{2,1,0:T(8,128)(2,1)}, u32[]{:S(2)}, u32[]{:S(2)}) %all-to-all-start) | async-done | bytes 1572896 | tf_op jit(solution)/shard_map/all_to_all | solution.py:604
  52.7 6.9 %rows_forward.1 = (bf16[512,1920]{1,0:T(8,128)(2,1)S(1)}, bf16[2,256,1536]{2,1,0:T(8,128)(2,1)S(1)}) custom-call(bf16[512,1536]{1,0:T(8,128)(2,1)} %bitcast.3.refs_0_, bf16[512,512]{1,0:T(8,128)(2,1)S(1)} %copy-done.20, bf16[512,512]{1,0:T(8,128)(2,1)S(1)} %copy-done.22, f32[32,1536]{1,0:T(8,128)S(1)} %copy-done.27, f32[32,1536]{1,0:T(8,128)S(1)} %copy-done.29, ...), custom_call_target="tpu_custom_call" | custom-call | flops 1610612736 | bytes 8126464 | tf_op jit(solution)/shard_map/rows_forward/pallas_call | solution.py:109
  59.7 32.1 %all_to_all.71 = bf16[32,16,1920]{2,1,0:T(8,128)(2,1)S(1)} all-to-all(bf16[32,16,1920]{2,1,0:T(8,128)(2,1)S(1)} %bitcast.29), channel_id=1, replica_groups=mesh['y'=4,'z'=4,'core'=2,'ch'=4] {'y','z','core'}, dimensions={0} | all-to-all | bytes 3932160 | tf_op jit(solution)/shard_map/all_to_all | solution.py:604
  95.3 3.4 %hidden.1.hidden_ref = bf16[1536,256]{1,0:T(8,128)(2,1)S(1)} custom-call(bf16[512,1920]{1,0:T(8,128)(2,1)S(1)} %bitcast.22, bf16[512,256]{1,0:T(8,128)(2,1)S(1)} %copy-done.10, f32[192,9]{1,0:T(8,128)S(1)} %copy-done.26, bf16[1536,256]{1,0:T(8,128)(2,1)S(1)} %copy-done.19), custom_call_target="tpu_custom_call" | custom-call | flops 503316480 | bytes 3808000 | tf_op jit(solution)/shard_map/hidden/pallas_call | solution.py:109
  98.8 16.1 %all_to_all.72 = bf16[4,384,256]{2,1,0:T(8,128)(2,1)S(1)} all-to-all(bf16[4,384,256]{2,1,0:T(8,128)(2,1)S(1)} %bitcast.24), channel_id=1, replica_groups=mesh['y'=4,'z'=4,'core'=2,'ch'=4] {'ch'}, dimensions={0} | all-to-all | bytes 1572864 | tf_op jit(solution)/shard_map/all_to_all | solution.py:604
  115.7 16.5 %mlp.1 = (bf16[384,256]{1,0:T(8,128)(2,1)S(1)}, bf16[384,256]{1,0:T(8,128)(2,1)S(1)}, bf16[384,256]{1,0:T(8,128)(2,1)S(1)}, bf16[384,256]{1,0:T(8,128)(2,1)S(1)}, bf16[1536,256]{1,0:T(8,128)(2,1)S(1)}) custom-call(s32[1]{0:T(128)} %bitcast.channel_ref, bf16[1536,256]{1,0:T(8,128)(2,1)S(1)} %bitcast.31, bf16[384,256]{1,0:T(8,128)(2,1)S(1)} %copy-done.35, ...), custom_call_target="tpu_custom_call" | custom-call | flops 9663676416 | bytes 12582912 | tf_op jit(solution)/shard_map/mlp/pallas_call | solution.py:531
  132.3 13.7 %all_to_all.73 = bf16[4,384,256]{2,1,0:T(8,128)(2,1)S(1)} all-to-all(bf16[4,384,256]{2,1,0:T(8,128)(2,1)S(1)} %bitcast.32), channel_id=1, replica_groups=mesh['y'=4,'z'=4,'core'=2,'ch'=4] {'ch'}, dimensions={0} | all-to-all | bytes 1572864 | tf_op jit(solution)/shard_map/all_to_all | solution.py:604
  146.1 3.8 %gradient_columns.1 = bf16[512,1920]{1,0:T(8,128)(2,1)S(1)} custom-call(bf16[1536,256]{1,0:T(8,128)(2,1)S(1)} %copy-done.7, bf16[1536,256]{1,0:T(8,128)(2,1)S(1)} %bitcast.25, f32[192,9]{1,0:T(8,128)S(1)} %copy.19.taps_ref, bf16[512,256]{1,0:T(8,128)(2,1)S(1)} %copy-done.10), custom_call_target="tpu_custom_call" | custom-call | flops 503316480 | bytes 3808000 | tf_op jit(solution)/shard_map/gradient_columns/pallas_call | solution.py:109
  149.9 32.5 %all_to_all.74 = bf16[32,16,1920]{2,1,0:T(8,128)(2,1)S(1)} all-to-all(bf16[32,16,1920]{2,1,0:T(8,128)(2,1)S(1)} %bitcast.23), channel_id=1, replica_groups=mesh['y'=4,'z'=4,'core'=2,'ch'=4] {'y','z','core'}, dimensions={0} | all-to-all | bytes 3932160 | tf_op jit(solution)/shard_map/all_to_all | solution.py:604
  182.4 6.7 %rows_backward.1 = (bf16[512,1536]{1,0:T(8,128)(2,1)S(1)}, bf16[2,256,1536]{2,1,0:T(8,128)(2,1)S(1)}) custom-call(bf16[512,1920]{1,0:T(8,128)(2,1)S(1)} %bitcast.21, bf16[512,512]{1,0:T(8,128)(2,1)S(1)} %copy-done.21, bf16[512,512]{1,0:T(8,128)(2,1)S(1)} %copy-done.23, f32[32,1536]{1,0:T(8,128)S(1)} %copy-done.28, f32[32,1536]{1,0:T(8,128)S(1)} %copy-done.30, ...), custom_call_target="tpu_custom_call" | custom-call | flops 1610612736 | bytes 9699328 | tf_op jit(solution)/shard_map/rows_backward/pallas_call | solution.py:109
  191.4 4.0 %all-to-all-start.5 = ((bf16[32,16,1536]{2,1,0:T(8,128)(2,1)}), bf16[32,16,1536]{2,1,0:T(8,128)(2,1)S(1)}, u32[]{:S(2)}, u32[]{:S(2)}) async-start(bf16[32,16,1536]{2,1,0:T(8,128)(2,1)} %bitcast.30), calls=%async_computation.5 | async-start | bytes 3145728 | tf_op jit(solution)/shard_map/all_to_all | solution.py:604
  195.8 1.8 collective-permute-start.4
  198.3 1.4 copy-done.16
  200.6 3.7 %grad_filter.1 = f32[2,1536,256]{2,1,0:T(8,128)} custom-call(bf16[2,256,1536]{2,1,0:T(8,128)(2,1)S(1)} %copy-done.16, bf16[256,256]{1,0:T(8,128)(2,1)S(1)} %copy-done.25), custom_call_target="tpu_custom_call" | custom-call | bytes 1024 | tf_op jit(solution)/shard_map/grad_filter/pallas_call | solution.py:109
  204.3 2.6 %collective-permute-done.4.two_ref = bf16[384,256]{1,0:T(8,128)(2,1)S(1)} collective-permute-done((bf16[384,256]{1,0:T(8,128)(2,1)}, bf16[384,256]{1,0:T(8,128)(2,1)S(1)}, u32[]{:S(2)}, u32[]{:S(2)}) %collective-permute-start.4) | collective-permute-done | bytes 196640 | tf_op jit(solution)/shard_map/ppermute | solution.py:611
  207.7 1.3 block_out.1
  209.0 9.1 %all-to-all-done.5 = bf16[32,16,1536]{2,1,0:T(8,128)(2,1)S(1)} async-done(((bf16[32,16,1536]{2,1,0:T(8,128)(2,1)}), bf16[32,16,1536]{2,1,0:T(8,128)(2,1)S(1)}, u32[]{:S(2)}, u32[]{:S(2)}) %all-to-all-start.5) | async-done | bytes 1572896 | tf_op jit(solution)/shard_map/all_to_all | solution.py:604
  220.2 1.9 image.1
  (113 shorter events, 27.0 us)
Async XLA Ops:
  7.2 108.5 %all-gather.2.cloned.1.call-start = ((), (), s32[]{:S(2)}) async-start(), calls=%async_computation.6 | async-start | bytes 10616832 | tf_op jit(solution)/shard_map/all_gather | solution.py:659
  17.2 32.6 %copy-start.20 = (bf16[512,512]{1,0:T(8,128)(2,1)S(1)}, bf16[512,512]{1,0:T(8,128)(2,1)}, u32[]{:S(2)}) copy-start(bf16[512,512]{1,0:T(8,128)(2,1)} %constant.27.clone.refs_1_) | copy-start | bytes 1572868
  17.2 32.5 %all-to-all-start = ((bf16[32,16,1536]{2,1,0:T(8,128)(2,1)}), bf16[32,16,1536]{2,1,0:T(8,128)(2,1)}, u32[]{:S(2)}, u32[]{:S(2)}) async-start(bf16[32,16,1536]{2,1,0:T(8,128)(2,1)} %bitcast.2), calls=%async_computation | async-start | bytes 3145728 | tf_op jit(solution)/shard_map/all_to_all | solution.py:604
  27.0 8.7 %collective-permute-start = (bf16[384,256]{1,0:T(8,128)(2,1)}, bf16[384,256]{1,0:T(8,128)(2,1)S(1)}, u32[]{:S(2)}, u32[]{:S(2)}) collective-permute-start(bf16[384,256]{1,0:T(8,128)(2,1)} %get-tuple-element.125), channel_id=1, source_target_pairs={{0,1},{1,2},{2,3},{3,0},{4,5},{5,6},{6,7},{7,4},{8,9},{9,10},{10,1... | collective-permute-start | bytes 589832 | tf_op jit(solution)/shard_map/ppermute | solution.py:611
  28.3 16.0 %collective-permute-start.1 = (bf16[384,256]{1,0:T(8,128)(2,1)}, bf16[384,256]{1,0:T(8,128)(2,1)S(1)}, u32[]{:S(2)}, u32[]{:S(2)}) collective-permute-start(bf16[384,256]{1,0:T(8,128)(2,1)} %get-tuple-element.126), channel_id=1, source_target_pairs={{0,2},{1,3},{2,0},{3,1},{4,6},{5,7},{6,4},{7,5},{8,10},{9,11},{10,... | collective-permute-start | bytes 589832 | tf_op jit(solution)/shard_map/ppermute | solution.py:611
  30.8 14.2 %collective-permute-start.2 = (bf16[384,256]{1,0:T(8,128)(2,1)}, bf16[384,256]{1,0:T(8,128)(2,1)S(1)}, u32[]{:S(2)}, u32[]{:S(2)}) collective-permute-start(bf16[384,256]{1,0:T(8,128)(2,1)} %get-tuple-element.127), channel_id=1, source_target_pairs={{0,3},{1,0},{2,1},{3,2},{4,7},{5,4},{6,5},{7,6},{8,11},{9,8},{10,9... | collective-permute-start | bytes 589832 | tf_op jit(solution)/shard_map/ppermute | solution.py:611
  35.7 24.0 %copy-start.3 = (bf16[2,256,1536]{2,1,0:T(8,128)(2,1)}, bf16[2,256,1536]{2,1,0:T(8,128)(2,1)S(1)}, u32[]{:S(2)}) copy-start(bf16[2,256,1536]{2,1,0:T(8,128)(2,1)S(1)} %filter.1.refs_5_) | copy-start | bytes 4718596
  59.7 32.1 %copy-start.13 = (bf16[2,256,1536]{2,1,0:T(8,128)(2,1)}, bf16[2,256,1536]{2,1,0:T(8,128)(2,1)S(1)}, u32[]{:S(2)}) copy-start(bf16[2,256,1536]{2,1,0:T(8,128)(2,1)S(1)} %get-tuple-element.229.refs_6_) | copy-start | bytes 4718596
  59.7 32.1 %copy-start.46 = (f32[192,9]{0,1:T(8,128)S(1)}, f32[192,9]{0,1:T(8,128)}, u32[]{:S(2)}) copy-start(f32[192,9]{0,1:T(8,128)} %param.16) | copy-start | bytes 20740
  59.7 33.6 %copy-start.10 = (bf16[512,256]{1,0:T(8,128)(2,1)S(1)}, bf16[512,256]{1,0:T(8,128)(2,1)}, u32[]{:S(2)}) copy-start(bf16[512,256]{1,0:T(8,128)(2,1)} %constant.31.clone.table_ref) | copy-start | bytes 786436
  98.7 17.0 %copy-start.35 = (bf16[384,256]{1,0:T(8,128)(2,1)S(1)}, bf16[384,256]{1,0:T(8,128)(2,1)}, u32[]{:S(2)}) copy-start(bf16[384,256]{1,0:T(8,128)(2,1)} %copy-done.34) | copy-start | bytes 589828
  98.7 17.0 %copy-start.38 = (bf16[384,256]{1,0:T(8,128)(2,1)S(1)}, bf16[384,256]{1,0:T(8,128)(2,1)}, u32[]{:S(2)}) copy-start(bf16[384,256]{1,0:T(8,128)(2,1)} %copy-done.37) | copy-start | bytes 589828
  98.7 17.0 %copy-start.41 = (bf16[384,256]{1,0:T(8,128)(2,1)S(1)}, bf16[384,256]{1,0:T(8,128)(2,1)}, u32[]{:S(2)}) copy-start(bf16[384,256]{1,0:T(8,128)(2,1)} %copy-done.40) | copy-start | bytes 589828
  98.7 17.0 %copy-start.44 = (bf16[384,256]{1,0:T(8,128)(2,1)S(1)}, bf16[384,256]{1,0:T(8,128)(2,1)}, u32[]{:S(2)}) copy-start(bf16[384,256]{1,0:T(8,128)(2,1)} %copy-done.43) | copy-start | bytes 589828
  146.1 36.3 %copy-start.23 = (bf16[512,512]{1,0:T(8,128)(2,1)S(1)}, bf16[512,512]{1,0:T(8,128)(2,1)}, u32[]{:S(2)}) copy-start(bf16[512,512]{1,0:T(8,128)(2,1)} %constant.28.clone.refs_2_) | copy-start | bytes 1572868
  146.1 36.3 %copy-start.30 = (f32[32,1536]{1,0:T(8,128)S(1)}, f32[32,1536]{1,0:T(8,128)}, u32[]{:S(2)}) copy-start(f32[32,1536]{1,0:T(8,128)} %constant.30.clone.refs_4_) | copy-start | bytes 589828
  149.9 32.5 %copy-start.4 = (bf16[2,256,1536]{2,1,0:T(8,128)(2,1)S(1)}, bf16[2,256,1536]{2,1,0:T(8,128)(2,1)}, u32[]{:S(2)}) copy-start(bf16[2,256,1536]{2,1,0:T(8,128)(2,1)} %copy-done.3) | copy-start | bytes 4718596
  149.9 32.5 %copy-start.14 = (bf16[2,256,1536]{2,1,0:T(8,128)(2,1)S(1)}, bf16[2,256,1536]{2,1,0:T(8,128)(2,1)}, u32[]{:S(2)}) copy-start(bf16[2,256,1536]{2,1,0:T(8,128)(2,1)} %copy-done.13) | copy-start | bytes 4718596
  149.9 32.5 %copy-start.21 = (bf16[512,512]{1,0:T(8,128)(2,1)S(1)}, bf16[512,512]{1,0:T(8,128)(2,1)}, u32[]{:S(2)}) copy-start(bf16[512,512]{1,0:T(8,128)(2,1)} %constant.27.clone.refs_1_) | copy-start | bytes 1572868
  149.9 32.5 %copy-start.28 = (f32[32,1536]{1,0:T(8,128)S(1)}, f32[32,1536]{1,0:T(8,128)}, u32[]{:S(2)}) copy-start(f32[32,1536]{1,0:T(8,128)} %constant.29.clone.refs_3_) | copy-start | bytes 589828
  191.4 26.7 %all-to-all-start.5 = ((bf16[32,16,1536]{2,1,0:T(8,128)(2,1)}), bf16[32,16,1536]{2,1,0:T(8,128)(2,1)S(1)}, u32[]{:S(2)}, u32[]{:S(2)}) async-start(bf16[32,16,1536]{2,1,0:T(8,128)(2,1)} %bitcast.30), calls=%async_computation.5 | async-start | bytes 3145728 | tf_op jit(solution)/shard_map/all_to_all | solution.py:604
  195.4 8.8 %collective-permute-start.3 = (bf16[384,256]{1,0:T(8,128)(2,1)}, bf16[384,256]{1,0:T(8,128)(2,1)S(1)}, u32[]{:S(2)}, u32[]{:S(2)}) collective-permute-start(bf16[384,256]{1,0:T(8,128)(2,1)} %copy-done.42), channel_id=1, source_target_pairs={{0,1},{1,2},{2,3},{3,0},{4,5},{5,6},{6,7},{7,4},{8,9},{9,10},{10,1... | collective-permute-start | bytes 589832 | tf_op jit(solution)/shard_map/ppermute | solution.py:611
  195.8 11.1 %collective-permute-start.4 = (bf16[384,256]{1,0:T(8,128)(2,1)}, bf16[384,256]{1,0:T(8,128)(2,1)S(1)}, u32[]{:S(2)}, u32[]{:S(2)}) collective-permute-start(bf16[384,256]{1,0:T(8,128)(2,1)} %copy-done.39), channel_id=1, source_target_pairs={{0,2},{1,3},{2,0},{3,1},{4,6},{5,7},{6,4},{7,5},{8,10},{9,11},{10,... | collective-permute-start | bytes 589832 | tf_op jit(solution)/shard_map/ppermute | solution.py:611
  197.6 10.1 %collective-permute-start.5 = (bf16[384,256]{1,0:T(8,128)(2,1)}, bf16[384,256]{1,0:T(8,128)(2,1)S(1)}, u32[]{:S(2)}, u32[]{:S(2)}) collective-permute-start(bf16[384,256]{1,0:T(8,128)(2,1)} %copy-done.36), channel_id=1, source_target_pairs={{0,3},{1,0},{2,1},{3,2},{4,7},{5,4},{6,5},{7,6},{8,11},{9,8},{10,9... | collective-permute-start | bytes 589832 | tf_op jit(solution)/shard_map/ppermute | solution.py:611
  (33 other events, 155.9 us)
Sparse Core Ops, SparseCore 0:
  17.3 62.6 all-gather.1

commit v5 on v2

--- a/solution.py
+++ b/solution.py
@@ -121,7 +121,7 @@
     return pl.BlockSpec(dims, lambda *_: (0,) * len(dims), pipeline_mode=pl.Buffered(1))
 
 
-def kernel_call(body, name, outs, scratch, operands, vmem, flops=0, smem=0, hint=0):
+def kernel_call(body, name, outs, scratch, operands, vmem, flops=0, smem=0, beside=False, hint=0):
     scalar = pl.BlockSpec(memory_space=pltpu.SMEM)
     moved = sum(a.size * a.dtype.itemsize for a in operands)
     moved += sum(o.size * np.dtype(o.dtype).itemsize for o in outs)
@@ -134,7 +134,9 @@
         out_specs=tuple(whole_block(o.shape) for o in outs),
         scratch_shapes=scratch,
         cost_estimate=pl.CostEstimate(
-            flops=flops + hint * 10**9, bytes_accessed=moved, transcendentals=0
+            flops=0 if beside else flops + hint * 10**9,
+            bytes_accessed=1024 if beside else moved,
+            transcendentals=0,
         ),
         compiler_params=pltpu.CompilerParams(vmem_limit_bytes=vmem * MIB),
     )(*operands)
@@ -663,7 +665,7 @@
             bytes_accessed=4 * UNITS * ALL_CH + 8 * LANES * LEN,
             transcendentals=2 * tokens * UNITS,
         ),
-        compiler_params=pltpu.CompilerParams(vmem_limit_bytes=28 * MIB),
+        compiler_params=pltpu.CompilerParams(vmem_limit_bytes=48 * MIB),
     )(channel, hidden, *dy_parts, gain, jnp.asarray(UNIT), weights, weights)
 
 
@@ -736,6 +738,11 @@
     return lax.optimization_barrier((value, earlier))
 
 
+def fenced(values, axis, live):
+    values, live = lax.optimization_barrier((values, live))
+    return lax.optimization_barrier((to_peers(values, axis), live))
+
+
 def on_device(tile_image, spectral_filter, conv_taps, norm_gain, up_weight, down_weight, upstream):
     device = lax.axis_index(ROWS)
     place = device.reshape(1).astype(jnp.int32)
@@ -758,25 +765,18 @@
     lone_in = [(i, ROWS_DEVICES - i) for i in range(1, 16)] + [(0, 16)]
     pair_filter = lax.ppermute(tail, ROWS, opposite)
     lone_filter = lax.ppermute(lone, ROWS, lone_in)
+    image_rows, _ = after(tile_image.reshape(flat), (tail, lone))
     message, signal = kernel_call(
         columns_kernel,
         "columns",
         [shape((LEN, LANES), BF16), shape(flat, BF16)],
         [wide, pltpu.VMEM(flat, BF16)],
-        [tile_image.reshape(flat), forward_columns],
+        [image_rows, forward_columns],
         16,
         2 * LEN * LEN * LANES,
     )
     received = to_peers(message, ROWS)
-
-    (up_own, down_own, upstream_rows), _ = after(
-        (up_weight, down_weight, upstream.reshape(flat)), message
-    )
-    start = lax.axis_index("core") * HALF_UNITS
-    own_up = lax.dynamic_slice_in_dim(up_own, start, HALF_UNITS, axis=1).T
-    own_down = lax.dynamic_slice_in_dim(down_own, start, HALF_UNITS, axis=0)
-    pack = jnp.concatenate([own_up, own_down], axis=1)
-    weights = lax.all_gather(pack, ("core", "ch"), axis=0, tiled=True)
+    upstream_rows, _ = after(upstream.reshape(flat), message)
     dy, *dy_turned = kernel_call(
         unfold_kernel,
         "unfold",
@@ -787,6 +787,13 @@
         smem=1,
         hint=6,
     )
+
+    (up_here, down_here), _ = after((up_weight, down_weight), dy_turned)
+    start = lax.axis_index("core") * HALF_UNITS
+    own_up = lax.dynamic_slice_in_dim(up_here, start, HALF_UNITS, axis=1).T
+    own_down = lax.dynamic_slice_in_dim(down_here, start, HALF_UNITS, axis=0)
+    pack = jnp.concatenate([own_up, own_down], axis=1)
+    weights = lax.all_gather(pack, ("core", "ch"), axis=0, tiled=True)
     dy_parts = turned_exchange(dy_turned)
     main, cross = kernel_call(
         filter_kernel,
@@ -799,7 +806,6 @@
         smem=1,
         hint=6,
     )
-    received, dy_parts = after(received, dy_parts)
 
     row_scratch = [pltpu.VMEM((320, LANES), F32), pltpu.VMEM((LEN, LANES), BF16)]
     message, seen = kernel_call(
@@ -812,7 +818,8 @@
         2 * 576 * LEN * LANES,
         smem=1,
     )
-    received = to_peers(message, ROWS)
+    received, live = fenced(message, ROWS, (seen, main, cross, signal, dy))
+    seen, main, cross, signal, dy = live
     (hidden,) = kernel_call(
         hidden_kernel,
         "hidden",
@@ -822,11 +829,14 @@
         16,
         2 * LEN * LEN * SENT,
     )
-    hidden_tokens = to_peers(hidden, "ch")
+    hidden_tokens, live = fenced(hidden, "ch", (seen, main, cross, dy, hidden))
+    seen, main, cross, dy, hidden = live
     *out_turned, grad_message = mlp(
         channel, hidden_tokens, dy_parts, norm_gain.reshape(1, ALL_CH), weights
     )
-    grad_mlp = to_peers(grad_message, "ch")
+    live = (seen, main, cross, dy, out_turned, hidden)
+    grad_mlp, live = fenced(grad_message, "ch", live)
+    seen, main, cross, dy, out_turned, hidden = live
     (message,) = kernel_call(
         gradient_columns_kernel,
         "gradient_columns",
@@ -836,12 +846,9 @@
         16,
         2 * LEN * LEN * SENT,
     )
-    out_turned, message = after(out_turned, message)
-    received = to_peers(message, ROWS)
-    out_parts = turned_exchange(out_turned)
-    (block_out,) = kernel_call(
-        block_out_kernel, "block_out", [shape(flat, BF16)], [wide], [channel, hidden, *out_parts], 16, smem=1
-    )
+    live = (seen, main, cross, dy, out_turned, grad_mlp, hidden)
+    received, live = fenced(message, ROWS, live)
+    seen, main, cross, dy, out_turned, grad_mlp, hidden = live
     message, products = kernel_call(
         rows_backward_kernel,
         "rows_backward",
@@ -852,6 +859,9 @@
         2 * 576 * LEN * LANES,
         smem=1,
     )
+    (dy, out_turned, grad_mlp, hidden), (message, products) = after(
+        (dy, out_turned, grad_mlp, hidden), (message, products)
+    )
     received = to_peers(message, ROWS)
     own, pair, lone = kernel_call(
         unturn_kernel,
@@ -861,7 +871,18 @@
         [products, straight, mirrored],
         16,
         2 * 18 * LEN * LEN * CH,
-        hint=12,
+        beside=True,
+    )
+    out_parts = turned_exchange(out_turned)
+    (block_out,) = kernel_call(
+        block_out_kernel,
+        "block_out",
+        [shape(flat, BF16)],
+        [wide],
+        [channel, hidden, *out_parts],
+        16,
+        smem=1,
+        beside=True,
     )
     pair = lax.ppermute(pair, ROWS, opposite)
     lone = lax.ppermute(lone, ROWS, [(b, a) for a, b in lone_in])

time: 236 us -> 245 us (1.038)
  waiting for transfers between devices: 58.4 us -> 72.6 us
  local copies, waits for them, and re-layouts: 31.8 us -> 28.5 us
    ppermute x1, waiting for transfers between devices: 1.58 us -> 21.9 us  [on_device(): lone_filter = lax.ppermute(lone, ROWS, lone_in)]
    all_to_all x4, waiting for transfers between devices: 38.2 us -> 33.2 us  [to_peers(): return lax.all_to_all(values, axis, split_axis=0, concat_axis=0, tiled=True)]
    ppermute x1, starting transfers between devices: 6.5 us -> 2.04 us  [on_device(): lone_filter = lax.ppermute(lone, ROWS, lone_in)]
    unnamed x111 -> x105, local copies, waits for them, and re-layouts: 30.1 us -> 26.8 us
  transfers between devices with their start and end apart: 15 -> 15, of which waited for: 10 -> 10; matrix products, arithmetic and copies ran while one was open for 0% -> 0% of each run, Pallas kernels for 7% -> 6%
where the time goes in v5:
time: 245 us; the launch traced here: 244 us
  waiting for transfers between devices  72.6 us (30%)
  Pallas kernels  48.5 us (20%)
  starting transfers between devices  43.1 us (18%)
  blocking collectives  35.5 us (14%)
  local copies, waits for them, and re-layouts  28.5 us (12%)
  between operations  14.4 us (6%)
    all_to_all x2, blocking collectives, to_peers(): return lax.all_to_all(values, axis, split_axis=0, concat_axis=0, tiled=True)  35.5 us
    all_to_all x4, waiting for transfers between devices, to_peers(): return lax.all_to_all(values, axis, split_axis=0, concat_axis=0, tiled=True)  33.2 us
    pallas_call x12, Pallas kernels, kernel_call(): pl.pallas_call(body, name=name, grid=(1,), out_shape=tuple(outs), in_spec...  31.1 us
    unnamed x105, local copies, waits for them, and re-layouts  26.8 us
    all_to_all x4, starting transfers between devices, to_peers(): return lax.all_to_all(values, axis, split_axis=0, concat_axis=0, tiled=True)  22.2 us
    ppermute x1, waiting for transfers between devices, on_device(): lone_filter = lax.ppermute(lone, ROWS, lone_in)  21.9 us
    pallas_call x1, Pallas kernels, mlp(): pl.pallas_call(mlp_kernel, name='mlp', grid=(steps,), out_shape=(*(shape(...  17.4 us
    ppermute x6, waiting for transfers between devices, turned_exchange(): received.append(lax.ppermute(parts[turn], 'ch', pairs))  16.7 us
  transfers between devices with their start and end apart: 15, of which 10 were waited for; matrix products, arithmetic and copies ran while one was open for 0% of the time, Pallas kernels for 6%

profile of v5, /device:TPU:1, one launch (start us, length us, event | category | flops | bytes accessed | tf_op | source)
XLA Modules:
  0.0 243.6 jit_solution(2206259146674458396)
XLA Ops:
  19.8 7.7 %collective-permute-start = (bf16[4,2,192,256]{3,2,1,0:T(8,128)(2,1)S(1)}, bf16[4,2,192,256]{3,2,1,0:T(8,128)(2,1)S(1)}, u32[]{:S(2)}, u32[]{:S(2)}) collective-permute-start(bf16[4,2,192,256]{3,2,1,0:T(8,128)(2,1)S(1)} %get-tuple-element.106.tail_ref), channel_id=1, source_target_pairs={{0,124},{4,120},{8,116},{12,112},{16,108},{20,104},{24,100},{28,96... | collective-permute-start | bytes 2359304 | tf_op jit(solution)/shard_map/ppermute | solution.py:766
  30.4 4.7 %all-to-all-start = ((bf16[32,8,1536]{2,1,0:T(8,128)(2,1)}), bf16[32,8,1536]{2,1,0:T(8,128)(2,1)S(1)}, u32[]{:S(2)}, u32[]{:S(2)}) async-start(bf16[32,8,1536]{2,1,0:T(8,128)(2,1)} %bitcast.4), calls=%async_computation | async-start | bytes 1572864 | tf_op jit(solution)/shard_map/all_to_all | solution.py:726
  35.1 21.9 %collective-permute-done.1.lone_ref = bf16[2,192,256]{2,1,0:T(8,128)(2,1)} collective-permute-done((bf16[2,192,256]{2,1,0:T(8,128)(2,1)}, bf16[2,192,256]{2,1,0:T(8,128)(2,1)}, u32[]{:S(2)}, u32[]{:S(2)}) %collective-permute-start.1) | collective-permute-done | bytes 196640 | tf_op jit(solution)/shard_map/ppermute | solution.py:767
  70.6 2.7 %rows_forward.1 = (bf16[256,1920]{1,0:T(8,128)(2,1)S(1)}, bf16[2,160,1536]{2,1,0:T(8,128)(2,1)S(1)}) custom-call(s32[1]{0:T(128)} %bitcast.1.place_ref.refs_0_, bf16[256,1536]{1,0:T(8,128)(2,1)S(1)} %bitcast.27, bf16[320,256]{1,0:T(8,128)(2,1)S(1)} %copy-done.23, bf16[256,256]{1,0:T(8,128)(2,1)S(1)} %copy-done.27, f32[32,1536]{1,0:T(8,128)S(1)} %copy-done.15, ...), custom_call_target="tpu_custom_call" | custom-call | flops 452984832 | bytes 5406724 | tf_op jit(solution)/shard_map/rows_forward/pallas_call | solution.py:128
  75.2 8.3 %all-to-all-start.1 = ((bf16[32,8,1920]{2,1,0:T(8,128)(2,1)}), bf16[32,8,1920]{2,1,0:T(8,128)(2,1)}, u32[]{:S(2)}, u32[]{:S(2)}) async-start(bf16[32,8,1920]{2,1,0:T(8,128)(2,1)} %bitcast.29), calls=%async_computation.1 | async-start | bytes 1966080 | tf_op jit(solution)/shard_map/all_to_all | solution.py:726
  83.7 16.1 %all-to-all-done.1 = bf16[32,8,1920]{2,1,0:T(8,128)(2,1)} async-done(((bf16[32,8,1920]{2,1,0:T(8,128)(2,1)}), bf16[32,8,1920]{2,1,0:T(8,128)(2,1)}, u32[]{:S(2)}, u32[]{:S(2)}) %all-to-all-start.1) | async-done | bytes 983072 | tf_op jit(solution)/shard_map/all_to_all | solution.py:726
  100.9 5.3 %hidden.1.hidden_ref = bf16[1536,256]{1,0:T(8,128)(2,1)} custom-call(bf16[256,1920]{1,0:T(8,128)(2,1)} %bitcast.8.received_ref, bf16[256,256]{1,0:T(8,128)(2,1)S(1)} %copy-done.25, f32[192,9]{1,0:T(8,128)S(1)} %copy.19.taps_ref, bf16[1536,256]{1,0:T(8,128)(2,1)S(1)} %copy-done.22), custom_call_target="tpu_custom_call" | custom-call | flops 251658240 | bytes 2693888 | tf_op jit(solution)/shard_map/hidden/pallas_call | solution.py:128
  106.2 4.2 %all-to-all-start.2 = ((bf16[4,384,256]{2,1,0:T(8,128)(2,1)}), bf16[4,384,256]{2,1,0:T(8,128)(2,1)S(1)}, u32[]{:S(2)}, u32[]{:S(2)}) async-start(bf16[4,384,256]{2,1,0:T(8,128)(2,1)} %bitcast.9), calls=%async_computation.2 | async-start | bytes 1572864 | tf_op jit(solution)/shard_map/all_to_all | solution.py:726
  111.8 2.4 collective-permute-start.3
  115.4 7.0 %all-to-all-done.2 = bf16[4,384,256]{2,1,0:T(8,128)(2,1)S(1)} async-done(((bf16[4,384,256]{2,1,0:T(8,128)(2,1)}), bf16[4,384,256]{2,1,0:T(8,128)(2,1)S(1)}, u32[]{:S(2)}, u32[]{:S(2)}) %all-to-all-start.2) | async-done | bytes 786464 | tf_op jit(solution)/shard_map/all_to_all | solution.py:726
  122.4 4.0 %collective-permute-done.2.dy_one_ref = bf16[384,256]{1,0:T(8,128)(2,1)} collective-permute-done((bf16[384,256]{1,0:T(8,128)(2,1)}, bf16[384,256]{1,0:T(8,128)(2,1)}, u32[]{:S(2)}, u32[]{:S(2)}) %collective-permute-start.2) | collective-permute-done | bytes 196640 | tf_op jit(solution)/shard_map/ppermute | solution.py:733
  126.4 4.6 %collective-permute-done.3.dy_two_ref = bf16[384,256]{1,0:T(8,128)(2,1)} collective-permute-done((bf16[384,256]{1,0:T(8,128)(2,1)}, bf16[384,256]{1,0:T(8,128)(2,1)}, u32[]{:S(2)}, u32[]{:S(2)}) %collective-permute-start.3) | collective-permute-done | bytes 196640 | tf_op jit(solution)/shard_map/ppermute | solution.py:733
  132.8 17.4 %mlp.1 = (bf16[384,256]{1,0:T(8,128)(2,1)S(1)}, bf16[384,256]{1,0:T(8,128)(2,1)}, bf16[384,256]{1,0:T(8,128)(2,1)}, bf16[384,256]{1,0:T(8,128)(2,1)}, bf16[1536,256]{1,0:T(8,128)(2,1)S(1)}) custom-call(s32[1]{0:T(128)} %bitcast.channel_ref, bf16[1536,256]{1,0:T(8,128)(2,1)S(1)} %bitcast.32, bf16[384,256]{1,0:T(8,128)(2,1)S(1)} %copy-done.49, ...), custom_call_target="tpu_custom_call" | custom-call | flops 9663676416 | bytes 12582912 | tf_op jit(solution)/shard_map/mlp/pallas_call | solution.py:635
  150.2 13.3 %all_to_all.70 = bf16[4,384,256]{2,1,0:T(8,128)(2,1)S(1)} all-to-all(bf16[4,384,256]{2,1,0:T(8,128)(2,1)S(1)} %bitcast.33), channel_id=1, replica_groups=mesh['y'=4,'z'=4,'core'=2,'ch'=4] {'ch'}, dimensions={0} | all-to-all | bytes 1572864 | tf_op jit(solution)/shard_map/all_to_all | solution.py:726
  163.5 3.4 %gradient_columns.1 = bf16[256,1920]{1,0:T(8,128)(2,1)S(1)} custom-call(bf16[1536,256]{1,0:T(8,128)(2,1)S(1)} %copy-done.3, bf16[1536,256]{1,0:T(8,128)(2,1)S(1)} %bitcast.22, f32[192,9]{1,0:T(8,128)S(1)} %copy-done.12, bf16[256,256]{1,0:T(8,128)(2,1)S(1)} %copy-done.30), custom_call_target="tpu_custom_call" | custom-call | flops 251658240 | bytes 2693888 | tf_op jit(solution)/shard_map/gradient_columns/pallas_call | solution.py:128
  167.0 22.2 %all_to_all.71 = bf16[32,8,1920]{2,1,0:T(8,128)(2,1)S(1)} all-to-all(bf16[32,8,1920]{2,1,0:T(8,128)(2,1)S(1)} %bitcast.25), channel_id=1, replica_groups=mesh['y'=4,'z'=4,'core'=2,'ch'=4] {'y','z','core'}, dimensions={0} | all-to-all | bytes 1966080 | tf_op jit(solution)/shard_map/all_to_all | solution.py:726
  189.3 3.3 %rows_backward.1 = (bf16[256,1536]{1,0:T(8,128)(2,1)S(1)}, bf16[2,160,1536]{2,1,0:T(8,128)(2,1)S(1)}) custom-call(s32[1]{0:T(128)} %bitcast.1.place_ref.refs_0_, bf16[256,1920]{1,0:T(8,128)(2,1)S(1)} %bitcast.24, bf16[320,256]{1,0:T(8,128)(2,1)S(1)} %copy-done.24, bf16[256,256]{1,0:T(8,128)(2,1)S(1)} %copy-done.28, f32[32,1536]{1,0:T(8,128)S(1)} %copy-done.16, ...), custom_call_target="tpu_custom_call" | custom-call | flops 452984832 | bytes 6389764 | tf_op jit(solution)/shard_map/rows_backward/pallas_call | solution.py:128
  192.6 2.4 unturn.1
  198.5 5.0 %all-to-all-start.5 = ((bf16[32,8,1536]{2,1,0:T(8,128)(2,1)}), bf16[32,8,1536]{2,1,0:T(8,128)(2,1)S(1)}, u32[]{:S(2)}, u32[]{:S(2)}) async-start(bf16[32,8,1536]{2,1,0:T(8,128)(2,1)} %bitcast.31), calls=%async_computation.5 | async-start | bytes 1572864 | tf_op jit(solution)/shard_map/all_to_all | solution.py:726
  207.8 4.2 %collective-permute-done.5.one_ref = bf16[384,256]{1,0:T(8,128)(2,1)S(1)} collective-permute-done((bf16[384,256]{1,0:T(8,128)(2,1)}, bf16[384,256]{1,0:T(8,128)(2,1)S(1)}, u32[]{:S(2)}, u32[]{:S(2)}) %collective-permute-start.5) | collective-permute-done | bytes 196640 | tf_op jit(solution)/shard_map/ppermute | solution.py:733
  212.0 3.0 %collective-permute-done.6.two_ref = bf16[384,256]{1,0:T(8,128)(2,1)S(1)} collective-permute-done((bf16[384,256]{1,0:T(8,128)(2,1)}, bf16[384,256]{1,0:T(8,128)(2,1)S(1)}, u32[]{:S(2)}, u32[]{:S(2)}) %collective-permute-start.6) | collective-permute-done | bytes 196640 | tf_op jit(solution)/shard_map/ppermute | solution.py:733
  216.9 2.4 %block_out.1 = bf16[1536,256]{1,0:T(8,128)(2,1)} custom-call(s32[1]{0:T(128)} %bitcast.channel_ref, bf16[1536,256]{1,0:T(8,128)(2,1)} %hidden.1.hidden_ref, bf16[384,256]{1,0:T(8,128)(2,1)S(1)} %copy-done.32, bf16[384,256]{1,0:T(8,128)(2,1)S(1)} %collective-permute-done.5.one_ref, bf16[384,256]{1,0:T(8,128)(2,1)S(1)} %collective-permute-done.6.two_ref, ...), custom_call_target="tpu_custom_call" | custom-call | bytes 1024 | tf_op jit(solution)/shard_map/block_out/pallas_call | solution.py:128
  219.3 10.1 %all-to-all-done.5 = bf16[32,8,1536]{2,1,0:T(8,128)(2,1)S(1)} async-done(((bf16[32,8,1536]{2,1,0:T(8,128)(2,1)}), bf16[32,8,1536]{2,1,0:T(8,128)(2,1)S(1)}, u32[]{:S(2)}, u32[]{:S(2)}) %all-to-all-start.5) | async-done | bytes 786464 | tf_op jit(solution)/shard_map/all_to_all | solution.py:726
  232.8 3.9 %grad_filter.1 = f32[2,1536,256]{2,1,0:T(8,128)} custom-call(s32[1]{0:T(128)} %bitcast.1.place_ref.refs_0_, bf16[4,2,192,256]{3,2,1,0:T(8,128)(2,1)S(1)} %copy-done.18, bf16[4,2,192,256]{3,2,1,0:T(8,128)(2,1)} %collective-permute-done.8.pair_ref, bf16[2,192,256]{2,1,0:T(8,128)(2,1)} %collective-permute-done.9.lone_ref), custom_call_target="tpu_custom_call" | custom-call | bytes 4915204 | tf_op jit(solution)/shard_map/grad_filter/pallas_call | solution.py:128
  (132 shorter events, 49.6 us)
Async XLA Ops:
  7.2 123.7 %all-gather.2.cloned.1.call-start = ((), (), s32[]{:S(2)}) async-start(), calls=%async_computation.6 | async-start | bytes 10616832 | tf_op jit(solution)/shard_map/all_gather | solution.py:796
  19.8 37.3 %collective-permute-start = (bf16[4,2,192,256]{3,2,1,0:T(8,128)(2,1)S(1)}, bf16[4,2,192,256]{3,2,1,0:T(8,128)(2,1)S(1)}, u32[]{:S(2)}, u32[]{:S(2)}) collective-permute-start(bf16[4,2,192,256]{3,2,1,0:T(8,128)(2,1)S(1)} %get-tuple-element.106.tail_ref), channel_id=1, source_target_pairs={{0,124},{4,120},{8,116},{12,112},{16,108},{20,104},{24,100},{28,96... | collective-permute-start | bytes 2359304 | tf_op jit(solution)/shard_map/ppermute | solution.py:766
  28.3 28.7 %collective-permute-start.1 = (bf16[2,192,256]{2,1,0:T(8,128)(2,1)}, bf16[2,192,256]{2,1,0:T(8,128)(2,1)}, u32[]{:S(2)}, u32[]{:S(2)}) collective-permute-start(bf16[2,192,256]{2,1,0:T(8,128)(2,1)} %get-tuple-element.107), channel_id=1, source_target_pairs={{4,124},{8,120},{12,116},{16,112},{20,108},{24,104},{28,100},{32,9... | collective-permute-start | bytes 589832 | tf_op jit(solution)/shard_map/ppermute | solution.py:767
  30.4 35.6 %all-to-all-start = ((bf16[32,8,1536]{2,1,0:T(8,128)(2,1)}), bf16[32,8,1536]{2,1,0:T(8,128)(2,1)S(1)}, u32[]{:S(2)}, u32[]{:S(2)}) async-start(bf16[32,8,1536]{2,1,0:T(8,128)(2,1)} %bitcast.4), calls=%async_computation | async-start | bytes 1572864 | tf_op jit(solution)/shard_map/all_to_all | solution.py:726
  75.2 24.6 %copy-start.25 = (bf16[256,256]{1,0:T(8,128)(2,1)S(1)}, bf16[256,256]{1,0:T(8,128)(2,1)}, u32[]{:S(2)}) copy-start(bf16[256,256]{1,0:T(8,128)(2,1)} %constant.47.clone.table_ref) | copy-start | bytes 393220
  75.2 24.6 %all-to-all-start.1 = ((bf16[32,8,1920]{2,1,0:T(8,128)(2,1)}), bf16[32,8,1920]{2,1,0:T(8,128)(2,1)}, u32[]{:S(2)}, u32[]{:S(2)}) async-start(bf16[32,8,1920]{2,1,0:T(8,128)(2,1)} %bitcast.29), calls=%async_computation.1 | async-start | bytes 1966080 | tf_op jit(solution)/shard_map/all_to_all | solution.py:726
  83.7 22.5 %copy-start.11 = (f32[192,9]{1,0:T(8,128)}, f32[192,9]{1,0:T(8,128)S(1)}, u32[]{:S(2)}) copy-start(f32[192,9]{1,0:T(8,128)S(1)} %copy.19.taps_ref) | copy-start | bytes 20740
  106.2 16.2 %all-to-all-start.2 = ((bf16[4,384,256]{2,1,0:T(8,128)(2,1)}), bf16[4,384,256]{2,1,0:T(8,128)(2,1)S(1)}, u32[]{:S(2)}, u32[]{:S(2)}) async-start(bf16[4,384,256]{2,1,0:T(8,128)(2,1)} %bitcast.9), calls=%async_computation.2 | async-start | bytes 1572864 | tf_op jit(solution)/shard_map/all_to_all | solution.py:726
  110.4 16.0 %collective-permute-start.2 = (bf16[384,256]{1,0:T(8,128)(2,1)}, bf16[384,256]{1,0:T(8,128)(2,1)}, u32[]{:S(2)}, u32[]{:S(2)}) collective-permute-start(bf16[384,256]{1,0:T(8,128)(2,1)} %copy-done.46), channel_id=1, source_target_pairs={{0,1},{1,2},{2,3},{3,0},{4,5},{5,6},{6,7},{7,4},{8,9},{9,10},{10,1... | collective-permute-start | bytes 589832 | tf_op jit(solution)/shard_map/ppermute | solution.py:733
  111.8 19.1 %collective-permute-start.3 = (bf16[384,256]{1,0:T(8,128)(2,1)}, bf16[384,256]{1,0:T(8,128)(2,1)}, u32[]{:S(2)}, u32[]{:S(2)}) collective-permute-start(bf16[384,256]{1,0:T(8,128)(2,1)} %copy-done.45), channel_id=1, source_target_pairs={{0,2},{1,3},{2,0},{3,1},{4,6},{5,7},{6,4},{7,5},{8,10},{9,11},{10,... | collective-permute-start | bytes 589832 | tf_op jit(solution)/shard_map/ppermute | solution.py:733
  114.2 16.7 %collective-permute-start.4 = (bf16[384,256]{1,0:T(8,128)(2,1)}, bf16[384,256]{1,0:T(8,128)(2,1)}, u32[]{:S(2)}, u32[]{:S(2)}) collective-permute-start(bf16[384,256]{1,0:T(8,128)(2,1)} %copy-done.44), channel_id=1, source_target_pairs={{0,3},{1,0},{2,1},{3,2},{4,7},{5,4},{6,5},{7,6},{8,11},{9,8},{10,9... | collective-permute-start | bytes 589832 | tf_op jit(solution)/shard_map/ppermute | solution.py:733
  163.5 25.7 %copy-start.28 = (bf16[256,256]{1,0:T(8,128)(2,1)S(1)}, bf16[256,256]{1,0:T(8,128)(2,1)}, u32[]{:S(2)}) copy-start(bf16[256,256]{1,0:T(8,128)(2,1)} %constant.43.clone.refs_3_) | copy-start | bytes 393220
  167.0 22.2 %copy-start.7 = (f32[2,32,1536]{2,1,0:T(8,128)S(1)}, f32[2,32,1536]{2,1,0:T(8,128)}, u32[]{:S(2)}) copy-start(f32[2,32,1536]{2,1,0:T(8,128)} %copy-done.5) | copy-start | bytes 1179652
  167.0 22.2 %copy-start.9 = (bf16[2,160,1536]{2,1,0:T(8,128)(2,1)S(1)}, bf16[2,160,1536]{2,1,0:T(8,128)(2,1)}, u32[]{:S(2)}) copy-start(bf16[2,160,1536]{2,1,0:T(8,128)(2,1)} %copy-done.8) | copy-start | bytes 2949124
  167.0 22.2 %copy-start.14 = (f32[32,1536]{1,0:T(8,128)S(1)}, f32[32,1536]{1,0:T(8,128)}, u32[]{:S(2)}) copy-start(f32[32,1536]{1,0:T(8,128)} %constant.45.clone.refs_5_) | copy-start | bytes 589828
  167.0 22.2 %copy-start.16 = (f32[32,1536]{1,0:T(8,128)S(1)}, f32[32,1536]{1,0:T(8,128)}, u32[]{:S(2)}) copy-start(f32[32,1536]{1,0:T(8,128)} %constant.44.clone.refs_4_) | copy-start | bytes 589828
  167.0 22.2 %copy-start.24 = (bf16[320,256]{1,0:T(8,128)(2,1)S(1)}, bf16[320,256]{1,0:T(8,128)(2,1)}, u32[]{:S(2)}) copy-start(bf16[320,256]{1,0:T(8,128)(2,1)} %constant.42.clone.refs_2_) | copy-start | bytes 491524
  196.6 36.2 %collective-permute-start.8 = (bf16[4,2,192,256]{3,2,1,0:T(8,128)(2,1)}, bf16[4,2,192,256]{3,2,1,0:T(8,128)(2,1)}, u32[]{:S(2)}, u32[]{:S(2)}) collective-permute-start(bf16[4,2,192,256]{3,2,1,0:T(8,128)(2,1)} %get-tuple-element.207), channel_id=1, source_target_pairs={{0,124},{4,120},{8,116},{12,112},{16,108},{20,104},{24,100},{28,96... | collective-permute-start | bytes 2359304 | tf_op jit(solution)/shard_map/ppermute | solution.py:887
  198.5 30.9 %all-to-all-start.5 = ((bf16[32,8,1536]{2,1,0:T(8,128)(2,1)}), bf16[32,8,1536]{2,1,0:T(8,128)(2,1)S(1)}, u32[]{:S(2)}, u32[]{:S(2)}) async-start(bf16[32,8,1536]{2,1,0:T(8,128)(2,1)} %bitcast.31), calls=%async_computation.5 | async-start | bytes 1572864 | tf_op jit(solution)/shard_map/all_to_all | solution.py:726
  203.6 8.5 %collective-permute-start.5 = (bf16[384,256]{1,0:T(8,128)(2,1)}, bf16[384,256]{1,0:T(8,128)(2,1)S(1)}, u32[]{:S(2)}, u32[]{:S(2)}) collective-permute-start(bf16[384,256]{1,0:T(8,128)(2,1)} %get-tuple-element.199), channel_id=1, source_target_pairs={{0,1},{1,2},{2,3},{3,0},{4,5},{5,6},{6,7},{7,4},{8,9},{9,10},{10,1... | collective-permute-start | bytes 589832 | tf_op jit(solution)/shard_map/ppermute | solution.py:733
  203.9 11.2 %collective-permute-start.6 = (bf16[384,256]{1,0:T(8,128)(2,1)}, bf16[384,256]{1,0:T(8,128)(2,1)S(1)}, u32[]{:S(2)}, u32[]{:S(2)}) collective-permute-start(bf16[384,256]{1,0:T(8,128)(2,1)} %get-tuple-element.200), channel_id=1, source_target_pairs={{0,2},{1,3},{2,0},{3,1},{4,6},{5,7},{6,4},{7,5},{8,10},{9,11},{10,... | collective-permute-start | bytes 589832 | tf_op jit(solution)/shard_map/ppermute | solution.py:733
  205.7 10.3 %collective-permute-start.7 = (bf16[384,256]{1,0:T(8,128)(2,1)}, bf16[384,256]{1,0:T(8,128)(2,1)S(1)}, u32[]{:S(2)}, u32[]{:S(2)}) collective-permute-start(bf16[384,256]{1,0:T(8,128)(2,1)} %get-tuple-element.201), channel_id=1, source_target_pairs={{0,3},{1,0},{2,1},{3,2},{4,7},{5,4},{6,5},{7,6},{8,11},{9,8},{10,9... | collective-permute-start | bytes 589832 | tf_op jit(solution)/shard_map/ppermute | solution.py:733
  206.4 23.1 %copy-start.4 = (bf16[1536,256]{1,0:T(8,128)(2,1)S(1)}, bf16[1536,256]{1,0:T(8,128)(2,1)}, u32[]{:S(2)}) copy-start(bf16[1536,256]{1,0:T(8,128)(2,1)} %copy-done.2) | copy-start | bytes 2359300
  206.4 26.4 %collective-permute-start.9 = (bf16[2,192,256]{2,1,0:T(8,128)(2,1)}, bf16[2,192,256]{2,1,0:T(8,128)(2,1)}, u32[]{:S(2)}, u32[]{:S(2)}) collective-permute-start(bf16[2,192,256]{2,1,0:T(8,128)(2,1)} %copy-done.47), channel_id=1, source_target_pairs={{124,4},{120,8},{116,12},{112,16},{108,20},{104,24},{100,28},{96,3... | collective-permute-start | bytes 589832 | tf_op jit(solution)/shard_map/ppermute | solution.py:888
  (43 other events, 134.9 us)
Sparse Core Ops, SparseCore 0:
  19.9 57.7 all-gather.1

commit v6 on v4

--- a/solution.py
+++ b/solution.py
@@ -80,8 +80,8 @@
 
 
 COLUMNS = narrow(column_tables())
-FORWARD_ROWS, INVERSE_ROWS = (narrow(t) for t in row_tables())
-TWIDDLE_COS, TWIDDLE_SIN = (t.astype(np.float32) for t in twiddle_tables())
+ROW_TABLES = narrow(np.stack(row_tables()))
+TWIDDLES = np.stack(twiddle_tables()).astype(np.float32)
 STRAIGHT = narrow(turn_table())
 UNIT = narrow(np.eye(LEN))
 
@@ -273,19 +273,19 @@
 
 
 def row_body(saves, refs):
-    received_ref, fwd_ref, inv_ref, cos_ref, sin_ref, main_ref = refs[:6]
+    received_ref, tables_ref, twiddles_ref, main_ref = refs[:4]
     if saves:
-        message_ref, seen_ref, mixed_ref, ready_ref = refs[6:]
+        message_ref, seen_ref, mixed_ref, ready_ref = refs[4:]
     else:
-        seen_ref, message_ref, product_ref, mixed_ref, ready_ref = refs[6:]
+        seen_ref, message_ref, product_ref, mixed_ref, ready_ref = refs[4:]
 
     def joined(at, width, edge, step):
         rows = received_ref[:, at : at + width].astype(F32)
         moved = moved_rows(received_ref[:, edge : edge + width].astype(F32), step)
-        return nn(fwd_ref[...], (rows + moved).astype(BF16))
+        return nn(tables_ref[0], (rows + moved).astype(BF16))
 
     for at in range(0, LANES, 512):
-        mixed_ref[:, at : at + 512] = nn(fwd_ref[...], received_ref[:, at : at + 512])
+        mixed_ref[:, at : at + 512] = nn(tables_ref[0], received_ref[:, at : at + 512])
     if not saves:
         for h, edge, step in ((0, SLAB, 1), (SLAB - 1, -1, -1)):
             at = wide_at(h)
@@ -297,7 +297,7 @@
         at = pl.ds(pl.multiple_of(index * 16, 16), 16)
         at_im = pl.ds(pl.multiple_of(LEN + index * 16, 16), 16)
         table = pl.ds(pl.multiple_of(lax.rem(index, 2) * 16, 16), 16)
-        cos, sin = cos_ref[table, :], sin_ref[table, :]
+        cos, sin = twiddles_ref[0, table, :], twiddles_ref[1, table, :]
         values = to_frequencies(mixed_ref[at, :], mixed_ref[at_im, :], cos, sin)
         filtered = []
         for n, (re, im) in enumerate(values):
@@ -320,7 +320,7 @@
 
     lax.fori_loop(0, 16, group, 0)
     for at in range(0, LANES, 512):
-        block = nn(inv_ref[...], ready_ref[:, at : at + 512])
+        block = nn(tables_ref[1], ready_ref[:, at : at + 512])
         message_ref[:, at : at + 512] = block.astype(BF16)
         if saves:
             for h, edge, step in ((0, SLAB, -1), (SLAB - 1, -1, 1)):
@@ -525,7 +525,7 @@
             out_ref[...] = parts_ref[lax.rem(channel + turn, CH_DEVICES)]
 
 
-def mlp(channel, hidden, dy_parts, gain, weights, block=256):
+def mlp(channel, hidden, dy_parts, gain, weights, block=512):
     tokens, steps = 2 * LEN, UNITS // 2 // block
     part = whole_block((2 * CH, LEN))
     return pl.pallas_call(
@@ -624,7 +624,7 @@
 def on_device(tile_image, spectral_filter, conv_taps, norm_gain, up_weight, down_weight, upstream):
     channel = lax.axis_index("ch").reshape(1).astype(jnp.int32)
     flat = (LANES, LEN)
-    tables = [jnp.asarray(t) for t in (FORWARD_ROWS, INVERSE_ROWS, TWIDDLE_COS, TWIDDLE_SIN)]
+    tables = [jnp.asarray(ROW_TABLES), jnp.asarray(TWIDDLES)]
     columns, straight = jnp.asarray(COLUMNS), jnp.asarray(STRAIGHT)
     wide = pltpu.VMEM((2, LANES, 128), F32)
     message, signal = kernel_call(
@@ -668,7 +668,7 @@
         2 * 16 * LEN * LEN * CH,
         beside=True,
     )
-    received, dy_parts, main = lax.optimization_barrier((received, dy_parts, main))
+    received, main = lax.optimization_barrier((received, main))
     row_scratch = [pltpu.VMEM((MESSAGE, LANES), F32), pltpu.VMEM((MESSAGE, LANES), BF16)]
     row_flops = 4 * MESSAGE * MESSAGE * LANES
     message, seen = kernel_call(
@@ -680,9 +680,9 @@
         20,
         row_flops,
     )
-    live = (seen, main, signal, dy, dy_parts, conv_taps, norm_gain)
+    live = (seen, main, signal, dy)
     received, live = fenced(message, ROWS, live)
-    seen, main, signal, dy, dy_parts, conv_taps, norm_gain = live
+    seen, main, signal, dy = live
     (hidden,) = kernel_call(
         hidden_kernel,
         "hidden",
@@ -692,12 +692,13 @@
         16,
         2 * MESSAGE * LEN * SENT,
     )
-    live = (seen, main, dy, dy_parts, conv_taps, norm_gain.reshape(1, ALL_CH), hidden)
+    live = (seen, main, dy, hidden)
     hidden_tokens, live = fenced(hidden, "ch", live)
-    seen, main, dy, dy_parts, conv_taps, gain_row, hidden = live
+    seen, main, dy, hidden = live
+    gain_row = norm_gain.reshape(1, ALL_CH)
     *out_turned, grad_message = mlp(channel, hidden_tokens, dy_parts, gain_row, weights)
-    grad_mlp, live = fenced(grad_message, "ch", (seen, main, dy, out_turned, conv_taps, hidden))
-    seen, main, dy, out_turned, conv_taps, hidden = live
+    grad_mlp, live = fenced(grad_message, "ch", (seen, main, dy, out_turned, hidden))
+    seen, main, dy, out_turned, hidden = live
     (message,) = kernel_call(
         gradient_columns_kernel,
         "gradient_columns",

time: 230 us -> 237 us (1.030)
  waiting for transfers between devices: 24.5 us -> 73.1 us
  blocking collectives: 94.3 us -> 46.8 us
  starting transfers between devices: 21.5 us -> 30.2 us
    all_to_all x2 -> x4, waiting for transfers between devices: 13.2 us -> 61.8 us  [to_peers(): return lax.all_to_all(values, axis, split_axis=0, concat_axis=0, tiled=True)]
    all_to_all x4 -> x2, blocking collectives: 94.3 us -> 46.8 us  [to_peers(): return lax.all_to_all(values, axis, split_axis=0, concat_axis=0, tiled=True)]
    all_to_all x2 -> x4, starting transfers between devices: 13.8 us -> 22.3 us  [to_peers(): return lax.all_to_all(values, axis, split_axis=0, concat_axis=0, tiled=True)]
    unnamed x96 -> x95, local copies, waits for them, and re-layouts: 21.9 us -> 22.7 us
  transfers between devices with their start and end apart: 9 -> 11, of which waited for: 5 -> 8; matrix products, arithmetic and copies ran while one was open for 1% -> 0% of each run, Pallas kernels for 7% -> 7%
where the time goes in v6:
time: 237 us; the launch traced here: 236 us
  waiting for transfers between devices  73.1 us (31%)
  Pallas kernels  47.3 us (20%)
  blocking collectives  46.8 us (20%)
  starting transfers between devices  30.2 us (13%)
  local copies, waits for them, and re-layouts  23.4 us (10%)
  between operations  14.4 us (6%)
    all_to_all x4, waiting for transfers between devices, to_peers(): return lax.all_to_all(values, axis, split_axis=0, concat_axis=0, tiled=True)  61.8 us
    all_to_all x2, blocking collectives, to_peers(): return lax.all_to_all(values, axis, split_axis=0, concat_axis=0, tiled=True)  46.8 us
    pallas_call x10, Pallas kernels, kernel_call(): pl.pallas_call(body, name=name, grid=(1,), out_shape=tuple(outs), in_spec...  31.8 us
    unnamed x95, local copies, waits for them, and re-layouts  22.7 us
    all_to_all x4, starting transfers between devices, to_peers(): return lax.all_to_all(values, axis, split_axis=0, concat_axis=0, tiled=True)  22.3 us
    pallas_call x1, Pallas kernels, mlp(): pl.pallas_call(mlp_kernel, name='mlp', grid=(steps,), out_shape=(*(shape(...  15.5 us
    ppermute x6, waiting for transfers between devices, turned_exchange(): received.append(lax.ppermute(parts[turn], 'ch', pairs))  11.3 us
    ppermute x6, starting transfers between devices, turned_exchange(): received.append(lax.ppermute(parts[turn], 'ch', pairs))  7.89 us
  transfers between devices with their start and end apart: 11, of which 8 were waited for; matrix products, arithmetic and copies ran while one was open for 0% of the time, Pallas kernels for 7%

profile of v6, /device:TPU:1, one launch (start us, length us, event | category | flops | bytes accessed | tf_op | source)
XLA Modules:
  0.0 236.3 jit_solution(3046497323964908308)
XLA Ops:
  9.4 2.0 columns.1
  18.6 9.8 %all-to-all-start = ((bf16[32,16,1536]{2,1,0:T(8,128)(2,1)}), bf16[32,16,1536]{2,1,0:T(8,128)(2,1)}, u32[]{:S(2)}, u32[]{:S(2)}) async-start(bf16[32,16,1536]{2,1,0:T(8,128)(2,1)} %bitcast.2), calls=%async_computation | async-start | bytes 3145728 | tf_op jit(solution)/shard_map/all_to_all | solution.py:604
  28.4 1.9 copy-done.5
  31.4 19.7 %all-to-all-done = bf16[32,16,1536]{2,1,0:T(8,128)(2,1)} async-done(((bf16[32,16,1536]{2,1,0:T(8,128)(2,1)}), bf16[32,16,1536]{2,1,0:T(8,128)(2,1)}, u32[]{:S(2)}, u32[]{:S(2)}) %all-to-all-start) | async-done | bytes 1572896 | tf_op jit(solution)/shard_map/all_to_all | solution.py:604
  52.3 7.0 %rows_forward.1 = (bf16[512,1920]{1,0:T(8,128)(2,1)S(1)}, bf16[2,256,1536]{2,1,0:T(8,128)(2,1)S(1)}) custom-call(bf16[512,1536]{1,0:T(8,128)(2,1)} %bitcast.3.refs_0_, bf16[2,512,512]{2,1,0:T(8,128)(2,1)S(1)} %copy-done.18, f32[2,32,1536]{2,1,0:T(8,128)S(1)} %copy-done.26, bf16[2,256,1536]{2,1,0:T(8,128)(2,1)S(1)} %filter.1.refs_3_), custom_call_target="tpu_custom_call" | custom-call | flops 1610612736 | bytes 8126464 | tf_op jit(solution)/shard_map/rows_forward/pallas_call | solution.py:109
  61.8 4.5 %all-to-all-start.1 = ((bf16[32,16,1920]{2,1,0:T(8,128)(2,1)}), bf16[32,16,1920]{2,1,0:T(8,128)(2,1)S(1)}, u32[]{:S(2)}, u32[]{:S(2)}) async-start(bf16[32,16,1920]{2,1,0:T(8,128)(2,1)} %bitcast.29), calls=%async_computation.1 | async-start | bytes 3932160 | tf_op jit(solution)/shard_map/all_to_all | solution.py:604
  66.4 26.9 %all-to-all-done.1 = bf16[32,16,1920]{2,1,0:T(8,128)(2,1)S(1)} async-done(((bf16[32,16,1920]{2,1,0:T(8,128)(2,1)}), bf16[32,16,1920]{2,1,0:T(8,128)(2,1)S(1)}, u32[]{:S(2)}, u32[]{:S(2)}) %all-to-all-start.1) | async-done | bytes 1966112 | tf_op jit(solution)/shard_map/all_to_all | solution.py:604
  94.3 3.4 %hidden.1.hidden_ref = bf16[1536,256]{1,0:T(8,128)(2,1)S(1)} custom-call(bf16[512,1920]{1,0:T(8,128)(2,1)S(1)} %bitcast.21, bf16[512,256]{1,0:T(8,128)(2,1)S(1)} %copy-done.10, f32[192,9]{1,0:T(8,128)S(1)} %copy.15.taps_ref, bf16[1536,256]{1,0:T(8,128)(2,1)S(1)} %copy-done.22), custom_call_target="tpu_custom_call" | custom-call | flops 503316480 | bytes 3808000 | tf_op jit(solution)/shard_map/hidden/pallas_call | solution.py:109
  98.7 4.1 %all-to-all-start.2 = ((bf16[4,384,256]{2,1,0:T(8,128)(2,1)}), bf16[4,384,256]{2,1,0:T(8,128)(2,1)S(1)}, u32[]{:S(2)}, u32[]{:S(2)}) async-start(bf16[4,384,256]{2,1,0:T(8,128)(2,1)} %bitcast.24), calls=%async_computation.2 | async-start | bytes 1572864 | tf_op jit(solution)/shard_map/all_to_all | solution.py:604
  104.2 2.4 %collective-permute-start.1 = (bf16[384,256]{1,0:T(8,128)(2,1)S(1)}, bf16[384,256]{1,0:T(8,128)(2,1)}, u32[]{:S(2)}, u32[]{:S(2)}) collective-permute-start(bf16[384,256]{1,0:T(8,128)(2,1)S(1)} %copy-done.36), channel_id=1, source_target_pairs={{0,2},{1,3},{2,0},{3,1},{4,6},{5,7},{6,4},{7,5},{8,10},{9,11},{10,... | collective-permute-start | bytes 589832 | tf_op jit(solution)/shard_map/ppermute | solution.py:611
  107.8 6.2 %all-to-all-done.2 = bf16[4,384,256]{2,1,0:T(8,128)(2,1)S(1)} async-done(((bf16[4,384,256]{2,1,0:T(8,128)(2,1)}), bf16[4,384,256]{2,1,0:T(8,128)(2,1)S(1)}, u32[]{:S(2)}, u32[]{:S(2)}) %all-to-all-start.2) | async-done | bytes 786464 | tf_op jit(solution)/shard_map/all_to_all | solution.py:604
  114.0 3.9 %collective-permute-done.dy_one_ref = bf16[384,256]{1,0:T(8,128)(2,1)S(1)} collective-permute-done((bf16[384,256]{1,0:T(8,128)(2,1)S(1)}, bf16[384,256]{1,0:T(8,128)(2,1)S(1)}, u32[]{:S(2)}, u32[]{:S(2)}) %collective-permute-start) | collective-permute-done | bytes 196640 | tf_op jit(solution)/shard_map/ppermute | solution.py:611
  118.6 4.0 %collective-permute-done.1.dy_two_ref = bf16[384,256]{1,0:T(8,128)(2,1)} collective-permute-done((bf16[384,256]{1,0:T(8,128)(2,1)S(1)}, bf16[384,256]{1,0:T(8,128)(2,1)}, u32[]{:S(2)}, u32[]{:S(2)}) %collective-permute-start.1) | collective-permute-done | bytes 196640 | tf_op jit(solution)/shard_map/ppermute | solution.py:611
  123.5 15.5 %mlp.1 = (bf16[384,256]{1,0:T(8,128)(2,1)S(1)}, bf16[384,256]{1,0:T(8,128)(2,1)S(1)}, bf16[384,256]{1,0:T(8,128)(2,1)S(1)}, bf16[384,256]{1,0:T(8,128)(2,1)S(1)}, bf16[1536,256]{1,0:T(8,128)(2,1)S(1)}) custom-call(s32[1]{0:T(128)} %bitcast.channel_ref, bf16[1536,256]{1,0:T(8,128)(2,1)S(1)} %bitcast.31, bf16[384,256]{1,0:T(8,128)(2,1)S(1)} %copy-done.32, ...), custom_call_target="tpu_custom_call" | custom-call | flops 9663676416 | bytes 12582912 | tf_op jit(solution)/shard_map/mlp/pallas_call | solution.py:531
  139.1 12.6 %all_to_all.71 = bf16[4,384,256]{2,1,0:T(8,128)(2,1)S(1)} all-to-all(bf16[4,384,256]{2,1,0:T(8,128)(2,1)S(1)} %bitcast.32), channel_id=1, replica_groups=mesh['y'=4,'z'=4,'core'=2,'ch'=4] {'ch'}, dimensions={0} | all-to-all | bytes 1572864 | tf_op jit(solution)/shard_map/all_to_all | solution.py:604
  151.7 3.8 %gradient_columns.1 = bf16[512,1920]{1,0:T(8,128)(2,1)S(1)} custom-call(bf16[1536,256]{1,0:T(8,128)(2,1)S(1)} %copy-done.7, bf16[1536,256]{1,0:T(8,128)(2,1)S(1)} %bitcast.25, f32[192,9]{1,0:T(8,128)S(1)} %copy.15.taps_ref, bf16[512,256]{1,0:T(8,128)(2,1)S(1)} %copy-done.10), custom_call_target="tpu_custom_call" | custom-call | flops 503316480 | bytes 3808000 | tf_op jit(solution)/shard_map/gradient_columns/pallas_call | solution.py:109
  155.5 34.3 %all_to_all.72 = bf16[32,16,1920]{2,1,0:T(8,128)(2,1)S(1)} all-to-all(bf16[32,16,1920]{2,1,0:T(8,128)(2,1)S(1)} %bitcast.23), channel_id=1, replica_groups=mesh['y'=4,'z'=4,'core'=2,'ch'=4] {'y','z','core'}, dimensions={0} | all-to-all | bytes 3932160 | tf_op jit(solution)/shard_map/all_to_all | solution.py:604
  189.8 6.7 %rows_backward.1 = (bf16[512,1536]{1,0:T(8,128)(2,1)S(1)}, bf16[2,256,1536]{2,1,0:T(8,128)(2,1)S(1)}) custom-call(bf16[512,1920]{1,0:T(8,128)(2,1)S(1)} %bitcast.22, bf16[2,512,512]{2,1,0:T(8,128)(2,1)S(1)} %copy-done.19, f32[2,32,1536]{2,1,0:T(8,128)S(1)} %copy-done.27, bf16[2,256,1536]{2,1,0:T(8,128)(2,1)S(1)} %copy-done.4, ...), custom_call_target="tpu_custom_call" | custom-call | flops 1610612736 | bytes 9699328 | tf_op jit(solution)/shard_map/rows_backward/pallas_call | solution.py:109
  198.8 4.0 %all-to-all-start.5 = ((bf16[32,16,1536]{2,1,0:T(8,128)(2,1)}), bf16[32,16,1536]{2,1,0:T(8,128)(2,1)S(1)}, u32[]{:S(2)}, u32[]{:S(2)}) async-start(bf16[32,16,1536]{2,1,0:T(8,128)(2,1)} %bitcast.30), calls=%async_computation.5 | async-start | bytes 3145728 | tf_op jit(solution)/shard_map/all_to_all | solution.py:604
  203.2 1.8 collective-permute-start.4
  208.0 3.7 %grad_filter.1 = f32[2,1536,256]{2,1,0:T(8,128)} custom-call(bf16[2,256,1536]{2,1,0:T(8,128)(2,1)S(1)} %copy-done.17, bf16[256,256]{1,0:T(8,128)(2,1)S(1)} %copy-done.25), custom_call_target="tpu_custom_call" | custom-call | bytes 1024 | tf_op jit(solution)/shard_map/grad_filter/pallas_call | solution.py:109
  211.7 2.6 %collective-permute-done.4.two_ref = bf16[384,256]{1,0:T(8,128)(2,1)S(1)} collective-permute-done((bf16[384,256]{1,0:T(8,128)(2,1)}, bf16[384,256]{1,0:T(8,128)(2,1)S(1)}, u32[]{:S(2)}, u32[]{:S(2)}) %collective-permute-start.4) | collective-permute-done | bytes 196640 | tf_op jit(solution)/shard_map/ppermute | solution.py:611
  216.4 9.1 %all-to-all-done.5 = bf16[32,16,1536]{2,1,0:T(8,128)(2,1)S(1)} async-done(((bf16[32,16,1536]{2,1,0:T(8,128)(2,1)}), bf16[32,16,1536]{2,1,0:T(8,128)(2,1)S(1)}, u32[]{:S(2)}, u32[]{:S(2)}) %all-to-all-start.5) | async-done | bytes 1572896 | tf_op jit(solution)/shard_map/all_to_all | solution.py:604
  227.6 1.9 image.1
  (112 shorter events, 30.5 us)
Async XLA Ops:
  7.2 115.4 %all-gather.2.cloned.1.call-start = ((), (), s32[]{:S(2)}) async-start(), calls=%async_computation.6 | async-start | bytes 10616832 | tf_op jit(solution)/shard_map/all_gather | solution.py:659
  18.6 32.5 %all-to-all-start = ((bf16[32,16,1536]{2,1,0:T(8,128)(2,1)}), bf16[32,16,1536]{2,1,0:T(8,128)(2,1)}, u32[]{:S(2)}, u32[]{:S(2)}) async-start(bf16[32,16,1536]{2,1,0:T(8,128)(2,1)} %bitcast.2), calls=%async_computation | async-start | bytes 3145728 | tf_op jit(solution)/shard_map/all_to_all | solution.py:604
  30.3 20.8 %copy-start.26 = (f32[2,32,1536]{2,1,0:T(8,128)S(1)}, f32[2,32,1536]{2,1,0:T(8,128)}, u32[]{:S(2)}) copy-start(f32[2,32,1536]{2,1,0:T(8,128)} %constant.24.clone.refs_2_) | copy-start | bytes 1179652
  31.4 27.9 %copy-start.3 = (bf16[2,256,1536]{2,1,0:T(8,128)(2,1)}, bf16[2,256,1536]{2,1,0:T(8,128)(2,1)S(1)}, u32[]{:S(2)}) copy-start(bf16[2,256,1536]{2,1,0:T(8,128)(2,1)S(1)} %filter.1.refs_3_) | copy-start | bytes 4718596
  61.8 31.4 %copy-start.10 = (bf16[512,256]{1,0:T(8,128)(2,1)S(1)}, bf16[512,256]{1,0:T(8,128)(2,1)}, u32[]{:S(2)}) copy-start(bf16[512,256]{1,0:T(8,128)(2,1)} %constant.25.clone.table_ref) | copy-start | bytes 786436
  61.8 31.4 %all-to-all-start.1 = ((bf16[32,16,1920]{2,1,0:T(8,128)(2,1)}), bf16[32,16,1920]{2,1,0:T(8,128)(2,1)S(1)}, u32[]{:S(2)}, u32[]{:S(2)}) async-start(bf16[32,16,1920]{2,1,0:T(8,128)(2,1)} %bitcast.29), calls=%async_computation.1 | async-start | bytes 3932160 | tf_op jit(solution)/shard_map/all_to_all | solution.py:604
  98.7 23.9 %copy-start.24 = (bf16[256,256]{1,0:T(8,128)(2,1)S(1)}, bf16[256,256]{1,0:T(8,128)(2,1)}, u32[]{:S(2)}) copy-start(bf16[256,256]{1,0:T(8,128)(2,1)} %constant.26.clone.straight_ref.unit_ref) | copy-start | bytes 393220
  98.7 23.9 %copy-start.32 = (bf16[384,256]{1,0:T(8,128)(2,1)S(1)}, bf16[384,256]{1,0:T(8,128)(2,1)}, u32[]{:S(2)}) copy-start(bf16[384,256]{1,0:T(8,128)(2,1)} %copy-done.31) | copy-start | bytes 589828
  98.7 15.3 %all-to-all-start.2 = ((bf16[4,384,256]{2,1,0:T(8,128)(2,1)}), bf16[4,384,256]{2,1,0:T(8,128)(2,1)S(1)}, u32[]{:S(2)}, u32[]{:S(2)}) async-start(bf16[4,384,256]{2,1,0:T(8,128)(2,1)} %bitcast.24), calls=%async_computation.2 | async-start | bytes 1572864 | tf_op jit(solution)/shard_map/all_to_all | solution.py:604
  102.8 15.1 %collective-permute-start = (bf16[384,256]{1,0:T(8,128)(2,1)S(1)}, bf16[384,256]{1,0:T(8,128)(2,1)S(1)}, u32[]{:S(2)}, u32[]{:S(2)}) collective-permute-start(bf16[384,256]{1,0:T(8,128)(2,1)S(1)} %copy-done.38), channel_id=1, source_target_pairs={{0,1},{1,2},{2,3},{3,0},{4,5},{5,6},{6,7},{7,4},{8,9},{9,10},{10,1... | collective-permute-start | bytes 589832 | tf_op jit(solution)/shard_map/ppermute | solution.py:611
  104.2 18.3 %collective-permute-start.1 = (bf16[384,256]{1,0:T(8,128)(2,1)S(1)}, bf16[384,256]{1,0:T(8,128)(2,1)}, u32[]{:S(2)}, u32[]{:S(2)}) collective-permute-start(bf16[384,256]{1,0:T(8,128)(2,1)S(1)} %copy-done.36), channel_id=1, source_target_pairs={{0,2},{1,3},{2,0},{3,1},{4,6},{5,7},{6,4},{7,5},{8,10},{9,11},{10,... | collective-permute-start | bytes 589832 | tf_op jit(solution)/shard_map/ppermute | solution.py:611
  106.6 15.9 %collective-permute-start.2 = (bf16[384,256]{1,0:T(8,128)(2,1)S(1)}, bf16[384,256]{1,0:T(8,128)(2,1)}, u32[]{:S(2)}, u32[]{:S(2)}) collective-permute-start(bf16[384,256]{1,0:T(8,128)(2,1)S(1)} %copy-done.34), channel_id=1, source_target_pairs={{0,3},{1,0},{2,1},{3,2},{4,7},{5,4},{6,5},{7,6},{8,11},{9,8},{10,9... | collective-permute-start | bytes 589832 | tf_op jit(solution)/shard_map/ppermute | solution.py:611
  139.1 16.4 %copy-start.28 = (bf16[384,256]{1,0:T(8,128)(2,1)}, bf16[384,256]{1,0:T(8,128)(2,1)S(1)}, u32[]{:S(2)}) copy-start(bf16[384,256]{1,0:T(8,128)(2,1)S(1)} %get-tuple-element.173.own_ref) | copy-start | bytes 589828
  139.1 16.4 %copy-start.40 = (bf16[384,256]{1,0:T(8,128)(2,1)}, bf16[384,256]{1,0:T(8,128)(2,1)S(1)}, u32[]{:S(2)}) copy-start(bf16[384,256]{1,0:T(8,128)(2,1)S(1)} %get-tuple-element.175) | copy-start | bytes 589828
  139.1 16.4 %copy-start.41 = (bf16[384,256]{1,0:T(8,128)(2,1)}, bf16[384,256]{1,0:T(8,128)(2,1)S(1)}, u32[]{:S(2)}) copy-start(bf16[384,256]{1,0:T(8,128)(2,1)S(1)} %get-tuple-element.174) | copy-start | bytes 589828
  139.1 57.4 %copy-start.39 = (bf16[384,256]{1,0:T(8,128)(2,1)}, bf16[384,256]{1,0:T(8,128)(2,1)S(1)}, u32[]{:S(2)}) copy-start(bf16[384,256]{1,0:T(8,128)(2,1)S(1)} %get-tuple-element.176) | copy-start | bytes 589828
  151.7 38.1 %copy-start.19 = (bf16[2,512,512]{2,1,0:T(8,128)(2,1)S(1)}, bf16[2,512,512]{2,1,0:T(8,128)(2,1)}, u32[]{:S(2)}) copy-start(bf16[2,512,512]{2,1,0:T(8,128)(2,1)} %constant.23.clone.refs_1_) | copy-start | bytes 3145732
  155.5 34.3 %copy-start.4 = (bf16[2,256,1536]{2,1,0:T(8,128)(2,1)S(1)}, bf16[2,256,1536]{2,1,0:T(8,128)(2,1)}, u32[]{:S(2)}) copy-start(bf16[2,256,1536]{2,1,0:T(8,128)(2,1)} %copy-done.3) | copy-start | bytes 4718596
  155.5 34.3 %copy-start.15 = (bf16[2,256,1536]{2,1,0:T(8,128)(2,1)S(1)}, bf16[2,256,1536]{2,1,0:T(8,128)(2,1)}, u32[]{:S(2)}) copy-start(bf16[2,256,1536]{2,1,0:T(8,128)(2,1)} %copy-done.14) | copy-start | bytes 4718596
  155.5 34.3 %copy-start.27 = (f32[2,32,1536]{2,1,0:T(8,128)S(1)}, f32[2,32,1536]{2,1,0:T(8,128)}, u32[]{:S(2)}) copy-start(f32[2,32,1536]{2,1,0:T(8,128)} %constant.24.clone.refs_2_) | copy-start | bytes 1179652
  198.8 26.7 %all-to-all-start.5 = ((bf16[32,16,1536]{2,1,0:T(8,128)(2,1)}), bf16[32,16,1536]{2,1,0:T(8,128)(2,1)S(1)}, u32[]{:S(2)}, u32[]{:S(2)}) async-start(bf16[32,16,1536]{2,1,0:T(8,128)(2,1)} %bitcast.30), calls=%async_computation.5 | async-start | bytes 3145728 | tf_op jit(solution)/shard_map/all_to_all | solution.py:604
  202.8 8.9 %collective-permute-start.3 = (bf16[384,256]{1,0:T(8,128)(2,1)}, bf16[384,256]{1,0:T(8,128)(2,1)S(1)}, u32[]{:S(2)}, u32[]{:S(2)}) collective-permute-start(bf16[384,256]{1,0:T(8,128)(2,1)} %copy-done.41), channel_id=1, source_target_pairs={{0,1},{1,2},{2,3},{3,0},{4,5},{5,6},{6,7},{7,4},{8,9},{9,10},{10,1... | collective-permute-start | bytes 589832 | tf_op jit(solution)/shard_map/ppermute | solution.py:611
  203.2 11.1 %collective-permute-start.4 = (bf16[384,256]{1,0:T(8,128)(2,1)}, bf16[384,256]{1,0:T(8,128)(2,1)S(1)}, u32[]{:S(2)}, u32[]{:S(2)}) collective-permute-start(bf16[384,256]{1,0:T(8,128)(2,1)} %copy-done.40), channel_id=1, source_target_pairs={{0,2},{1,3},{2,0},{3,1},{4,6},{5,7},{6,4},{7,5},{8,10},{9,11},{10,... | collective-permute-start | bytes 589832 | tf_op jit(solution)/shard_map/ppermute | solution.py:611
  204.9 10.2 %collective-permute-start.5 = (bf16[384,256]{1,0:T(8,128)(2,1)}, bf16[384,256]{1,0:T(8,128)(2,1)S(1)}, u32[]{:S(2)}, u32[]{:S(2)}) collective-permute-start(bf16[384,256]{1,0:T(8,128)(2,1)} %copy-done.39), channel_id=1, source_target_pairs={{0,3},{1,0},{2,1},{3,2},{4,7},{5,4},{6,5},{7,6},{8,11},{9,8},{10,9... | collective-permute-start | bytes 589832 | tf_op jit(solution)/shard_map/ppermute | solution.py:611
  (34 other events, 115.9 us)
Sparse Core Ops, SparseCore 0:
  18.7 57.7 all-gather.1

commit v7 on v6

--- a/solution.py
+++ b/solution.py
@@ -668,7 +668,7 @@
         2 * 16 * LEN * LEN * CH,
         beside=True,
     )
-    received, main = lax.optimization_barrier((received, main))
+    received, dy_parts, main = lax.optimization_barrier((received, dy_parts, main))
     row_scratch = [pltpu.VMEM((MESSAGE, LANES), F32), pltpu.VMEM((MESSAGE, LANES), BF16)]
     row_flops = 4 * MESSAGE * MESSAGE * LANES
     message, seen = kernel_call(
@@ -680,9 +680,9 @@
         20,
         row_flops,
     )
-    live = (seen, main, signal, dy)
+    live = (seen, main, signal, dy, dy_parts, conv_taps, norm_gain)
     received, live = fenced(message, ROWS, live)
-    seen, main, signal, dy = live
+    seen, main, signal, dy, dy_parts, conv_taps, norm_gain = live
     (hidden,) = kernel_call(
         hidden_kernel,
         "hidden",
@@ -692,13 +692,12 @@
         16,
         2 * MESSAGE * LEN * SENT,
     )
-    live = (seen, main, dy, hidden)
+    live = (seen, main, dy, dy_parts, conv_taps, norm_gain.reshape(1, ALL_CH), hidden)
     hidden_tokens, live = fenced(hidden, "ch", live)
-    seen, main, dy, hidden = live
-    gain_row = norm_gain.reshape(1, ALL_CH)
+    seen, main, dy, dy_parts, conv_taps, gain_row, hidden = live
     *out_turned, grad_message = mlp(channel, hidden_tokens, dy_parts, gain_row, weights)
-    grad_mlp, live = fenced(grad_message, "ch", (seen, main, dy, out_turned, hidden))
-    seen, main, dy, out_turned, hidden = live
+    grad_mlp, live = fenced(grad_message, "ch", (seen, main, dy, out_turned, conv_taps, hidden))
+    seen, main, dy, out_turned, conv_taps, hidden = live
     (message,) = kernel_call(
         gradient_columns_kernel,
         "gradient_columns",

time: 237 us -> 228 us (0.962)
  waiting for transfers between devices: 73.1 us -> 24.5 us
  blocking collectives: 46.8 us -> 94.4 us
  starting transfers between devices: 30.2 us -> 21.5 us
    all_to_all x4 -> x2, waiting for transfers between devices: 61.8 us -> 13.2 us  [to_peers(): return lax.all_to_all(values, axis, split_axis=0, concat_axis=0, tiled=True)]
    all_to_all x2 -> x4, blocking collectives: 46.8 us -> 94.4 us  [to_peers(): return lax.all_to_all(values, axis, split_axis=0, concat_axis=0, tiled=True)]
    all_to_all x4 -> x2, starting transfers between devices: 22.3 us -> 13.8 us  [to_peers(): return lax.all_to_all(values, axis, split_axis=0, concat_axis=0, tiled=True)]
    unnamed x95 -> x86, local copies, waits for them, and re-layouts: 22.7 us -> 20.2 us
  transfers between devices with their start and end apart: 11 -> 9, of which waited for: 8 -> 5; matrix products, arithmetic and copies ran while one was open for 0% -> 1% of each run, Pallas kernels for 7% -> 7%
where the time goes in v7:
time: 228 us; the launch traced here: 227 us
  blocking collectives  94.4 us (41%)
  Pallas kernels  47.9 us (21%)
  waiting for transfers between devices  24.5 us (11%)
  local copies, waits for them, and re-layouts  23.4 us (10%)
  starting transfers between devices  21.5 us (9%)
  between operations  14.4 us (6%)
    all_to_all x4, blocking collectives, to_peers(): return lax.all_to_all(values, axis, split_axis=0, concat_axis=0, tiled=True)  94.4 us
    pallas_call x10, Pallas kernels, kernel_call(): pl.pallas_call(body, name=name, grid=(1,), out_shape=tuple(outs), in_spec...  32.4 us
    unnamed x86, local copies, waits for them, and re-layouts  20.2 us
    pallas_call x1, Pallas kernels, mlp(): pl.pallas_call(mlp_kernel, name='mlp', grid=(steps,), out_shape=(*(shape(...  15.5 us
    all_to_all x2, starting transfers between devices, to_peers(): return lax.all_to_all(values, axis, split_axis=0, concat_axis=0, tiled=True)  13.8 us
    all_to_all x2, waiting for transfers between devices, to_peers(): return lax.all_to_all(values, axis, split_axis=0, concat_axis=0, tiled=True)  13.2 us
    ppermute x6, waiting for transfers between devices, turned_exchange(): received.append(lax.ppermute(parts[turn], 'ch', pairs))  11.3 us
    ppermute x6, starting transfers between devices, turned_exchange(): received.append(lax.ppermute(parts[turn], 'ch', pairs))  7.73 us
  transfers between devices with their start and end apart: 9, of which 5 were waited for; matrix products, arithmetic and copies ran while one was open for 1% of the time, Pallas kernels for 7%

profile of v7, /device:TPU:1, one launch (start us, length us, event | category | flops | bytes accessed | tf_op | source)
XLA Modules:
  0.0 227.2 jit_solution(9224136950303513779)
XLA Ops:
  9.4 2.0 columns.1
  12.3 1.5 unfold.1
  15.3 1.6 copy.16
  18.2 9.8 %all-to-all-start = ((bf16[32,16,1536]{2,1,0:T(8,128)(2,1)}), bf16[32,16,1536]{2,1,0:T(8,128)(2,1)}, u32[]{:S(2)}, u32[]{:S(2)}) async-start(bf16[32,16,1536]{2,1,0:T(8,128)(2,1)} %bitcast.2), calls=%async_computation | async-start | bytes 3145728 | tf_op jit(solution)/shard_map/all_to_all | solution.py:604
  29.3 2.5 %collective-permute-start.1 = (bf16[384,256]{1,0:T(8,128)(2,1)}, bf16[384,256]{1,0:T(8,128)(2,1)S(1)}, u32[]{:S(2)}, u32[]{:S(2)}) collective-permute-start(bf16[384,256]{1,0:T(8,128)(2,1)} %get-tuple-element.126), channel_id=1, source_target_pairs={{0,2},{1,3},{2,0},{3,1},{4,6},{5,7},{6,4},{7,5},{8,10},{9,11},{10,... | collective-permute-start | bytes 589832 | tf_op jit(solution)/shard_map/ppermute | solution.py:611
  32.9 2.6 %copy-done.5 = f32[2,192,8,256]{3,2,1,0:T(8,128)S(1)} copy-done((f32[2,192,8,256]{3,2,1,0:T(8,128)S(1)}, f32[2,192,8,256]{3,2,1,0:T(8,128)}, u32[]{:S(2)}) %copy-start.5) | copy-done | bytes 3145752
  37.4 7.8 %collective-permute-done.1.dy_two_ref = bf16[384,256]{1,0:T(8,128)(2,1)S(1)} collective-permute-done((bf16[384,256]{1,0:T(8,128)(2,1)}, bf16[384,256]{1,0:T(8,128)(2,1)S(1)}, u32[]{:S(2)}, u32[]{:S(2)}) %collective-permute-start.1) | collective-permute-done | bytes 196640 | tf_op jit(solution)/shard_map/ppermute | solution.py:611
  46.6 4.2 %all-to-all-done = bf16[32,16,1536]{2,1,0:T(8,128)(2,1)} async-done(((bf16[32,16,1536]{2,1,0:T(8,128)(2,1)}), bf16[32,16,1536]{2,1,0:T(8,128)(2,1)}, u32[]{:S(2)}, u32[]{:S(2)}) %all-to-all-start) | async-done | bytes 1572896 | tf_op jit(solution)/shard_map/all_to_all | solution.py:604
  52.0 6.9 %rows_forward.1 = (bf16[512,1920]{1,0:T(8,128)(2,1)S(1)}, bf16[2,256,1536]{2,1,0:T(8,128)(2,1)S(1)}) custom-call(bf16[512,1536]{1,0:T(8,128)(2,1)} %bitcast.3.refs_0_, bf16[2,512,512]{2,1,0:T(8,128)(2,1)S(1)} %copy-done.17, f32[2,32,1536]{2,1,0:T(8,128)S(1)} %copy-done.24, bf16[2,256,1536]{2,1,0:T(8,128)(2,1)S(1)} %filter.1.refs_3_), custom_call_target="tpu_custom_call" | custom-call | flops 1610612736 | bytes 8126464 | tf_op jit(solution)/shard_map/rows_forward/pallas_call | solution.py:109
  58.9 32.1 %all_to_all.71 = bf16[32,16,1920]{2,1,0:T(8,128)(2,1)S(1)} all-to-all(bf16[32,16,1920]{2,1,0:T(8,128)(2,1)S(1)} %bitcast.29), channel_id=1, replica_groups=mesh['y'=4,'z'=4,'core'=2,'ch'=4] {'y','z','core'}, dimensions={0} | all-to-all | bytes 3932160 | tf_op jit(solution)/shard_map/all_to_all | solution.py:604
  94.5 3.4 %hidden.1.hidden_ref = bf16[1536,256]{1,0:T(8,128)(2,1)S(1)} custom-call(bf16[512,1920]{1,0:T(8,128)(2,1)S(1)} %bitcast.22, bf16[512,256]{1,0:T(8,128)(2,1)S(1)} %copy-done.10, f32[192,9]{1,0:T(8,128)S(1)} %copy-done.26, bf16[1536,256]{1,0:T(8,128)(2,1)S(1)} %copy-done.21), custom_call_target="tpu_custom_call" | custom-call | flops 503316480 | bytes 3808000 | tf_op jit(solution)/shard_map/hidden/pallas_call | solution.py:109
  98.0 16.1 %all_to_all.72 = bf16[4,384,256]{2,1,0:T(8,128)(2,1)S(1)} all-to-all(bf16[4,384,256]{2,1,0:T(8,128)(2,1)S(1)} %bitcast.24), channel_id=1, replica_groups=mesh['y'=4,'z'=4,'core'=2,'ch'=4] {'ch'}, dimensions={0} | all-to-all | bytes 1572864 | tf_op jit(solution)/shard_map/all_to_all | solution.py:604
  115.0 15.5 %mlp.1 = (bf16[384,256]{1,0:T(8,128)(2,1)S(1)}, bf16[384,256]{1,0:T(8,128)(2,1)S(1)}, bf16[384,256]{1,0:T(8,128)(2,1)S(1)}, bf16[384,256]{1,0:T(8,128)(2,1)S(1)}, bf16[1536,256]{1,0:T(8,128)(2,1)S(1)}) custom-call(s32[1]{0:T(128)} %bitcast.channel_ref, bf16[1536,256]{1,0:T(8,128)(2,1)S(1)} %bitcast.31, bf16[384,256]{1,0:T(8,128)(2,1)S(1)} %copy-done.31, ...), custom_call_target="tpu_custom_call" | custom-call | flops 9663676416 | bytes 12582912 | tf_op jit(solution)/shard_map/mlp/pallas_call | solution.py:531
  130.6 13.7 %all_to_all.73 = bf16[4,384,256]{2,1,0:T(8,128)(2,1)S(1)} all-to-all(bf16[4,384,256]{2,1,0:T(8,128)(2,1)S(1)} %bitcast.32), channel_id=1, replica_groups=mesh['y'=4,'z'=4,'core'=2,'ch'=4] {'ch'}, dimensions={0} | all-to-all | bytes 1572864 | tf_op jit(solution)/shard_map/all_to_all | solution.py:604
  144.4 3.8 %gradient_columns.1 = bf16[512,1920]{1,0:T(8,128)(2,1)S(1)} custom-call(bf16[1536,256]{1,0:T(8,128)(2,1)S(1)} %copy-done.7, bf16[1536,256]{1,0:T(8,128)(2,1)S(1)} %bitcast.25, f32[192,9]{1,0:T(8,128)S(1)} %copy.17.taps_ref, bf16[512,256]{1,0:T(8,128)(2,1)S(1)} %copy-done.10), custom_call_target="tpu_custom_call" | custom-call | flops 503316480 | bytes 3808000 | tf_op jit(solution)/shard_map/gradient_columns/pallas_call | solution.py:109
  148.2 32.5 %all_to_all.74 = bf16[32,16,1920]{2,1,0:T(8,128)(2,1)S(1)} all-to-all(bf16[32,16,1920]{2,1,0:T(8,128)(2,1)S(1)} %bitcast.23), channel_id=1, replica_groups=mesh['y'=4,'z'=4,'core'=2,'ch'=4] {'y','z','core'}, dimensions={0} | all-to-all | bytes 3932160 | tf_op jit(solution)/shard_map/all_to_all | solution.py:604
  180.7 6.7 %rows_backward.1 = (bf16[512,1536]{1,0:T(8,128)(2,1)S(1)}, bf16[2,256,1536]{2,1,0:T(8,128)(2,1)S(1)}) custom-call(bf16[512,1920]{1,0:T(8,128)(2,1)S(1)} %bitcast.21, bf16[2,512,512]{2,1,0:T(8,128)(2,1)S(1)} %copy-done.18, f32[2,32,1536]{2,1,0:T(8,128)S(1)} %copy-done.25, bf16[2,256,1536]{2,1,0:T(8,128)(2,1)S(1)} %copy-done.4, ...), custom_call_target="tpu_custom_call" | custom-call | flops 1610612736 | bytes 9699328 | tf_op jit(solution)/shard_map/rows_backward/pallas_call | solution.py:109
  189.7 4.0 %all-to-all-start.5 = ((bf16[32,16,1536]{2,1,0:T(8,128)(2,1)}), bf16[32,16,1536]{2,1,0:T(8,128)(2,1)S(1)}, u32[]{:S(2)}, u32[]{:S(2)}) async-start(bf16[32,16,1536]{2,1,0:T(8,128)(2,1)} %bitcast.30), calls=%async_computation.5 | async-start | bytes 3145728 | tf_op jit(solution)/shard_map/all_to_all | solution.py:604
  194.1 1.8 collective-permute-start.4
  196.5 1.4 copy-done.16
  198.9 3.7 %grad_filter.1 = f32[2,1536,256]{2,1,0:T(8,128)} custom-call(bf16[2,256,1536]{2,1,0:T(8,128)(2,1)S(1)} %copy-done.16, bf16[256,256]{1,0:T(8,128)(2,1)S(1)} %copy-done.23), custom_call_target="tpu_custom_call" | custom-call | bytes 1024 | tf_op jit(solution)/shard_map/grad_filter/pallas_call | solution.py:109
  202.5 2.6 %collective-permute-done.4.two_ref = bf16[384,256]{1,0:T(8,128)(2,1)S(1)} collective-permute-done((bf16[384,256]{1,0:T(8,128)(2,1)}, bf16[384,256]{1,0:T(8,128)(2,1)S(1)}, u32[]{:S(2)}, u32[]{:S(2)}) %collective-permute-start.4) | collective-permute-done | bytes 196640 | tf_op jit(solution)/shard_map/ppermute | solution.py:611
  207.3 9.1 %all-to-all-done.5 = bf16[32,16,1536]{2,1,0:T(8,128)(2,1)S(1)} async-done(((bf16[32,16,1536]{2,1,0:T(8,128)(2,1)}), bf16[32,16,1536]{2,1,0:T(8,128)(2,1)S(1)}, u32[]{:S(2)}, u32[]{:S(2)}) %all-to-all-start.5) | async-done | bytes 1572896 | tf_op jit(solution)/shard_map/all_to_all | solution.py:604
  218.5 1.9 image.1
  (103 shorter events, 26.0 us)
Async XLA Ops:
  7.2 107.8 %all-gather.2.cloned.1.call-start = ((), (), s32[]{:S(2)}) async-start(), calls=%async_computation.6 | async-start | bytes 10616832 | tf_op jit(solution)/shard_map/all_gather | solution.py:659
  18.2 14.7 %copy-start.22 = (bf16[256,256]{1,0:T(8,128)(2,1)S(1)}, bf16[256,256]{1,0:T(8,128)(2,1)}, u32[]{:S(2)}) copy-start(bf16[256,256]{1,0:T(8,128)(2,1)} %constant.26.clone.straight_ref.unit_ref) | copy-start | bytes 393220
  18.2 32.5 %copy-start.24 = (f32[2,32,1536]{2,1,0:T(8,128)S(1)}, f32[2,32,1536]{2,1,0:T(8,128)}, u32[]{:S(2)}) copy-start(f32[2,32,1536]{2,1,0:T(8,128)} %constant.24.clone.refs_2_) | copy-start | bytes 1179652
  18.2 32.5 %all-to-all-start = ((bf16[32,16,1536]{2,1,0:T(8,128)(2,1)}), bf16[32,16,1536]{2,1,0:T(8,128)(2,1)}, u32[]{:S(2)}, u32[]{:S(2)}) async-start(bf16[32,16,1536]{2,1,0:T(8,128)(2,1)} %bitcast.2), calls=%async_computation | async-start | bytes 3145728 | tf_op jit(solution)/shard_map/all_to_all | solution.py:604
  28.0 8.7 %collective-permute-start = (bf16[384,256]{1,0:T(8,128)(2,1)}, bf16[384,256]{1,0:T(8,128)(2,1)S(1)}, u32[]{:S(2)}, u32[]{:S(2)}) collective-permute-start(bf16[384,256]{1,0:T(8,128)(2,1)} %get-tuple-element.125), channel_id=1, source_target_pairs={{0,1},{1,2},{2,3},{3,0},{4,5},{5,6},{6,7},{7,4},{8,9},{9,10},{10,1... | collective-permute-start | bytes 589832 | tf_op jit(solution)/shard_map/ppermute | solution.py:611
  29.3 16.0 %collective-permute-start.1 = (bf16[384,256]{1,0:T(8,128)(2,1)}, bf16[384,256]{1,0:T(8,128)(2,1)S(1)}, u32[]{:S(2)}, u32[]{:S(2)}) collective-permute-start(bf16[384,256]{1,0:T(8,128)(2,1)} %get-tuple-element.126), channel_id=1, source_target_pairs={{0,2},{1,3},{2,0},{3,1},{4,6},{5,7},{6,4},{7,5},{8,10},{9,11},{10,... | collective-permute-start | bytes 589832 | tf_op jit(solution)/shard_map/ppermute | solution.py:611
  31.7 14.2 %collective-permute-start.2 = (bf16[384,256]{1,0:T(8,128)(2,1)S(1)}, bf16[384,256]{1,0:T(8,128)(2,1)S(1)}, u32[]{:S(2)}, u32[]{:S(2)}) collective-permute-start(bf16[384,256]{1,0:T(8,128)(2,1)S(1)} %get-tuple-element.127), channel_id=1, source_target_pairs={{0,3},{1,0},{2,1},{3,2},{4,7},{5,4},{6,5},{7,6},{8,11},{9,8},{10,9... | collective-permute-start | bytes 589832 | tf_op jit(solution)/shard_map/ppermute | solution.py:611
  36.7 22.2 %copy-start.3 = (bf16[2,256,1536]{2,1,0:T(8,128)(2,1)}, bf16[2,256,1536]{2,1,0:T(8,128)(2,1)S(1)}, u32[]{:S(2)}) copy-start(bf16[2,256,1536]{2,1,0:T(8,128)(2,1)S(1)} %filter.1.refs_3_) | copy-start | bytes 4718596
  58.9 32.2 %copy-start.13 = (bf16[2,256,1536]{2,1,0:T(8,128)(2,1)}, bf16[2,256,1536]{2,1,0:T(8,128)(2,1)S(1)}, u32[]{:S(2)}) copy-start(bf16[2,256,1536]{2,1,0:T(8,128)(2,1)S(1)} %get-tuple-element.229.refs_4_) | copy-start | bytes 4718596
  58.9 32.1 %copy-start.41 = (f32[192,9]{0,1:T(8,128)S(1)}, f32[192,9]{0,1:T(8,128)}, u32[]{:S(2)}) copy-start(f32[192,9]{0,1:T(8,128)} %param.14) | copy-start | bytes 20740
  58.9 33.6 %copy-start.10 = (bf16[512,256]{1,0:T(8,128)(2,1)S(1)}, bf16[512,256]{1,0:T(8,128)(2,1)}, u32[]{:S(2)}) copy-start(bf16[512,256]{1,0:T(8,128)(2,1)} %constant.25.clone.table_ref) | copy-start | bytes 786436
  98.0 17.0 %copy-start.31 = (bf16[384,256]{1,0:T(8,128)(2,1)S(1)}, bf16[384,256]{1,0:T(8,128)(2,1)}, u32[]{:S(2)}) copy-start(bf16[384,256]{1,0:T(8,128)(2,1)} %copy-done.30) | copy-start | bytes 589828
  98.0 17.0 %copy-start.33 = (bf16[384,256]{1,0:T(8,128)(2,1)S(1)}, bf16[384,256]{1,0:T(8,128)(2,1)}, u32[]{:S(2)}) copy-start(bf16[384,256]{1,0:T(8,128)(2,1)} %copy-done.32) | copy-start | bytes 589828
  98.0 17.0 %copy-start.36 = (bf16[384,256]{1,0:T(8,128)(2,1)S(1)}, bf16[384,256]{1,0:T(8,128)(2,1)}, u32[]{:S(2)}) copy-start(bf16[384,256]{1,0:T(8,128)(2,1)} %copy-done.35) | copy-start | bytes 589828
  98.0 17.0 %copy-start.39 = (bf16[384,256]{1,0:T(8,128)(2,1)S(1)}, bf16[384,256]{1,0:T(8,128)(2,1)}, u32[]{:S(2)}) copy-start(bf16[384,256]{1,0:T(8,128)(2,1)} %copy-done.38) | copy-start | bytes 589828
  130.6 13.8 %copy-start.7 = (bf16[1536,256]{1,0:T(8,128)(2,1)S(1)}, bf16[1536,256]{1,0:T(8,128)(2,1)}, u32[]{:S(2)}) copy-start(bf16[1536,256]{1,0:T(8,128)(2,1)} %copy-done.6) | copy-start | bytes 2359300
  144.4 36.3 %copy-start.18 = (bf16[2,512,512]{2,1,0:T(8,128)(2,1)S(1)}, bf16[2,512,512]{2,1,0:T(8,128)(2,1)}, u32[]{:S(2)}) copy-start(bf16[2,512,512]{2,1,0:T(8,128)(2,1)} %constant.23.clone.refs_1_) | copy-start | bytes 3145732
  148.2 32.5 %copy-start.4 = (bf16[2,256,1536]{2,1,0:T(8,128)(2,1)S(1)}, bf16[2,256,1536]{2,1,0:T(8,128)(2,1)}, u32[]{:S(2)}) copy-start(bf16[2,256,1536]{2,1,0:T(8,128)(2,1)} %copy-done.3) | copy-start | bytes 4718596
  148.2 32.5 %copy-start.14 = (bf16[2,256,1536]{2,1,0:T(8,128)(2,1)S(1)}, bf16[2,256,1536]{2,1,0:T(8,128)(2,1)}, u32[]{:S(2)}) copy-start(bf16[2,256,1536]{2,1,0:T(8,128)(2,1)} %copy-done.13) | copy-start | bytes 4718596
  148.2 32.5 %copy-start.25 = (f32[2,32,1536]{2,1,0:T(8,128)S(1)}, f32[2,32,1536]{2,1,0:T(8,128)}, u32[]{:S(2)}) copy-start(f32[2,32,1536]{2,1,0:T(8,128)} %constant.24.clone.refs_2_) | copy-start | bytes 1179652
  189.7 26.7 %all-to-all-start.5 = ((bf16[32,16,1536]{2,1,0:T(8,128)(2,1)}), bf16[32,16,1536]{2,1,0:T(8,128)(2,1)S(1)}, u32[]{:S(2)}, u32[]{:S(2)}) async-start(bf16[32,16,1536]{2,1,0:T(8,128)(2,1)} %bitcast.30), calls=%async_computation.5 | async-start | bytes 3145728 | tf_op jit(solution)/shard_map/all_to_all | solution.py:604
  193.7 8.8 %collective-permute-start.3 = (bf16[384,256]{1,0:T(8,128)(2,1)}, bf16[384,256]{1,0:T(8,128)(2,1)S(1)}, u32[]{:S(2)}, u32[]{:S(2)}) collective-permute-start(bf16[384,256]{1,0:T(8,128)(2,1)} %copy-done.40), channel_id=1, source_target_pairs={{0,1},{1,2},{2,3},{3,0},{4,5},{5,6},{6,7},{7,4},{8,9},{9,10},{10,1... | collective-permute-start | bytes 589832 | tf_op jit(solution)/shard_map/ppermute | solution.py:611
  194.1 11.1 %collective-permute-start.4 = (bf16[384,256]{1,0:T(8,128)(2,1)}, bf16[384,256]{1,0:T(8,128)(2,1)S(1)}, u32[]{:S(2)}, u32[]{:S(2)}) collective-permute-start(bf16[384,256]{1,0:T(8,128)(2,1)} %copy-done.37), channel_id=1, source_target_pairs={{0,2},{1,3},{2,0},{3,1},{4,6},{5,7},{6,4},{7,5},{8,10},{9,11},{10,... | collective-permute-start | bytes 589832 | tf_op jit(solution)/shard_map/ppermute | solution.py:611
  195.8 10.2 %collective-permute-start.5 = (bf16[384,256]{1,0:T(8,128)(2,1)}, bf16[384,256]{1,0:T(8,128)(2,1)S(1)}, u32[]{:S(2)}, u32[]{:S(2)}) collective-permute-start(bf16[384,256]{1,0:T(8,128)(2,1)} %copy-done.34), channel_id=1, source_target_pairs={{0,3},{1,0},{2,1},{3,2},{4,7},{5,4},{6,5},{7,6},{8,11},{9,8},{10,9... | collective-permute-start | bytes 589832 | tf_op jit(solution)/shard_map/ppermute | solution.py:611
  (28 other events, 120.8 us)
Sparse Core Ops, SparseCore 0:
  18.3 62.5 all-gather.1
